TPU v7x, 512 devices: a whole 4x4x16 slice. The times are simulated.
512 devices in a mesh: ctx: 64 (over x, z), head: 2 (over core), seq: 4 (over y).
Axes of the slice: x: 4, y: 4, z: 16, core: 2. Of those that a mesh axis runs over, the one named last changes fastest.
Arguments:
- mixer_input: bfloat16 [32768, 5120], P(('seq', 'ctx'), 'head'), parts along dimension 0, may hold values from -6 to 6
- gate_input: bfloat16 [32768, 5120], P(('seq', 'ctx'), 'head'), parts along dimension 0, may hold values from -12 to 12
- input_proj: bfloat16 [32768, 128], P(('seq', 'ctx')), parts along dimension 0, may hold values from -0.5 to 0.5
- output_proj: bfloat16 [32768, 128], P(('seq', 'ctx')), parts along dimension 0, may hold values from -20 to 20
- step_size: float32 [80, 32768], P('head', ('seq', 'ctx')), parts along dimension 1, may hold values from 0 to 1, as said below
- decay_log: float32 [80, 32768], P('head', ('seq', 'ctx')), parts along dimension 1, may hold values from -2 to 0, as said below
- level_weight: float32 [7, 80, 32768], P(None, 'head', ('seq', 'ctx')), parts along dimension 2, may hold values from 0.25 to 2.5
- norm_weight: float32 [5120], P('head'), may hold values from 0.1 to 1.9
Outputs:
- mixed_out: bfloat16 [32768, 5120], P(('seq', 'ctx'), 'head'), parts along dimension 0
There are 4 independent parts, one for each index of `seq`. A program takes and returns all parts, laid end to end along the dimension named above; an argument that names none is the same for every part. Nothing has to cross between parts.
Inputs may be any that keep to these rules, and one draw needn't show every extreme that they name: `step_size`: positive. `decay_log`: never positive.
All inputs are finite; a program needn't handle non-finite values.
Results may differ from a plain program's by a relative error of at most 0.0058.
Values may be sent and summed in bfloat16 or wider, within the bound.
No kernel may reach another device: no remote copies, remote signals or barrier semaphores. Data moves between devices by JAX's collectives and lax.ppermute only.
A program may use at most 64 MiB of HBM per device.

v0:
```python
import jax
import jax.numpy as jnp
from jax import lax
from jax.sharding import PartitionSpec as P

BLOCK = 128


highest = lax.Precision.HIGHEST


def from_partner(value, axis, distance):
    mask = 2**distance
    pairs = [(source, source ^ mask) for source in range(lax.axis_size(axis))]
    return lax.ppermute(value, axis, pairs)


def widen(array, head_size):
    return jnp.repeat(array, head_size, axis=0)


def on_device(
    mixer_input,
    gate_input,
    input_proj,
    output_proj,
    step_size,
    decay_log,
    level_weight,
    norm_weight,
):
    heads_dev, tokens = decay_log.shape
    columns = mixer_input.shape[1]
    head_size = columns // heads_dev
    state_size = input_proj.shape[1]
    block_count = tokens // BLOCK
    local_levels = block_count.bit_length() - 1
    ctx_levels = lax.axis_size("ctx").bit_length() - 1
    level_count = level_weight.shape[0]
    within = jnp.cumsum(decay_log.reshape(heads_dev, block_count, BLOCK), axis=2)
    totals = within[:, :, -1]
    run_total = jnp.cumsum(totals, axis=1)
    before = run_total - totals
    run_wide = widen(run_total, head_size)
    values = mixer_input.reshape(block_count, BLOCK, heads_dev, head_size)
    b_blocks = input_proj.reshape(block_count, BLOCK, state_size)
    c_blocks = output_proj.reshape(block_count, BLOCK, state_size)
    c_wide = c_blocks.astype(jnp.float32)
    step_rows = step_size.reshape(heads_dev, block_count, BLOCK)
    weights = level_weight.reshape(level_count, heads_dev, block_count, BLOCK)
    scores = jnp.einsum("kqn,ksn->kqs", c_blocks, b_blocks, preferred_element_type=jnp.float32)
    causal = jnp.arange(BLOCK)[:, None] >= jnp.arange(BLOCK)[None, :]
    log_gap = within[:, :, :, None] - within[:, :, None, :]
    decay_mat = jnp.where(causal, jnp.exp(jnp.where(causal, log_gap, 0.0)), 0.0)
    mixing = (
        weights[0][:, :, :, None] * decay_mat * scores[None] * step_rows[:, :, None, :]
    ).astype(jnp.bfloat16)
    output = jnp.einsum(
        "hkqs,kshp->kqhp", mixing, values, preferred_element_type=jnp.float32
    ).reshape(tokens, columns)
    carry_in = widen(jnp.exp(totals[:, :, None] - within) * step_rows, head_size)
    scaled = (
        jnp.transpose(carry_in, (1, 2, 0)) * mixer_input.reshape(block_count, BLOCK, columns)
    ).astype(jnp.bfloat16)
    states = jnp.einsum("kqm,kqn->kmn", scaled, b_blocks, preferred_element_type=jnp.float32)
    c_index = jnp.arange(block_count, dtype=jnp.int32)
    tail_decay = jnp.exp(run_wide - run_wide)
    aggregate = jnp.einsum("mk,kmn->mn", tail_decay, states, precision=highest)
    block_decay = run_total[:, -1]
    offset = jnp.zeros_like(block_decay)
    position = lax.axis_index("ctx")
    c_flat = c_wide.reshape(tokens, state_size)
    token_base = (within + before[:, :, None]).reshape(heads_dev, tokens)
    for bit_number in range(ctx_levels):
        upper_side = position // 2**bit_number % 2 == 1
        other_state, other_decay = from_partner((aggregate, block_decay), "ctx", bit_number)
        level_gain = level_weight[1 + local_levels + bit_number]

        def level_term(operands):
            gain_rows, base_rows, shift_now, state_now = operands
            coefficient = (gain_rows * jnp.exp(base_rows + shift_now[:, None])).T
            reached = jnp.einsum("tn,mn->tm", c_flat, state_now, precision=highest)
            product = coefficient[:, :, None] * reached.reshape(tokens, heads_dev, head_size)
            return product.reshape(tokens, columns)

        def no_term(operands):
            return jnp.zeros((tokens, columns), jnp.float32)

        output = output + lax.cond(
            upper_side, level_term, no_term, (level_gain, token_base, offset, other_state)
        )
        own_keep = widen(jnp.exp(block_decay), head_size)[:, None]
        other_keep = widen(jnp.exp(other_decay), head_size)[:, None]
        aggregate = jnp.where(
            upper_side, own_keep * other_state + aggregate, other_keep * aggregate + other_state
        )
        offset = jnp.where(upper_side, offset + other_decay, offset)
        block_decay = block_decay + other_decay
    gated_rows = (output * jax.nn.silu(gate_input.astype(jnp.float32))).astype(jnp.bfloat16)
    gated_wide = gated_rows.astype(jnp.float32)
    whole_rows = lax.all_gather(gated_rows, "head", axis=1, tiled=True).astype(jnp.float32)
    mean_square = jnp.mean(whole_rows * whole_rows, axis=1)
    inverse_rms = lax.rsqrt(mean_square + 1e-05)
    return (gated_wide * inverse_rms[:, None] * norm_weight[None, :]).astype(jnp.bfloat16)


def solution(mesh):
    in_specs = (
        P(("seq", "ctx"), "head"),
        P(("seq", "ctx"), "head"),
        P(("seq", "ctx"), None),
        P(("seq", "ctx"), None),
        P("head", ("seq", "ctx")),
        P("head", ("seq", "ctx")),
        P(None, "head", ("seq", "ctx")),
        P("head"),
    )
    out_specs = P(("seq", "ctx"), "head")
    return jax.shard_map(
        on_device, mesh=mesh, in_specs=in_specs, out_specs=out_specs, check_vma=False
    )
```

profile of v0, /device:TPU:1, one launch (start us, length us, event | category | flops | bytes accessed | tf_op | source)
XLA Modules:
  0.0 505.5 jit_solution(15267808060756948158)
XLA Ops:
  6.5 1.0 reduce_window_sum.17
  7.6 0.2 subtract_reduce_fusion
  7.7 4.4 collective-permute-start.1
  12.1 0.8 exponential_multiply_fusion
  12.9 1.4 copy.30
  14.4 0.1 fusion.11
  14.7 1.2 convolution_multiply_fusion.6
  15.9 1.9 collective-permute-start
  18.1 24.4 %collective-permute-done = f32[2560,128]{1,0:T(8,128)S(1)} collective-permute-done((f32[2560,128]{1,0:T(8,128)S(1)}, f32[2560,128]{1,0:T(8,128)S(1)}, u32[]{:S(2)}, u32[]{:S(2)}) %collective-permute-start) | collective-permute-done | bytes 1310752 | tf_op jit(solution)/shard_map/ppermute | solution.py:15
  42.5 2.2 add_select_fusion.4
  44.7 9.5 %collective-permute-start.2 = (f32[2560,128]{1,0:T(8,128)}, f32[2560,128]{1,0:T(8,128)S(1)}, u32[]{:S(2)}, u32[]{:S(2)}) collective-permute-start(f32[2560,128]{1,0:T(8,128)} %add_select_fusion.4), channel_id=1, source_target_pairs={{0,16},{8,24},{16,0},{24,8},{32,48},{40,56},{48,32},{56,40},{64,80... | collective-permute-start | bytes 3932168 | tf_op jit(solution)/shard_map/ppermute | solution.py:15
  54.2 1.9 collective-permute-start.3
  56.3 54.4 %collective-permute-done.3 = f32[40]{0:T(128)S(1)} collective-permute-done((f32[40]{0:T(128)S(1)}, f32[40]{0:T(128)S(1)}, u32[]{:S(2)}, u32[]{:S(2)}) %collective-permute-start.3) | collective-permute-done | bytes 192 | tf_op jit(solution)/shard_map/ppermute | solution.py:15
  110.9 3.8 add_select_fusion.3
  114.6 8.8 %collective-permute-start.4 = (f32[2560,128]{1,0:T(8,128)}, f32[2560,128]{1,0:T(8,128)S(1)}, u32[]{:S(2)}, u32[]{:S(2)}) collective-permute-start(f32[2560,128]{1,0:T(8,128)} %add_select_fusion.3), channel_id=1, source_target_pairs={{0,32},{8,40},{16,48},{24,56},{32,0},{40,8},{48,16},{56,24},{64,96... | collective-permute-start | bytes 3932168 | tf_op jit(solution)/shard_map/ppermute | solution.py:15
  123.5 1.9 collective-permute-start.5
  125.5 137.3 %collective-permute-done.5 = f32[40]{0:T(128)S(1)} collective-permute-done((f32[40]{0:T(128)S(1)}, f32[40]{0:T(128)S(1)}, u32[]{:S(2)}, u32[]{:S(2)}) %collective-permute-start.5) | collective-permute-done | bytes 192 | tf_op jit(solution)/shard_map/ppermute | solution.py:15
  263.0 3.8 add_select_fusion.2
  266.8 70.2 %collective-permute-start.6 = (f32[2560,128]{1,0:T(8,128)}, f32[2560,128]{1,0:T(8,128)S(1)}, u32[]{:S(2)}, u32[]{:S(2)}) collective-permute-start(f32[2560,128]{1,0:T(8,128)} %add_select_fusion.2), channel_id=1, source_target_pairs={{0,64},{8,72},{16,80},{24,88},{32,96},{40,104},{48,112},{56,120},{... | collective-permute-start | bytes 3932168 | tf_op jit(solution)/shard_map/ppermute | solution.py:15
  337.1 1.9 collective-permute-start.7
  339.1 54.8 %collective-permute-done.7 = f32[40]{0:T(128)S(1)} collective-permute-done((f32[40]{0:T(128)S(1)}, f32[40]{0:T(128)S(1)}, u32[]{:S(2)}, u32[]{:S(2)}) %collective-permute-start.7) | collective-permute-done | bytes 192 | tf_op jit(solution)/shard_map/ppermute | solution.py:15
  394.1 3.8 add_select_fusion.1
  397.8 3.1 collective-permute-start.8
  401.0 2.2 collective-permute-start.9
  403.3 25.5 %collective-permute-done.9 = f32[40]{0:T(128)S(1)} collective-permute-done((f32[40]{0:T(128)S(1)}, f32[40]{0:T(128)S(1)}, u32[]{:S(2)}, u32[]{:S(2)}) %collective-permute-start.9) | collective-permute-done | bytes 192 | tf_op jit(solution)/shard_map/ppermute | solution.py:15
  429.0 3.8 add_select_fusion
  432.8 4.6 collective-permute-start.10
  437.5 0.7 slice_bitcast_fusion
  438.2 0.1 fusion.26
  438.4 1.6 fusion.6
  440.0 0.4 copy.32
  440.4 0.5 copy-done.8
  440.9 0.1 conditional.6
  441.0 1.3 conditional.7
  441.0 1.3 broadcast.104
  442.3 1.2 conditional.8
  442.3 1.2 broadcast.105
  443.5 1.2 conditional.9
  443.5 1.2 broadcast.106
  444.7 1.3 conditional.10
  444.7 1.3 broadcast.107
  446.0 18.4 %collective-permute-done.10 = f32[2560,128]{1,0:T(8,128)} collective-permute-done((f32[2560,128]{1,0:T(8,128)}, f32[2560,128]{1,0:T(8,128)}, u32[]{:S(2)}, u32[]{:S(2)}) %collective-permute-start.10) | collective-permute-done | bytes 1310752 | tf_op jit(solution)/shard_map/ppermute | solution.py:15
  464.4 1.2 conditional.11
  464.4 1.2 broadcast.108
  465.6 4.7 fusion.18
  470.4 25.5 %all-gather.2.cloned.1.call-done = bf16[128,5120]{1,0:T(8,128)(2,1)} async-done(((bf16[128,2560]{1,0:T(8,128)(2,1)}), bf16[128,5120]{1,0:T(8,128)(2,1)}) %all-gather.2.cloned.1.call-update) | async-done | bytes 1310736 | tf_op jit(solution)/shard_map/all_gather | solution.py:101
  495.9 1.6 multiply_reduce_fusion
  497.6 1.1 multiply_convert_fusion.2
  (65 shorter events, 1.9 us)
Async XLA Ops:
  6.5 8.1 %copy-start = (bf16[128,128]{1,0:T(8,128)(2,1)S(1)}, bf16[128,128]{1,0:T(8,128)(2,1)}, u32[]{:S(2)}) copy-start(bf16[128,128]{1,0:T(8,128)(2,1)} %param.22) | copy-start | bytes 98308
  6.5 489.4 %all-gather.2.cloned.1.call-start = ((), (), s32[]{:S(2)}) async-start(), calls=%async_computation | async-start | bytes 1966080 | tf_op jit(solution)/shard_map/all_gather | solution.py:101
  7.7 6.8 %collective-permute-start.1 = (f32[40]{0:T(128)S(1)}, f32[40]{0:T(128)S(1)}, u32[]{:S(2)}, u32[]{:S(2)}) collective-permute-start(f32[40]{0:T(128)S(1)} %get-tuple-element.164), channel_id=1, source_target_pairs={{0,8},{8,0},{16,24},{24,16},{32,40},{40,32},{48,56},{56,48},{64,72... | collective-permute-start | bytes 488 | tf_op jit(solution)/shard_map/ppermute | solution.py:15
  15.9 26.6 %collective-permute-start = (f32[2560,128]{1,0:T(8,128)S(1)}, f32[2560,128]{1,0:T(8,128)S(1)}, u32[]{:S(2)}, u32[]{:S(2)}) collective-permute-start(f32[2560,128]{1,0:T(8,128)S(1)} %convolution_multiply_fusion.6), channel_id=1, source_target_pairs={{0,8},{8,0},{16,24},{24,16},{32,40},{40,32},{48,56},{56,48},{64,72... | collective-permute-start | bytes 3932168 | tf_op jit(solution)/shard_map/ppermute | solution.py:15
  42.5 2.2 copy-start.2
  44.7 66.2 %collective-permute-start.2 = (f32[2560,128]{1,0:T(8,128)}, f32[2560,128]{1,0:T(8,128)S(1)}, u32[]{:S(2)}, u32[]{:S(2)}) collective-permute-start(f32[2560,128]{1,0:T(8,128)} %add_select_fusion.4), channel_id=1, source_target_pairs={{0,16},{8,24},{16,0},{24,8},{32,48},{40,56},{48,32},{56,40},{64,80... | collective-permute-start | bytes 3932168 | tf_op jit(solution)/shard_map/ppermute | solution.py:15
  54.2 56.5 %collective-permute-start.3 = (f32[40]{0:T(128)S(1)}, f32[40]{0:T(128)S(1)}, u32[]{:S(2)}, u32[]{:S(2)}) collective-permute-start(f32[40]{0:T(128)S(1)} %get-tuple-element.172), channel_id=1, source_target_pairs={{0,16},{8,24},{16,0},{24,8},{32,48},{40,56},{48,32},{56,40},{64,80... | collective-permute-start | bytes 488 | tf_op jit(solution)/shard_map/ppermute | solution.py:15
  110.9 3.8 copy-start.3
  114.6 148.4 %collective-permute-start.4 = (f32[2560,128]{1,0:T(8,128)}, f32[2560,128]{1,0:T(8,128)S(1)}, u32[]{:S(2)}, u32[]{:S(2)}) collective-permute-start(f32[2560,128]{1,0:T(8,128)} %add_select_fusion.3), channel_id=1, source_target_pairs={{0,32},{8,40},{16,48},{24,56},{32,0},{40,8},{48,16},{56,24},{64,96... | collective-permute-start | bytes 3932168 | tf_op jit(solution)/shard_map/ppermute | solution.py:15
  123.5 139.4 %collective-permute-start.5 = (f32[40]{0:T(128)S(1)}, f32[40]{0:T(128)S(1)}, u32[]{:S(2)}, u32[]{:S(2)}) collective-permute-start(f32[40]{0:T(128)S(1)} %get-tuple-element.170), channel_id=1, source_target_pairs={{0,32},{8,40},{16,48},{24,56},{32,0},{40,8},{48,16},{56,24},{64,96... | collective-permute-start | bytes 488 | tf_op jit(solution)/shard_map/ppermute | solution.py:15
  263.0 3.8 copy-start.4
  266.8 127.3 %collective-permute-start.6 = (f32[2560,128]{1,0:T(8,128)}, f32[2560,128]{1,0:T(8,128)S(1)}, u32[]{:S(2)}, u32[]{:S(2)}) collective-permute-start(f32[2560,128]{1,0:T(8,128)} %add_select_fusion.2), channel_id=1, source_target_pairs={{0,64},{8,72},{16,80},{24,88},{32,96},{40,104},{48,112},{56,120},{... | collective-permute-start | bytes 3932168 | tf_op jit(solution)/shard_map/ppermute | solution.py:15
  337.1 56.9 %collective-permute-start.7 = (f32[40]{0:T(128)S(1)}, f32[40]{0:T(128)S(1)}, u32[]{:S(2)}, u32[]{:S(2)}) collective-permute-start(f32[40]{0:T(128)S(1)} %get-tuple-element.168), channel_id=1, source_target_pairs={{0,64},{8,72},{16,80},{24,88},{32,96},{40,104},{48,112},{56,120},{... | collective-permute-start | bytes 488 | tf_op jit(solution)/shard_map/ppermute | solution.py:15
  394.1 3.8 copy-start.5
  397.8 31.1 %collective-permute-start.8 = (f32[2560,128]{1,0:T(8,128)}, f32[2560,128]{1,0:T(8,128)S(1)}, u32[]{:S(2)}, u32[]{:S(2)}) collective-permute-start(f32[2560,128]{1,0:T(8,128)} %add_select_fusion.1), channel_id=1, source_target_pairs={{0,128},{8,136},{16,144},{24,152},{32,160},{40,168},{48,176},{56,1... | collective-permute-start | bytes 3932168 | tf_op jit(solution)/shard_map/ppermute | solution.py:15
  401.0 27.8 %collective-permute-start.9 = (f32[40]{0:T(128)S(1)}, f32[40]{0:T(128)S(1)}, u32[]{:S(2)}, u32[]{:S(2)}) collective-permute-start(f32[40]{0:T(128)S(1)} %get-tuple-element.166), channel_id=1, source_target_pairs={{0,128},{8,136},{16,144},{24,152},{32,160},{40,168},{48,176},{56,1... | collective-permute-start | bytes 488 | tf_op jit(solution)/shard_map/ppermute | solution.py:15
  428.8 4.0 copy-start.12
  429.0 8.5 %copy-start.9 = (bf16[128,128]{1,0:T(8,128)(2,1)S(1)}, bf16[128,128]{1,0:T(8,128)(2,1)}, u32[]{:S(2)}) copy-start(bf16[128,128]{1,0:T(8,128)(2,1)} %param.23) | copy-start | bytes 98308
  429.0 9.4 %copy-start.10 = (f32[40,128]{1,0:T(8,128)S(1)}, f32[40,128]{1,0:T(8,128)}, u32[]{:S(2)}) copy-start(f32[40,128]{1,0:T(8,128)} %param.24) | copy-start | bytes 61444
  429.0 3.8 copy-start.6
  432.8 31.6 %collective-permute-start.10 = (f32[2560,128]{1,0:T(8,128)}, f32[2560,128]{1,0:T(8,128)}, u32[]{:S(2)}, u32[]{:S(2)}) collective-permute-start(f32[2560,128]{1,0:T(8,128)} %add_select_fusion), channel_id=1, source_target_pairs={{0,256},{8,264},{16,272},{24,280},{32,288},{40,296},{48,304},{56,3... | collective-permute-start | bytes 3932168 | tf_op jit(solution)/shard_map/ppermute | solution.py:15
  440.0 0.9 copy-start.8
  444.7 19.7 %copy-start.13 = (f32[40]{0:T(128)S(1)}, f32[40]{0:T(128)}, u32[]{:S(2)}) copy-start(f32[40]{0:T(128)} %copy-done.12) | copy-start | bytes 484
  464.4 1.2 copy-start.7
  470.3 27.2 %copy-start.1 = (bf16[128,2560]{1,0:T(8,128)(2,1)S(1)}, bf16[128,2560]{1,0:T(8,128)(2,1)}, u32[]{:S(2)}) copy-start(bf16[128,2560]{1,0:T(8,128)(2,1)} %fusion.18) | copy-start | bytes 1966084
  470.3 27.2 %copy-start.11 = (f32[2560]{0:T(1024)S(1)}, f32[2560]{0:T(1024)}, u32[]{:S(2)}) copy-start(f32[2560]{0:T(1024)} %param.27) | copy-start | bytes 30724
Sparse Core Ops, SparseCore 0:
  470.5 25.3 all-gather.1
where the time goes:
time: 507 us; the launch traced here: 505 us
  waiting for transfers between devices  340 us (67%)
  starting transfers between devices  110 us (22%)
  other arithmetic  26.9 us (5%)
  between operations  13.8 us (3%)
  local copies, waits for them, and re-layouts  11 us (2%)
    ppermute x11, waiting for transfers between devices, from_partner(): return lax.ppermute(value, axis, pairs)  315 us
    ppermute x11, starting transfers between devices, from_partner(): return lax.ppermute(value, axis, pairs)  110 us
    all_gather x1, waiting for transfers between devices, on_device(): lax.all_gather(gated_rows, 'head', axis=1, tiled=True).astype(jnp.float32)  25.5 us
    select_n x5, other arithmetic, on_device(): jnp.where(upper_side, own_keep * other_state + aggregate, other_keep * ag...  17.3 us
  transfers between devices with their start and end apart: 12, of which 7 were waited for; matrix products, arithmetic and copies ran while one was open for 2% of the time, Pallas kernels for 0%

commit v1 on v0

v1 whole, which is shorter than its diff:
```python
import jax
import jax.numpy as jnp
from jax import lax
from jax.experimental import pallas as pl
from jax.experimental.pallas import tpu as pltpu
from jax.sharding import PartitionSpec as P

ROWS, GROUPS, PLACES = 4, 4, 4
BLOCK = 128
STATE = 128
HEADDIM = 64
HEADS = 40
COLS = HEADS * HEADDIM
PART_HEADS = HEADS // PLACES
PART = COLS // PLACES
TILES = PART // 128
BODY = TILES * STATE
META = 16
MSG = BODY + META
LEVELS = 6
f32, bf16, i32 = jnp.float32, jnp.bfloat16, jnp.int32
VMEM = 24 * 2**20


def dot(a, b):
    return jnp.dot(a, b, preferred_element_type=f32)


def three(v):
    hi = v.astype(bf16)
    rest = v - hi.astype(f32)
    mid = rest.astype(bf16)
    return hi, mid, (rest - mid.astype(f32)).astype(bf16)


def iota(shape, dim):
    return lax.broadcasted_iota(i32, shape, dim)


def ones_where(cond):
    return jnp.where(cond, 1.0, 0.0).astype(bf16)


def row_mod(rows, period, shape):
    r = iota(shape, 0)
    turn = jnp.zeros(shape, i32)
    for k in range(period, rows, period):
        turn = turn + jnp.where(r >= k, 1, 0)
    return r - turn * period, turn


def state_kernel(x_ref, b_ref, decay_ref, step_ref, msg_ref, within_ref):
    upper = ones_where(iota((128, 128), 0) <= iota((128, 128), 1))
    within = sum(dot(p, upper) for p in three(decay_ref[...]))
    within_ref[...] = within
    total = within[:, 127:128]
    carry = jnp.exp(total - within) * step_ref[...]
    pad = jnp.zeros((8, 128), f32)

    def stacked(v):
        return jnp.concatenate([p.astype(f32) for p in three(v)] + [pad], axis=0).T

    carry_t = stacked(carry).astype(bf16)
    last = stacked(within)[127:128, :]
    b_t = b_ref[...].astype(f32).T.astype(bf16)
    head, term = row_mod(120, HEADS, (128, 128))
    term = jnp.where(iota((128, 128), 0) >= 120, 7, term)
    side = jnp.where(iota((128, 128), 1) >= HEADDIM, 1, 0)
    lane_term = jnp.where(iota((META, 128), 1) >= 80, 2, jnp.where(iota((META, 128), 1) >= 40, 1, 0))
    meta_row = iota((META, 128), 0)
    for part in range(PLACES):
        meta = jnp.zeros((META, 128), f32)
        for tile in range(TILES):
            pair = part * TILES + tile
            spread = ones_where(jnp.logical_and(head == 2 * pair + side, term < 3))
            cols = slice(pair * 128, (pair + 1) * 128)
            scaled = (dot(carry_t, spread) * x_ref[:, cols].astype(f32)).astype(bf16)
            msg_ref[part, tile * STATE : (tile + 1) * STATE, :] = dot(b_t, scaled).astype(bf16)
            pick = jnp.where(meta_row == 3 * tile + lane_term, last, 0.0).astype(bf16)
            meta = meta + dot(pick, spread)
        msg_ref[part, BODY:MSG, :] = meta.astype(bf16)


def coef_kernel(weight_ref, within_ref, coef_ref):
    grown = jnp.exp(within_ref[...])
    rows = [weight_ref[level] * grown for level in range(1, LEVELS + 1)]
    stack = jnp.concatenate(rows + [jnp.zeros((16, 128), f32)], axis=0).T
    hi, lo, _ = three(stack)
    shape = (256, 128)
    head, level = row_mod(240, HEADS, shape)
    level = jnp.where(iota(shape, 0) >= 240, 99, level)
    lane = iota(shape, 1)
    for part in range(PLACES):
        own = head - part * PART_HEADS
        ok = jnp.logical_and(jnp.logical_and(own >= 0, own < PART_HEADS), level < LEVELS)
        target = jnp.where(ok, level * PART_HEADS + own, 999)
        packed = dot(hi, ones_where(lane == target)) + dot(lo, ones_where(lane == target + 64))
        coef_ref[part] = packed.astype(bf16)


def local_kernel(x_ref, b_ref, c_ref, step_ref, weight_ref, within_ref, out_ref):
    scores = lax.dot_general(
        c_ref[...], b_ref[...], (((1,), (1,)), ((), ())), preferred_element_type=f32
    )
    scores = jnp.where(iota((128, 128), 0) >= iota((128, 128), 1), scores, 0.0)
    pad = jnp.zeros((128 - HEADS, 128), f32)
    within = within_ref[...]
    within_t = jnp.concatenate([within, pad], axis=0).T
    weight_t = jnp.concatenate([weight_ref[0], pad], axis=0).T
    step = step_ref[...]
    left = iota((128, 128), 1) < HEADDIM
    zero = jnp.zeros((128, 128), bf16)

    def mixing(h):
        gap = jnp.minimum(within_t[:, h : h + 1] - within[h : h + 1, :], 0.0)
        gain = weight_t[:, h : h + 1] * jnp.exp(gap)
        return (gain * scores * step[h : h + 1, :]).astype(bf16)

    for pair in range(HEADS // 2):
        cols = slice(pair * 128, (pair + 1) * 128)
        x = x_ref[:, cols]
        both = jnp.concatenate([mixing(2 * pair), mixing(2 * pair + 1)], axis=1)
        sides = jnp.concatenate([jnp.where(left, x, zero), jnp.where(left, zero, x)], axis=0)
        out_ref[:, cols] = dot(both, sides)


def total_of(meta, tile):
    return meta[3 * tile : 3 * tile + 1] + meta[3 * tile + 1 : 3 * tile + 2] + meta[3 * tile + 2 : 3 * tile + 3]


def put_total(meta, tile, total):
    row = iota((META, 128), 0)
    for k, p in enumerate(three(total)):
        meta = jnp.where(row == 3 * tile + k, p.astype(f32), meta)
    return meta


def group_kernel(parts_ref, out_ref):
    metas = [parts_ref[j, BODY:MSG, :].astype(f32) for j in range(PLACES)]
    meta = jnp.zeros((META, 128), f32)
    for tile in range(TILES):
        rows = slice(tile * STATE, (tile + 1) * STATE)
        t = [total_of(m, tile) for m in metas]
        s = [parts_ref[j, rows, :].astype(f32) for j in range(PLACES)]
        acc = s[0]
        for j in range(1, PLACES):
            acc = jnp.exp(t[j]) * acc + s[j]
        out_ref[rows, :] = acc.astype(bf16)
        meta = put_total(meta, tile, t[0] + t[1] + t[2] + t[3])
    out_ref[BODY:MSG, :] = meta.astype(bf16)


def flag(cond):
    return jnp.where(cond, 1.0, 0.0).astype(f32)


def row_kernel(place_ref, own_ref, one_ref, two_ref, three_ref, out_ref):
    group = place_ref[0]
    refs = (own_ref, one_ref, two_ref, three_ref)
    spot = [(group + 4 - k) % 4 for k in range(GROUPS)]
    metas = [r[BODY:MSG, :].astype(f32) for r in refs]
    meta = jnp.zeros((META, 128), f32)
    for tile in range(TILES):
        rows = slice(tile * STATE, (tile + 1) * STATE)
        t = [total_of(m, tile) for m in metas]
        acc = None
        for k in range(GROUPS):
            gap = sum(t[j] * flag(spot[j] > spot[k]) for j in range(GROUPS) if j != k)
            term = jnp.exp(gap) * refs[k][rows, :].astype(f32)
            acc = term if acc is None else acc + term
        out_ref[rows, :] = acc.astype(bf16)
        meta = put_total(meta, tile, t[0] + t[1] + t[2] + t[3])
    out_ref[BODY:MSG, :] = meta.astype(bf16)


def reach_kernel(
    place_ref, c_ref, coef_ref, parts_ref, g1_ref, g2_ref, g3_ref, r1_ref, r2_ref, r3_ref, out_ref
):
    group, row = place_ref[0], place_ref[1]
    part_metas = [parts_ref[j, BODY:MSG, :].astype(f32) for j in range(PLACES)]
    group_refs = (g1_ref, g2_ref, g3_ref)
    row_refs = (r1_ref, r2_ref, r3_ref)
    group_metas = [r[BODY:MSG, :].astype(f32) for r in group_refs]
    row_metas = [r[BODY:MSG, :].astype(f32) for r in row_refs]

    def buckets(index, refs, t, rows):
        vals = [r[rows, :].astype(f32) for r in refs]
        near = flag(index % 2 == 1) * vals[0]
        w1 = flag(index == 2)
        w2 = flag(index >= 2) * jnp.exp(t[0])
        w3 = flag(index == 3) * jnp.exp(t[0] + t[1])
        far = w1 * vals[0] + w2 * vals[1] + w3 * vals[2]
        return near, far

    def split(v):
        hi = v.astype(bf16)
        return jnp.concatenate([hi, (v - hi.astype(f32)).astype(bf16)], axis=0)

    slot = iota((128, 128), 0)
    slot = jnp.where(slot >= 64, slot - 64, slot)
    side = jnp.where(iota((128, 128), 1) >= HEADDIM, 1, 0)
    for first in range(0, TILES, 2):
        tiles = range(first, min(first + 2, TILES))
        low_b, mid_b, high_b = [], [], []
        group_b = [[], [], [], []]
        offs, skip = [[], [], [], []], []
        for tile in tiles:
            rows = slice(tile * STATE, (tile + 1) * STATE)
            t = [total_of(m, tile) for m in part_metas]
            s0, s1 = parts_ref[0, rows, :], parts_ref[1, rows, :]
            low_b.append(s0)
            mid_b.append(split(jnp.exp(t[1]) * s0.astype(f32) + s1.astype(f32)))
            high_b.append(parts_ref[2, rows, :])
            tg = [total_of(m, tile) for m in group_metas]
            tr = [total_of(m, tile) for m in row_metas]
            b3, b4 = buckets(group, group_refs, tg, rows)
            b5, b6 = buckets(row, row_refs, tr, rows)
            lead = jnp.exp(
                flag(group >= 1) * tg[0] + flag(group >= 2) * tg[1] + flag(group >= 3) * tg[2]
            )
            for k, v in enumerate((b3, b4, lead * b5, lead * b6)):
                group_b[k].append(split(v))
            offs[1].append(jnp.exp(t[0]))
            offs[2].append(jnp.exp(t[0] + t[1]))
            offs[3].append(jnp.exp(t[0] + t[1] + t[2]))
            skip.append(jnp.exp(t[2]))

        def wide(pieces):
            return pieces[0] if len(pieces) == 1 else jnp.concatenate(pieces, axis=1)

        spread = [
            wide([ones_where(slot == level * PART_HEADS + 2 * tile + side) for tile in tiles])
            for level in range(LEVELS)
        ]
        low_w, mid_w, high_w = wide(low_b), wide(mid_b), wide(high_b)
        group_w = [wide(v) for v in group_b]
        lanes = slice(first * 128, (first + len(tiles)) * 128)
        for place in range(PLACES):
            c = c_ref[place]
            cc = jnp.concatenate([c, c], axis=1)
            coef = coef_ref[place]
            acc = None
            for k in range(4):
                term = dot(coef, spread[2 + k]) * dot(cc, group_w[k])
                acc = term if acc is None else acc + term
            if place:
                acc = acc * wide(offs[place])
            if place == 1:
                acc = acc + dot(coef, spread[0]) * dot(c, low_w)
            if place == 3:
                acc = acc + dot(coef, spread[0]) * dot(c, high_w)
            if place >= 2:
                term = dot(coef, spread[1]) * dot(cc, mid_w)
                acc = acc + (term * wide(skip) if place == 3 else term)
            out_ref[place, :, lanes] = acc.astype(bf16)


def gate_kernel(local_ref, reached_ref, gate_ref, gated_ref, square_ref):
    acc = jnp.zeros((128, 128), f32)
    for pair in range(HEADS // 2):
        cols = slice(pair * 128, (pair + 1) * 128)
        part, tile = pair // TILES, pair % TILES
        mixed = local_ref[:, cols] + reached_ref[part, :, tile * 128 : (tile + 1) * 128].astype(f32)
        gate = gate_ref[:, cols].astype(f32)
        gated = (mixed * (gate / (1.0 + jnp.exp(-gate)))).astype(bf16)
        gated_ref[:, cols] = gated
        wide = gated.astype(f32)
        acc = acc + wide * wide
    square_ref[...] = acc


def norm_kernel(gated_ref, own_ref, other_ref, weight_ref, out_ref):
    mean = jnp.sum(own_ref[...] + other_ref[...], axis=1, keepdims=True) / (2.0 * COLS)
    inverse = lax.rsqrt(mean + 1e-05)
    for pair in range(HEADS // 2):
        cols = slice(pair * 128, (pair + 1) * 128)
        out_ref[:, cols] = (
            gated_ref[:, cols].astype(f32) * inverse * weight_ref[:, cols]
        ).astype(bf16)


def call(kernel, name, outs, *args, smem=0, flops=10**8, size=4 * 10**6):
    specs = [pl.BlockSpec(memory_space=pltpu.SMEM)] * smem
    specs += [pl.BlockSpec(memory_space=pltpu.VMEM)] * (len(args) - smem)
    many = isinstance(outs, list)
    shapes = [jax.ShapeDtypeStruct(*o) for o in outs] if many else jax.ShapeDtypeStruct(*outs)
    return kernel_call(kernel, name, specs, shapes, flops, size)(*args)


def kernel_call(kernel, name, specs, shapes, flops, size):
    many = isinstance(shapes, list)
    out_specs = pl.BlockSpec(memory_space=pltpu.VMEM)
    return pl.pallas_call(
        kernel,
        name=name,
        in_specs=specs,
        out_specs=[out_specs] * len(shapes) if many else out_specs,
        out_shape=shapes,
        cost_estimate=pl.CostEstimate(flops=flops, bytes_accessed=size, transcendentals=0),
        compiler_params=pltpu.CompilerParams(vmem_limit_bytes=VMEM),
    )


def spot_of(index):
    return index // 16, index // 4 % 4, index % 4


def index_of(row, group, place):
    return row * 16 + group * 4 + place


def along_groups(value, shift):
    pairs = []
    for index in range(ROWS * GROUPS * PLACES):
        row, group, place = spot_of(index)
        pairs.append((index, index_of(row, (group + shift) % GROUPS, place)))
    return lax.ppermute(value, "ctx", pairs)


def along_rows(value, shift):
    pairs = []
    for index in range(ROWS * GROUPS * PLACES):
        row, group, place = spot_of(index)
        if row + shift < ROWS:
            pairs.append((index, index_of(row + shift, group, place)))
    return lax.ppermute(value, "ctx", pairs)


def on_device(
    mixer_input,
    gate_input,
    input_proj,
    output_proj,
    step_size,
    decay_log,
    level_weight,
    norm_weight,
):
    position = lax.axis_index("ctx")
    place = jnp.stack([position // 4 % 4, position // 16]).astype(i32)
    lines = [
        [index_of(row, group, p) for p in range(PLACES)]
        for row in range(ROWS)
        for group in range(GROUPS)
    ]

    def within_line(value):
        return lax.all_to_all(value, "ctx", 0, 0, axis_index_groups=lines)

    states, within = call(
        state_kernel,
        "block_states",
        [((PLACES, MSG, 128), bf16), ((HEADS, 128), f32)],
        mixer_input,
        input_proj,
        decay_log,
        step_size,
    )
    coefs = call(coef_kernel, "level_gains", ((PLACES, 128, 128), bf16), level_weight, within)
    c_all = jnp.broadcast_to(output_proj[None], (PLACES, 128, 128))
    parts = within_line(states)
    side = within_line(jnp.concatenate([c_all, coefs], axis=1))
    local = call(
        local_kernel,
        "local_part",
        ((128, COLS), f32),
        mixer_input,
        input_proj,
        output_proj,
        step_size,
        level_weight,
        within,
        flops=10**10,
        size=10**7,
    )
    group = call(group_kernel, "group_state", ((MSG, 128), bf16), parts)
    others = [along_groups(group, k) for k in (1, 2, 3)]
    total = call(row_kernel, "row_state", ((MSG, 128), bf16), place, group, *others, smem=1)
    rows = [along_rows(total, k) for k in (1, 2, 3)]
    reached = call(
        reach_kernel,
        "level_outputs",
        ((PLACES, 128, PART), bf16),
        place,
        side[:, :128],
        side[:, 128:],
        parts,
        *others,
        *rows,
        smem=1,
    )
    back = within_line(reached)
    gated, square = call(
        gate_kernel, "gate", [((128, COLS), bf16), ((128, 128), f32)], local, back, gate_input
    )
    other = lax.ppermute(square, "head", [(0, 1), (1, 0)])
    return call(
        norm_kernel, "norm", ((128, COLS), bf16), gated, square, other, norm_weight.reshape(1, COLS)
    )


def solution(mesh):
    in_specs = (
        P(("seq", "ctx"), "head"),
        P(("seq", "ctx"), "head"),
        P(("seq", "ctx"), None),
        P(("seq", "ctx"), None),
        P("head", ("seq", "ctx")),
        P("head", ("seq", "ctx")),
        P(None, "head", ("seq", "ctx")),
        P("head"),
    )
    out_specs = P(("seq", "ctx"), "head")
    return jax.shard_map(
        on_device, mesh=mesh, in_specs=in_specs, out_specs=out_specs, check_vma=False
    )
```

time: 507 us -> 127 us (0.25)
  waiting for transfers between devices: 340 us -> 53.4 us
  starting transfers between devices: 110 us -> 56.4 us
  other arithmetic: 26.9 us -> 0.8 us
  between operations: 13.8 us -> 0.21 us
  Pallas kernels: 0 us -> 11.7 us
  local copies, waits for them, and re-layouts: 11 us -> 3.38 us
    ppermute x11 -> x7, waiting for transfers between devices: 315 us -> 26.1 us  [the longest x3 21.1 us: along_groups(): return lax.ppermute(value, 'ctx', pairs)]
    ppermute x11 -> x7, starting transfers between devices: 110 us -> 36.7 us  [the longest x3 24.6 us: along_groups(): return lax.ppermute(value, 'ctx', pairs)]
    all_to_all x0 -> x3, waiting for transfers between devices: none -> 27.3 us  [within_line(): return lax.all_to_all(value, 'ctx', 0, 0, axis_index_groups=lines)]
    all_gather x1 -> x0, waiting for transfers between devices: 25.5 us -> none  [on_device(): lax.all_gather(gated_rows, 'head', axis=1, tiled=True).astype(jnp.float32)]
    all_to_all x0 -> x3, starting transfers between devices: none -> 19.7 us  [within_line(): return lax.all_to_all(value, 'ctx', 0, 0, axis_index_groups=lines)]
    select_n x5 -> x0, other arithmetic: 17.3 us -> none  [on_device(): jnp.where(upper_side, own_keep * other_state + aggregate, other_keep * ag...]
    pallas_call x0 -> x8, Pallas kernels: none -> 11.7 us  [call(): return kernel_call(kernel, name, specs, shapes, flops, size)(*args)]
    another operation x6 -> x0, local copies, waits for them, and re-layouts: 6.27 us -> none
  transfers between devices with their start and end apart: 12 -> 10, of which waited for: 7 -> 7; matrix products, arithmetic and copies ran while one was open for 2% -> 1% of each run, Pallas kernels for 0% -> 2%
where the time goes in v1:
time: 127 us; the launch traced here: 126 us
  starting transfers between devices  56.4 us (44%)
  waiting for transfers between devices  53.4 us (42%)
  Pallas kernels  11.7 us (9%)
  local copies, waits for them, and re-layouts  3.38 us (3%)
    all_to_all x3, waiting for transfers between devices, within_line(): return lax.all_to_all(value, 'ctx', 0, 0, axis_index_groups=lines)  27.3 us
    ppermute x3, starting transfers between devices, along_groups(): return lax.ppermute(value, 'ctx', pairs)  24.6 us
    ppermute x3, waiting for transfers between devices, along_groups(): return lax.ppermute(value, 'ctx', pairs)  21.1 us
    all_to_all x3, starting transfers between devices, within_line(): return lax.all_to_all(value, 'ctx', 0, 0, axis_index_groups=lines)  19.7 us
    pallas_call x8, Pallas kernels, call(): return kernel_call(kernel, name, specs, shapes, flops, size)(*args)  11.7 us
    ppermute x3, starting transfers between devices, along_rows(): return lax.ppermute(value, 'ctx', pairs)  8.77 us
    ppermute x3, waiting for transfers between devices, along_rows(): return lax.ppermute(value, 'ctx', pairs)  4.22 us
    ppermute x1, starting transfers between devices, on_device(): other = lax.ppermute(square, 'head', [(0, 1), (1, 0)])  3.37 us
  transfers between devices with their start and end apart: 10, of which 7 were waited for; matrix products, arithmetic and copies ran while one was open for 1% of the time, Pallas kernels for 2%

profile of v1, /device:TPU:1, one launch (start us, length us, event | category | flops | bytes accessed | tf_op | source)
XLA Modules:
  0.0 125.9 jit_solution(1034984214099765462)
XLA Ops:
  0.0 0.0 copy-start.1
  0.0 1.1 copy-done.1
  1.1 0.0 copy-start.3
  1.1 0.8 copy-done.3
  1.8 0.0 copy-start.6
  1.8 0.7 copy-done.6
  2.6 0.7 copy-done.7
  3.3 0.0 copy-start.9
  3.3 3.4 %block_states.1 = (bf16[4,656,128]{2,1,0:T(8,128)(2,1)}, f32[40,128]{1,0:T(8,128)S(1)}) custom-call(bf16[128,2560]{1,0:T(8,128)(2,1)S(1)} %copy-done.1, bf16[128,128]{1,0:T(8,128)(2,1)S(1)} %copy-done.3, f32[40,128]{1,0:T(8,128)S(1)} %copy-done.6, f32[40,128]{1,0:T(8,128)S(1)} %copy-done.7), custom_call_target="tpu_custom_call" | custom-call | flops 100000000 | bytes 4000000 | tf_op jit(solution)/shard_map/block_states/pallas_call | solution.py:287
  6.7 6.4 %all-to-all-start.1 = ((bf16[4,656,128]{2,1,0:T(8,128)(2,1)}), bf16[4,656,128]{2,1,0:T(8,128)(2,1)S(1)}, u32[]{:S(2)}, u32[]{:S(2)}) async-start(bf16[4,656,128]{2,1,0:T(8,128)(2,1)} %get-tuple-element.10), calls=%async_computation.1 | async-start | bytes 1343488 | tf_op jit(solution)/shard_map/all_to_all | solution.py:348
  13.2 0.0 copy-done.9
  13.2 0.4 level_gains.1
  13.6 0.0 copy-done.5
  13.6 0.7 pad_maximum_fusion
  14.3 12.4 %all-to-all-done.1.parts_ref = bf16[4,656,128]{2,1,0:T(8,128)(2,1)S(1)} async-done(((bf16[4,656,128]{2,1,0:T(8,128)(2,1)}), bf16[4,656,128]{2,1,0:T(8,128)(2,1)S(1)}, u32[]{:S(2)}, u32[]{:S(2)}) %all-to-all-start.1) | async-done | bytes 671776 | tf_op jit(solution)/shard_map/all_to_all | solution.py:348
  26.7 5.0 %all-to-all-start = ((bf16[4,256,128]{2,1,0:T(8,128)(2,1)}), bf16[4,256,128]{2,1,0:T(8,128)(2,1)S(1)}, u32[]{:S(2)}, u32[]{:S(2)}) async-start(bf16[4,256,128]{2,1,0:T(8,128)(2,1)} %pad_maximum_fusion), calls=%async_computation | async-start | bytes 524288 | tf_op jit(solution)/shard_map/all_to_all | solution.py:348
  31.7 0.1 group_state.1.own_ref
  31.8 10.9 %collective-permute-start = (bf16[656,128]{1,0:T(8,128)(2,1)S(1)}, bf16[656,128]{1,0:T(8,128)(2,1)S(1)}, u32[]{:S(2)}, u32[]{:S(2)}) collective-permute-start(bf16[656,128]{1,0:T(8,128)(2,1)S(1)} %group_state.1.own_ref), channel_id=1, source_target_pairs={{0,32},{8,40},{16,48},{24,56},{32,64},{40,72},{48,80},{56,88},{64,... | collective-permute-start | bytes 503816 | tf_op jit(solution)/shard_map/ppermute | solution.py:317
  42.7 8.5 %collective-permute-start.1 = (bf16[656,128]{1,0:T(8,128)(2,1)S(1)}, bf16[656,128]{1,0:T(8,128)(2,1)S(1)}, u32[]{:S(2)}, u32[]{:S(2)}) collective-permute-start(bf16[656,128]{1,0:T(8,128)(2,1)S(1)} %group_state.1.own_ref), channel_id=1, source_target_pairs={{0,64},{8,72},{16,80},{24,88},{32,96},{40,104},{48,112},{56,120},{... | collective-permute-start | bytes 503816 | tf_op jit(solution)/shard_map/ppermute | solution.py:317
  51.3 5.2 %collective-permute-start.2 = (bf16[656,128]{1,0:T(8,128)(2,1)S(1)}, bf16[656,128]{1,0:T(8,128)(2,1)S(1)}, u32[]{:S(2)}, u32[]{:S(2)}) collective-permute-start(bf16[656,128]{1,0:T(8,128)(2,1)S(1)} %group_state.1.own_ref), channel_id=1, source_target_pairs={{0,96},{8,104},{16,112},{24,120},{32,0},{40,8},{48,16},{56,24},{64... | collective-permute-start | bytes 503816 | tf_op jit(solution)/shard_map/ppermute | solution.py:317
  56.5 0.1 pad_add_fusion.place_ref
  56.6 0.0 collective-permute-done.one_ref.g1_ref
  56.6 10.8 %collective-permute-done.1.two_ref.g2_ref = bf16[656,128]{1,0:T(8,128)(2,1)S(1)} collective-permute-done((bf16[656,128]{1,0:T(8,128)(2,1)S(1)}, bf16[656,128]{1,0:T(8,128)(2,1)S(1)}, u32[]{:S(2)}, u32[]{:S(2)}) %collective-permute-start.1) | collective-permute-done | bytes 167968 | tf_op jit(solution)/shard_map/ppermute | solution.py:317
  67.3 10.3 %collective-permute-done.2.three_ref.g3_ref = bf16[656,128]{1,0:T(8,128)(2,1)S(1)} collective-permute-done((bf16[656,128]{1,0:T(8,128)(2,1)S(1)}, bf16[656,128]{1,0:T(8,128)(2,1)S(1)}, u32[]{:S(2)}, u32[]{:S(2)}) %collective-permute-start.2) | collective-permute-done | bytes 167968 | tf_op jit(solution)/shard_map/ppermute | solution.py:317
  77.6 0.7 row_state.1
  78.3 3.1 %collective-permute-start.3 = (bf16[656,128]{1,0:T(8,128)(2,1)S(1)}, bf16[656,128]{1,0:T(8,128)(2,1)S(1)}, u32[]{:S(2)}, u32[]{:S(2)}) collective-permute-start(bf16[656,128]{1,0:T(8,128)(2,1)S(1)} %row_state.1), channel_id=1, source_target_pairs={{0,128},{8,136},{16,144},{24,152},{32,160},{40,168},{48,176},{56,1... | collective-permute-start | bytes 503816 | tf_op jit(solution)/shard_map/ppermute | solution.py:326
  81.5 4.4 %collective-permute-start.4 = (bf16[656,128]{1,0:T(8,128)(2,1)S(1)}, bf16[656,128]{1,0:T(8,128)(2,1)S(1)}, u32[]{:S(2)}, u32[]{:S(2)}) collective-permute-start(bf16[656,128]{1,0:T(8,128)(2,1)S(1)} %row_state.1), channel_id=1, source_target_pairs={{0,256},{8,264},{16,272},{24,280},{32,288},{40,296},{48,304},{56,3... | collective-permute-start | bytes 503816 | tf_op jit(solution)/shard_map/ppermute | solution.py:326
  85.8 1.3 %collective-permute-start.5 = (bf16[656,128]{1,0:T(8,128)(2,1)S(1)}, bf16[656,128]{1,0:T(8,128)(2,1)S(1)}, u32[]{:S(2)}, u32[]{:S(2)}) collective-permute-start(bf16[656,128]{1,0:T(8,128)(2,1)S(1)} %row_state.1), channel_id=1, source_target_pairs={{0,384},{8,392},{16,400},{24,408},{32,416},{40,424},{48,432},{56,4... | collective-permute-start | bytes 503816 | tf_op jit(solution)/shard_map/ppermute | solution.py:326
  87.1 0.0 all-to-all-done
  87.2 0.0 collective-permute-done.3.r1_ref
  87.2 1.3 %collective-permute-done.4.r2_ref = bf16[656,128]{1,0:T(8,128)(2,1)S(1)} collective-permute-done((bf16[656,128]{1,0:T(8,128)(2,1)S(1)}, bf16[656,128]{1,0:T(8,128)(2,1)S(1)}, u32[]{:S(2)}, u32[]{:S(2)}) %collective-permute-start.4) | collective-permute-done | bytes 167968 | tf_op jit(solution)/shard_map/ppermute | solution.py:326
  88.5 2.9 %collective-permute-done.5.r3_ref = bf16[656,128]{1,0:T(8,128)(2,1)S(1)} collective-permute-done((bf16[656,128]{1,0:T(8,128)(2,1)S(1)}, bf16[656,128]{1,0:T(8,128)(2,1)S(1)}, u32[]{:S(2)}, u32[]{:S(2)}) %collective-permute-start.5) | collective-permute-done | bytes 167968 | tf_op jit(solution)/shard_map/ppermute | solution.py:326
  91.4 0.0 copy-start.2
  91.4 3.5 %level_outputs.1 = bf16[4,128,640]{2,1,0:T(8,128)(2,1)} custom-call(s32[2]{0:T(128)S(1)} %pad_add_fusion.place_ref, bf16[4,128,128]{2,1,0:T(8,128)(2,1)S(1)} %get-tuple-element.14.c_ref, bf16[4,128,128]{2,1,0:T(8,128)(2,1)S(1)} %get-tuple-element.13.coef_ref, bf16[4,656,128]{2,1,0:T(8,128)(2,1)S(1)} %all-to-all-done.1.parts_ref, ...), custom_call_target="tpu_custom_call" | custom-call | flops 100000000 | bytes 4000000 | tf_op jit(solution)/shard_map/level_outputs/pallas_call | solution.py:287
  94.9 8.2 %all-to-all-start.2 = ((bf16[4,128,640]{2,1,0:T(8,128)(2,1)}), bf16[4,128,640]{2,1,0:T(8,128)(2,1)S(1)}, u32[]{:S(2)}, u32[]{:S(2)}) async-start(bf16[4,128,640]{2,1,0:T(8,128)(2,1)} %level_outputs.1), calls=%async_computation.2 | async-start | bytes 1310720 | tf_op jit(solution)/shard_map/all_to_all | solution.py:348
  103.2 0.0 copy-done.2
  103.2 0.0 copy-done.4
  103.2 0.0 copy-done.8
  103.2 0.0 copy-start
  103.2 1.8 %local_part.1.local_ref = f32[128,2560]{1,0:T(8,128)S(1)} custom-call(bf16[128,2560]{1,0:T(8,128)(2,1)S(1)} %copy-done.2, bf16[128,128]{1,0:T(8,128)(2,1)S(1)} %copy-done.4, bf16[128,128]{1,0:T(8,128)(2,1)S(1)} %copy-done.5, f32[40,128]{1,0:T(8,128)S(1)} %copy-done.8, f32[7,40,128]{2,1,0:T(8,128)S(1)} %copy-done.9, f32[40,128]{1,0:T(8,128)S(1)} %get-tuple-element.9.within_ref), custom_call_target="tpu_custom_call" | custom-call | flops 10000000000 | bytes 10000000 | tf_op jit(solution)/shard_map/local_part/pallas_call | solution.py:287
  105.0 0.0 copy-start.10
  105.0 14.9 %all-to-all-done.2.reached_ref = bf16[4,128,640]{2,1,0:T(8,128)(2,1)S(1)} async-done(((bf16[4,128,640]{2,1,0:T(8,128)(2,1)}), bf16[4,128,640]{2,1,0:T(8,128)(2,1)S(1)}, u32[]{:S(2)}, u32[]{:S(2)}) %all-to-all-start.2) | async-done | bytes 655392 | tf_op jit(solution)/shard_map/all_to_all | solution.py:348
  120.0 0.0 copy-done
  120.0 0.6 gate.1
  120.6 3.4 %collective-permute-start.6 = (f32[128,128]{1,0:T(8,128)S(1)}, f32[128,128]{1,0:T(8,128)S(1)}, u32[]{:S(2)}, u32[]{:S(2)}) collective-permute-start(f32[128,128]{1,0:T(8,128)S(1)} %get-tuple-element.12.own_ref), channel_id=1, source_target_pairs={{0,4},{4,0},{1,5},{5,1},{2,6},{6,2},{3,7},{7,3},{8,12},{12,8},{9,1... | collective-permute-start | bytes 196616 | tf_op jit(solution)/shard_map/ppermute | solution.py:396
  124.0 0.0 copy-done.10
  124.0 0.9 collective-permute-done.6.other_ref
  124.8 1.1 norm.1
  (7 shorter events, 0.1 us)
Async XLA Ops:
  0.0 1.1 copy-start.1
  1.1 0.8 copy-start.3
  1.8 0.7 copy-start.6
  2.6 0.7 copy-start.7
  3.3 9.9 %copy-start.9 = (f32[7,40,128]{2,1,0:T(8,128)S(1)}, f32[7,40,128]{2,1,0:T(8,128)}, u32[]{:S(2)}) copy-start(f32[7,40,128]{2,1,0:T(8,128)} %weight_ref.3) | copy-start | bytes 430084
  3.3 10.3 %copy-start.5 = (bf16[128,128]{1,0:T(8,128)(2,1)S(1)}, bf16[128,128]{1,0:T(8,128)(2,1)}, u32[]{:S(2)}) copy-start(bf16[128,128]{1,0:T(8,128)(2,1)} %c_ref.1) | copy-start | bytes 98308
  6.7 19.9 %all-to-all-start.1 = ((bf16[4,656,128]{2,1,0:T(8,128)(2,1)}), bf16[4,656,128]{2,1,0:T(8,128)(2,1)S(1)}, u32[]{:S(2)}, u32[]{:S(2)}) async-start(bf16[4,656,128]{2,1,0:T(8,128)(2,1)} %get-tuple-element.10), calls=%async_computation.1 | async-start | bytes 1343488 | tf_op jit(solution)/shard_map/all_to_all | solution.py:348
  26.7 60.5 %all-to-all-start = ((bf16[4,256,128]{2,1,0:T(8,128)(2,1)}), bf16[4,256,128]{2,1,0:T(8,128)(2,1)S(1)}, u32[]{:S(2)}, u32[]{:S(2)}) async-start(bf16[4,256,128]{2,1,0:T(8,128)(2,1)} %pad_maximum_fusion), calls=%async_computation | async-start | bytes 524288 | tf_op jit(solution)/shard_map/all_to_all | solution.py:348
  31.8 24.7 %collective-permute-start = (bf16[656,128]{1,0:T(8,128)(2,1)S(1)}, bf16[656,128]{1,0:T(8,128)(2,1)S(1)}, u32[]{:S(2)}, u32[]{:S(2)}) collective-permute-start(bf16[656,128]{1,0:T(8,128)(2,1)S(1)} %group_state.1.own_ref), channel_id=1, source_target_pairs={{0,32},{8,40},{16,48},{24,56},{32,64},{40,72},{48,80},{56,88},{64,... | collective-permute-start | bytes 503816 | tf_op jit(solution)/shard_map/ppermute | solution.py:317
  42.7 24.6 %collective-permute-start.1 = (bf16[656,128]{1,0:T(8,128)(2,1)S(1)}, bf16[656,128]{1,0:T(8,128)(2,1)S(1)}, u32[]{:S(2)}, u32[]{:S(2)}) collective-permute-start(bf16[656,128]{1,0:T(8,128)(2,1)S(1)} %group_state.1.own_ref), channel_id=1, source_target_pairs={{0,64},{8,72},{16,80},{24,88},{32,96},{40,104},{48,112},{56,120},{... | collective-permute-start | bytes 503816 | tf_op jit(solution)/shard_map/ppermute | solution.py:317
  51.3 26.4 %collective-permute-start.2 = (bf16[656,128]{1,0:T(8,128)(2,1)S(1)}, bf16[656,128]{1,0:T(8,128)(2,1)S(1)}, u32[]{:S(2)}, u32[]{:S(2)}) collective-permute-start(bf16[656,128]{1,0:T(8,128)(2,1)S(1)} %group_state.1.own_ref), channel_id=1, source_target_pairs={{0,96},{8,104},{16,112},{24,120},{32,0},{40,8},{48,16},{56,24},{64... | collective-permute-start | bytes 503816 | tf_op jit(solution)/shard_map/ppermute | solution.py:317
  78.3 8.8 %collective-permute-start.3 = (bf16[656,128]{1,0:T(8,128)(2,1)S(1)}, bf16[656,128]{1,0:T(8,128)(2,1)S(1)}, u32[]{:S(2)}, u32[]{:S(2)}) collective-permute-start(bf16[656,128]{1,0:T(8,128)(2,1)S(1)} %row_state.1), channel_id=1, source_target_pairs={{0,128},{8,136},{16,144},{24,152},{32,160},{40,168},{48,176},{56,1... | collective-permute-start | bytes 503816 | tf_op jit(solution)/shard_map/ppermute | solution.py:326
  81.5 7.1 %collective-permute-start.4 = (bf16[656,128]{1,0:T(8,128)(2,1)S(1)}, bf16[656,128]{1,0:T(8,128)(2,1)S(1)}, u32[]{:S(2)}, u32[]{:S(2)}) collective-permute-start(bf16[656,128]{1,0:T(8,128)(2,1)S(1)} %row_state.1), channel_id=1, source_target_pairs={{0,256},{8,264},{16,272},{24,280},{32,288},{40,296},{48,304},{56,3... | collective-permute-start | bytes 503816 | tf_op jit(solution)/shard_map/ppermute | solution.py:326
  85.8 5.6 %collective-permute-start.5 = (bf16[656,128]{1,0:T(8,128)(2,1)S(1)}, bf16[656,128]{1,0:T(8,128)(2,1)S(1)}, u32[]{:S(2)}, u32[]{:S(2)}) collective-permute-start(bf16[656,128]{1,0:T(8,128)(2,1)S(1)} %row_state.1), channel_id=1, source_target_pairs={{0,384},{8,392},{16,400},{24,408},{32,416},{40,424},{48,432},{56,4... | collective-permute-start | bytes 503816 | tf_op jit(solution)/shard_map/ppermute | solution.py:326
  91.4 11.8 %copy-start.2 = (bf16[128,2560]{1,0:T(8,128)(2,1)S(1)}, bf16[128,2560]{1,0:T(8,128)(2,1)}, u32[]{:S(2)}) copy-start(bf16[128,2560]{1,0:T(8,128)(2,1)} %x_ref.3) | copy-start | bytes 1966084
  91.4 11.8 %copy-start.4 = (bf16[128,128]{1,0:T(8,128)(2,1)S(1)}, bf16[128,128]{1,0:T(8,128)(2,1)}, u32[]{:S(2)}) copy-start(bf16[128,128]{1,0:T(8,128)(2,1)} %b_ref.3) | copy-start | bytes 98308
  91.4 11.8 %copy-start.8 = (f32[40,128]{1,0:T(8,128)S(1)}, f32[40,128]{1,0:T(8,128)}, u32[]{:S(2)}) copy-start(f32[40,128]{1,0:T(8,128)} %step_ref.3) | copy-start | bytes 61444
  94.9 25.0 %all-to-all-start.2 = ((bf16[4,128,640]{2,1,0:T(8,128)(2,1)}), bf16[4,128,640]{2,1,0:T(8,128)(2,1)S(1)}, u32[]{:S(2)}, u32[]{:S(2)}) async-start(bf16[4,128,640]{2,1,0:T(8,128)(2,1)} %level_outputs.1), calls=%async_computation.2 | async-start | bytes 1310720 | tf_op jit(solution)/shard_map/all_to_all | solution.py:348
  103.2 16.8 %copy-start = (bf16[128,2560]{1,0:T(8,128)(2,1)S(1)}, bf16[128,2560]{1,0:T(8,128)(2,1)}, u32[]{:S(2)}) copy-start(bf16[128,2560]{1,0:T(8,128)(2,1)} %gate_ref.1) | copy-start | bytes 1966084
  105.0 18.9 %copy-start.10 = (f32[2560]{0:T(1024)S(1)}, f32[2560]{0:T(1024)}, u32[]{:S(2)}) copy-start(f32[2560]{0:T(1024)} %param.15) | copy-start | bytes 30724
  120.6 4.3 %collective-permute-start.6 = (f32[128,128]{1,0:T(8,128)S(1)}, f32[128,128]{1,0:T(8,128)S(1)}, u32[]{:S(2)}, u32[]{:S(2)}) collective-permute-start(f32[128,128]{1,0:T(8,128)S(1)} %get-tuple-element.12.own_ref), channel_id=1, source_target_pairs={{0,4},{4,0},{1,5},{5,1},{2,6},{6,2},{3,7},{7,3},{8,12},{12,8},{9,1... | collective-permute-start | bytes 196616 | tf_op jit(solution)/shard_map/ppermute | solution.py:396

commit v2 on v1

v2 whole, which is shorter than its diff:
```python
import jax
import jax.numpy as jnp
from jax import lax
from jax.experimental import pallas as pl
from jax.experimental.pallas import tpu as pltpu
from jax.sharding import PartitionSpec as P

ROWS, GROUPS, PLACES = 4, 4, 4
BLOCK = 128
STATE = 128
HEADDIM = 64
HEADS = 40
COLS = HEADS * HEADDIM
PART_HEADS = HEADS // PLACES
PART = COLS // PLACES
TILES = PART // 128
BODY = TILES * STATE
HALF = BODY // 2
META = 16
SIDE = BODY + META
LEVELS = 6
f32, bf16, i32 = jnp.float32, jnp.bfloat16, jnp.int32
VMEM = 24 * 2**20


def dot(a, b):
    return jnp.dot(a, b, preferred_element_type=f32)


def three(v):
    hi = v.astype(bf16)
    rest = v - hi.astype(f32)
    mid = rest.astype(bf16)
    return hi, mid, (rest - mid.astype(f32)).astype(bf16)


def iota(shape, dim):
    return lax.broadcasted_iota(i32, shape, dim)


def ones_where(cond):
    return jnp.where(cond, 1.0, 0.0).astype(bf16)


def row_mod(rows, period, shape):
    r = iota(shape, 0)
    turn = jnp.zeros(shape, i32)
    for k in range(period, rows, period):
        turn = turn + jnp.where(r >= k, 1, 0)
    return r - turn * period, turn


def worker_message(part, x, carry_t, last, b_t, msg_ref):
    head, _ = row_mod(120, HEADS, (128, 128))
    head = jnp.where(iota((128, 128), 0) >= 120, 999, head)
    side = jnp.where(iota((128, 128), 1) >= HEADDIM, 1, 0)
    lane = iota((META, 128), 1)
    lane_term = jnp.where(lane >= 2 * HEADS, 2, jnp.where(lane >= HEADS, 1, 0))
    meta_row = iota((META, 128), 0)
    base = part * PART_HEADS
    spread = [ones_where(head == base + 2 * k + side) for k in range(TILES)]
    scaled = (dot(carry_t, jnp.concatenate(spread, axis=1)) * x.astype(f32)).astype(bf16)
    state = dot(b_t, scaled).astype(bf16)
    meta = jnp.zeros((META, 128), f32)
    for k in range(TILES):
        msg_ref[part, k * STATE : (k + 1) * STATE, :] = state[:, k * 128 : (k + 1) * 128]
        pick = jnp.where(meta_row == 3 * k + lane_term, last, 0.0).astype(bf16)
        meta = meta + dot(pick, spread[k])
    msg_ref[part, BODY:SIDE, :] = meta.astype(bf16)


def state_kernel(
    x_ref, b_ref, c_ref, decay_ref, step_ref, weight_ref, msg_ref, within_ref,
    x_buf, b_buf, c_buf, decay_buf, step_buf, weight_buf, sems,
):
    copies = [
        pltpu.make_async_copy(decay_ref, decay_buf, sems.at[0]),
        pltpu.make_async_copy(step_ref, step_buf, sems.at[1]),
        pltpu.make_async_copy(b_ref, b_buf, sems.at[2]),
    ]
    for part in range(PLACES):
        cols = pl.ds(part * PART, PART)
        copies.append(pltpu.make_async_copy(x_ref.at[:, cols], x_buf.at[part], sems.at[3 + part]))
    copies.append(pltpu.make_async_copy(weight_ref, weight_buf, sems.at[7]))
    copies.append(pltpu.make_async_copy(c_ref, c_buf, sems.at[8]))
    for c in copies:
        c.start()
    upper = ones_where(iota((128, 128), 0) <= iota((128, 128), 1))
    copies[0].wait()
    within = sum(dot(p, upper) for p in three(decay_buf[...]))
    within_ref[...] = within
    total = within[:, 127:128]
    copies[1].wait()
    carry = jnp.exp(total - within) * step_buf[...]
    pad = jnp.zeros((8, 128), f32)

    def stacked(v):
        return jnp.concatenate([p.astype(f32) for p in three(v)] + [pad], axis=0).T

    carry_t = stacked(carry).astype(bf16)
    last = stacked(within)[127:128, :]
    copies[2].wait()
    b_t = b_buf[...].astype(f32).T.astype(bf16)
    for part in range(PLACES):
        copies[3 + part].wait()
        worker_message(part, x_buf[part], carry_t, last, b_t, msg_ref)
    copies[7].wait()
    copies[8].wait()
    gains = level_gains(weight_buf, within)
    for part in range(PLACES):
        msg_ref[part, SIDE : SIDE + 128, :] = c_buf[...]
        msg_ref[part, SIDE + 128 :, :] = gains[part]


def level_gains(weights, within):
    grown = jnp.exp(within)
    rows = [weights[level] * grown for level in range(1, LEVELS + 1)]
    stack = jnp.concatenate(rows + [jnp.zeros((16, 128), f32)], axis=0).T
    hi, lo, _ = three(stack)
    shape = (256, 128)
    head, level = row_mod(240, HEADS, shape)
    level = jnp.where(iota(shape, 0) >= 240, 99, level)
    lane = iota(shape, 1)
    gains = []
    for part in range(PLACES):
        own = head - part * PART_HEADS
        ok = jnp.logical_and(jnp.logical_and(own >= 0, own < PART_HEADS), level < LEVELS)
        target = jnp.where(ok, level * PART_HEADS + own, 999)
        packed = dot(hi, ones_where(lane == target)) + dot(lo, ones_where(lane == target + 64))
        gains.append(packed.astype(bf16))
    return gains


def local_kernel(x_ref, b_ref, c_ref, step_ref, weight_ref, within_ref, out_ref):
    scores = lax.dot_general(
        c_ref[...], b_ref[...], (((1,), (1,)), ((), ())), preferred_element_type=f32
    )
    scores = jnp.where(iota((128, 128), 0) >= iota((128, 128), 1), scores, 0.0)
    pad = jnp.zeros((128 - HEADS, 128), f32)
    within = within_ref[...]
    within_t = jnp.concatenate([within, pad], axis=0).T
    weight_t = jnp.concatenate([weight_ref[0], pad], axis=0).T
    step = step_ref[...]
    left = iota((128, 128), 1) < HEADDIM
    zero = jnp.zeros((128, 128), bf16)

    def mixing(h):
        gap = jnp.minimum(within_t[:, h : h + 1] - within[h : h + 1, :], 0.0)
        gain = weight_t[:, h : h + 1] * jnp.exp(gap)
        return (gain * scores * step[h : h + 1, :]).astype(bf16)

    for pair in range(HEADS // 2):
        cols = slice(pair * 128, (pair + 1) * 128)
        x = x_ref[:, cols]
        both = jnp.concatenate([mixing(2 * pair), mixing(2 * pair + 1)], axis=1)
        sides = jnp.concatenate([jnp.where(left, x, zero), jnp.where(left, zero, x)], axis=0)
        out_ref[:, cols] = dot(both, sides)


def total_of(meta, tile):
    return meta[3 * tile : 3 * tile + 1] + meta[3 * tile + 1 : 3 * tile + 2] + meta[3 * tile + 2 : 3 * tile + 3]


def put_total(meta, tile, total):
    row = iota((META, 128), 0)
    for k, p in enumerate(three(total)):
        meta = jnp.where(row == 3 * tile + k, p.astype(f32), meta)
    return meta


def tile_rows(tile):
    return slice(tile * STATE, (tile + 1) * STATE)


def group_kernel(parts_ref, out_ref):
    metas = [parts_ref[j, BODY:SIDE, :].astype(f32) for j in range(PLACES)]
    meta = jnp.zeros((META, 128), f32)
    for tile in range(TILES):
        rows = tile_rows(tile)
        t = [total_of(m, tile) for m in metas]
        acc = parts_ref[0, rows, :].astype(f32)
        for j in range(1, PLACES):
            acc = jnp.exp(t[j]) * acc + parts_ref[j, rows, :].astype(f32)
        out_ref[rows, :] = acc.astype(bf16)
        meta = put_total(meta, tile, t[0] + t[1] + t[2] + t[3])
    out_ref[BODY:, :] = meta.astype(bf16)


def flag(cond):
    return jnp.where(cond, 1.0, 0.0).astype(f32)


def opposite_tile(top_ref, low_ref, tile):
    start, end = tile * STATE, (tile + 1) * STATE
    if end <= HALF:
        return top_ref[start:end, :].astype(f32)
    if start >= HALF:
        return low_ref[start - HALF : end - HALF, :].astype(f32)
    pieces = [top_ref[start:HALF, :], low_ref[: end - HALF, :]]
    return jnp.concatenate([p.astype(f32) for p in pieces], axis=0)


def group_tiles(g1_ref, top_ref, low_ref, g3_ref, tile):
    rows = tile_rows(tile)
    return (
        g1_ref[rows, :].astype(f32),
        opposite_tile(top_ref, low_ref, tile),
        g3_ref[rows, :].astype(f32),
    )


def group_totals(g1_ref, low_ref, g3_ref):
    return [
        g1_ref[BODY:, :].astype(f32),
        low_ref[BODY - HALF :, :].astype(f32),
        g3_ref[BODY:, :].astype(f32),
    ]


def row_kernel(place_ref, own_ref, g1_ref, top_ref, low_ref, g3_ref, out_ref):
    spot = [(place_ref[0] + GROUPS - k) % GROUPS for k in range(GROUPS)]
    metas = [own_ref[BODY:, :].astype(f32)] + group_totals(g1_ref, low_ref, g3_ref)
    meta = jnp.zeros((META, 128), f32)
    for tile in range(TILES):
        rows = tile_rows(tile)
        t = [total_of(m, tile) for m in metas]
        values = (own_ref[rows, :].astype(f32),) + group_tiles(g1_ref, top_ref, low_ref, g3_ref, tile)
        acc = None
        for k in range(GROUPS):
            gap = sum(t[j] * flag(spot[j] > spot[k]) for j in range(GROUPS) if j != k)
            term = jnp.exp(gap) * values[k]
            acc = term if acc is None else acc + term
        out_ref[rows, :] = acc.astype(bf16)
        meta = put_total(meta, tile, t[0] + t[1] + t[2] + t[3])
    out_ref[BODY:, :] = meta.astype(bf16)


def split(v):
    hi = v.astype(bf16)
    return jnp.concatenate([hi, (v - hi.astype(f32)).astype(bf16)], axis=0)


def wide(pieces):
    return pieces[0] if len(pieces) == 1 else jnp.concatenate(pieces, axis=1)


def gain_spread(tiles, level):
    slot = iota((128, 128), 0)
    slot = jnp.where(slot >= 64, slot - 64, slot)
    side = jnp.where(iota((128, 128), 1) >= HEADDIM, 1, 0)
    return wide(
        [ones_where(slot == level * PART_HEADS + 2 * tile + side) for tile in tiles]
    )


def token_side(parts_ref, place):
    c, coef = parts_ref[place, SIDE : SIDE + 128, :], parts_ref[place, SIDE + 128 :, :]
    return c, jnp.concatenate([c, c], axis=1), coef


def block_lead(metas, place, tiles):
    return wide(
        [jnp.exp(sum(total_of(m, tile) for m in metas[:place])) for tile in tiles]
    )


def near_kernel(place_ref, parts_ref, g1_ref, top_ref, low_ref, g3_ref, out_ref):
    group = place_ref[0]
    part_metas = [parts_ref[j, BODY:SIDE, :].astype(f32) for j in range(PLACES)]
    metas = group_totals(g1_ref, low_ref, g3_ref)
    odd, upper = flag(group % 2 == 1), flag(group >= 2)
    second, third = flag(group == 2), flag(group == 3)
    for start in range(0, TILES, 2):
        tiles = range(start, min(start + 2, TILES))
        low_b, mid_b, high_b, b3, b4, skip = [], [], [], [], [], []
        for tile in tiles:
            rows = tile_rows(tile)
            t = [total_of(m, tile) for m in part_metas]
            s0, s1 = parts_ref[0, rows, :], parts_ref[1, rows, :]
            low_b.append(s0)
            mid_b.append(split(jnp.exp(t[1]) * s0.astype(f32) + s1.astype(f32)))
            high_b.append(parts_ref[2, rows, :])
            skip.append(jnp.exp(t[2]))
            t1, t2 = total_of(metas[0], tile), total_of(metas[1], tile)
            v1, v2, v3 = group_tiles(g1_ref, top_ref, low_ref, g3_ref, tile)
            b3.append(split(odd * v1))
            w2, w3 = upper * jnp.exp(t1), third * jnp.exp(t1 + t2)
            b4.append(split(second * v1 + w2 * v2 + w3 * v3))
        spread = [gain_spread(tiles, level) for level in range(4)]
        low_w, mid_w, high_w = wide(low_b), wide(mid_b), wide(high_b)
        b3_w, b4_w = wide(b3), wide(b4)
        lanes = slice(start * 128, (start + len(tiles)) * 128)
        for place in range(PLACES):
            c, cc, coef = token_side(parts_ref, place)
            acc = dot(coef, spread[2]) * dot(cc, b3_w) + dot(coef, spread[3]) * dot(cc, b4_w)
            if place:
                acc = acc * block_lead(part_metas, place, tiles)
            if place == 1:
                acc = acc + dot(coef, spread[0]) * dot(c, low_w)
            if place == 3:
                acc = acc + dot(coef, spread[0]) * dot(c, high_w)
            if place >= 2:
                term = dot(coef, spread[1]) * dot(cc, mid_w)
                acc = acc + (term * wide(skip) if place == 3 else term)
            out_ref[place, :, lanes] = acc


def far_kernel(
    place_ref, parts_ref, g1_ref, low_ref, g3_ref, r1_ref, r2_ref, r3_ref, near_ref, out_ref
):
    group, row = place_ref[0], place_ref[1]
    part_metas = [parts_ref[j, BODY:SIDE, :].astype(f32) for j in range(PLACES)]
    metas = group_totals(g1_ref, low_ref, g3_ref)
    row_metas = [r[BODY:, :].astype(f32) for r in (r1_ref, r2_ref)]
    odd, upper = flag(row % 2 == 1), flag(row >= 2)
    second, third = flag(row == 2), flag(row == 3)
    for start in range(0, TILES, 2):
        tiles = range(start, min(start + 2, TILES))
        b5, b6 = [], []
        for tile in tiles:
            rows = tile_rows(tile)
            t = [total_of(m, tile) for m in metas]
            t1, t2 = (total_of(m, tile) for m in row_metas)
            lead = jnp.exp(sum(flag(group > k) * t[k] for k in range(3)))
            v1, v2, v3 = (r[rows, :].astype(f32) for r in (r1_ref, r2_ref, r3_ref))
            b5.append(split((lead * odd) * v1))
            w2, w3 = lead * upper * jnp.exp(t1), lead * third * jnp.exp(t1 + t2)
            b6.append(split((lead * second) * v1 + w2 * v2 + w3 * v3))
        spread = [gain_spread(tiles, level) for level in (4, 5)]
        b5_w, b6_w = wide(b5), wide(b6)
        lanes = slice(start * 128, (start + len(tiles)) * 128)
        for place in range(PLACES):
            _, cc, coef = token_side(parts_ref, place)
            acc = dot(coef, spread[0]) * dot(cc, b5_w) + dot(coef, spread[1]) * dot(cc, b6_w)
            if place:
                acc = acc * block_lead(part_metas, place, tiles)
            out_ref[place, :, lanes] = (acc + near_ref[place, :, lanes]).astype(bf16)


def gate_kernel(local_ref, reached_ref, gate_ref, gated_ref, square_ref):
    acc = jnp.zeros((128, 128), f32)
    for pair in range(HEADS // 2):
        cols = slice(pair * 128, (pair + 1) * 128)
        part, tile = pair // TILES, pair % TILES
        mixed = local_ref[:, cols] + reached_ref[part, :, tile * 128 : (tile + 1) * 128].astype(f32)
        gate = gate_ref[:, cols].astype(f32)
        gated = (mixed * (gate / (1.0 + jnp.exp(-gate)))).astype(bf16)
        gated_ref[:, cols] = gated
        wide = gated.astype(f32)
        acc = acc + wide * wide
    square_ref[...] = acc


def norm_kernel(gated_ref, own_ref, other_ref, weight_ref, out_ref):
    mean = jnp.sum(own_ref[...] + other_ref[...], axis=1, keepdims=True) / (2.0 * COLS)
    inverse = jnp.broadcast_to(lax.rsqrt(mean + 1e-05), (128, 128))
    for pair in range(HEADS // 2):
        cols = slice(pair * 128, (pair + 1) * 128)
        out_ref[:, cols] = (
            gated_ref[:, cols].astype(f32) * inverse * weight_ref[:, cols]
        ).astype(bf16)


def call(
    kernel, name, outs, *args, smem=0, far=0, scratch=(), flops=10**8, size=4 * 10**6, vmem=VMEM
):
    whole = pl.BlockSpec(memory_space=pltpu.VMEM)
    specs = [pl.BlockSpec(memory_space=pltpu.SMEM)] * smem
    specs += [pl.BlockSpec(memory_space=pl.ANY)] * far
    specs += [whole] * (len(args) - smem - far)
    return pl.pallas_call(
        kernel,
        name=name,
        in_specs=specs,
        out_specs=[whole] * len(outs),
        out_shape=[jax.ShapeDtypeStruct(*o) for o in outs],
        scratch_shapes=list(scratch),
        cost_estimate=pl.CostEstimate(flops=flops, bytes_accessed=size, transcendentals=0),
        compiler_params=pltpu.CompilerParams(vmem_limit_bytes=vmem),
    )(*args)


def spot_of(index):
    return index // 16, index // 4 % 4, index % 4


def index_of(row, group, place):
    return row * 16 + group * 4 + place


def to_group(value, shift):
    pairs = []
    for index in range(ROWS * GROUPS * PLACES):
        row, group, place = spot_of(index)
        pairs.append((index, index_of(row, (group + shift) % GROUPS, place)))
    return lax.ppermute(value, "ctx", pairs)


def to_row(value, shift):
    pairs = []
    for index in range(ROWS * GROUPS * PLACES):
        row, group, place = spot_of(index)
        if row + shift < ROWS:
            pairs.append((index, index_of(row + shift, group, place)))
    return lax.ppermute(value, "ctx", pairs)


LINES = [[index_of(r, g, p) for p in range(PLACES)] for r in range(ROWS) for g in range(GROUPS)]


def exchange(value, lines):
    return lax.all_to_all(value, "ctx", 0, 0, axis_index_groups=lines)


def on_device(
    mixer_input,
    gate_input,
    input_proj,
    output_proj,
    step_size,
    decay_log,
    level_weight,
    norm_weight,
):
    position = lax.axis_index("ctx")
    group = position // 4 % 4
    place = jnp.stack([group, position // 16]).astype(i32)

    messages, within = call(
        state_kernel,
        "block_states",
        [((PLACES, SIDE + 256, 128), bf16), ((HEADS, 128), f32)],
        mixer_input,
        input_proj,
        output_proj,
        decay_log,
        step_size,
        level_weight,
        far=6,
        vmem=60 * 2**20,
        scratch=[
            pltpu.VMEM((PLACES, 128, PART), bf16),
            pltpu.VMEM((128, 128), bf16),
            pltpu.VMEM((128, 128), bf16),
            pltpu.VMEM((HEADS, 128), f32),
            pltpu.VMEM((HEADS, 128), f32),
            pltpu.VMEM((LEVELS + 1, HEADS, 128), f32),
            pltpu.SemaphoreType.DMA((9,)),
        ],
    )
    (local,) = call(
        local_kernel,
        "local_part",
        [((128, COLS), f32)],
        mixer_input,
        input_proj,
        output_proj,
        step_size,
        level_weight,
        within,
        flops=10**10,
        size=10**7,
    )
    parts = exchange(messages, LINES)
    (own,) = call(group_kernel, "group_state", [((BODY + META, 128), bf16)], parts)
    before, after = to_group(own, 1), to_group(own, 3)
    top, low = to_group(before[:HALF], 1), to_group(after[HALF:], 3)
    groups = (before, top, low, after)
    (total,) = call(
        row_kernel, "row_state", [((BODY + META, 128), bf16)], place, own, *groups, smem=1
    )
    rows = [to_row(total, k) for k in (1, 2, 3)]
    (near,) = call(
        near_kernel,
        "near_levels",
        [((PLACES, 128, PART), f32)],
        place,
        parts,
        *groups,
        smem=1,
        flops=10**10,
    )
    (reached,) = call(
        far_kernel,
        "far_levels",
        [((PLACES, 128, PART), bf16)],
        place,
        parts,
        before,
        low,
        after,
        *rows,
        near,
        smem=1,
    )
    back = exchange(reached, LINES)
    gated, square = call(
        gate_kernel, "gate", [((128, COLS), bf16), ((128, 128), f32)], local, back, gate_input
    )
    other = lax.ppermute(square, "head", [(0, 1), (1, 0)])
    (out,) = call(
        norm_kernel,
        "norm",
        [((128, COLS), bf16)],
        gated,
        square,
        other,
        norm_weight.reshape(1, COLS),
    )
    return out


def solution(mesh):
    in_specs = (
        P(("seq", "ctx"), "head"),
        P(("seq", "ctx"), "head"),
        P(("seq", "ctx"), None),
        P(("seq", "ctx"), None),
        P("head", ("seq", "ctx")),
        P("head", ("seq", "ctx")),
        P(None, "head", ("seq", "ctx")),
        P("head"),
    )
    out_specs = P(("seq", "ctx"), "head")
    return jax.shard_map(
        on_device, mesh=mesh, in_specs=in_specs, out_specs=out_specs, check_vma=False
    )
```

time: 127 us -> 119 us (0.937)
  blocking collectives: 0 us -> 28 us
  starting transfers between devices: 56.4 us -> 39.5 us
  waiting for transfers between devices: 53.4 us -> 37.7 us
  local copies, waits for them, and re-layouts: 3.38 us -> 0.06 us
  Pallas kernels: 11.7 us -> 13 us
    all_to_all x0 -> x1, blocking collectives: none -> 28 us  [exchange(): return lax.all_to_all(value, 'ctx', 0, 0, axis_index_groups=lines)]
    all_to_all x3 -> x1, starting transfers between devices: 19.7 us -> 3.63 us  [exchange(): return lax.all_to_all(value, 'ctx', 0, 0, axis_index_groups=lines)]
    all_to_all x3 -> x1, waiting for transfers between devices: 27.3 us -> 13.8 us  [exchange(): return lax.all_to_all(value, 'ctx', 0, 0, axis_index_groups=lines)]
    unnamed x22 -> x16, local copies, waits for them, and re-layouts: 3.33 us -> 0.04 us
    ppermute x6 -> x7, waiting for transfers between devices: 25.3 us -> 23.1 us  [the longest x4 20.8 us: to_group(): return lax.ppermute(value, 'ctx', pairs)]
    ppermute x6 -> x7, starting transfers between devices: 33.4 us -> 31.5 us  [the longest x4 22.7 us: to_group(): return lax.ppermute(value, 'ctx', pairs)]
  transfers between devices with their start and end apart: 10 -> 9, of which waited for: 7 -> 5; matrix products, arithmetic and copies ran while one was open for 1% -> 0% of each run, Pallas kernels for 2% -> 3%
where the time goes in v2:
time: 119 us
  starting transfers between devices  39.5 us (33%)
  waiting for transfers between devices  37.7 us (32%)
  blocking collectives  28 us (24%)
  Pallas kernels  13 us (11%)
    all_to_all x1, blocking collectives, exchange(): return lax.all_to_all(value, 'ctx', 0, 0, axis_index_groups=lines)  28 us
    ppermute x4, starting transfers between devices, to_group(): return lax.ppermute(value, 'ctx', pairs)  22.7 us
    ppermute x4, waiting for transfers between devices, to_group(): return lax.ppermute(value, 'ctx', pairs)  20.8 us
    all_to_all x1, waiting for transfers between devices, exchange(): return lax.all_to_all(value, 'ctx', 0, 0, axis_index_groups=lines)  13.8 us
    pallas_call x8, Pallas kernels, call(): pl.pallas_call(kernel, name=name, in_specs=specs, out_specs=[whole] * len...  13 us
    ppermute x3, starting transfers between devices, to_row(): return lax.ppermute(value, 'ctx', pairs)  8.75 us
    ppermute x1, starting transfers between devices, on_device(): other = lax.ppermute(square, 'head', [(0, 1), (1, 0)])  4.45 us
    all_to_all x1, starting transfers between devices, exchange(): return lax.all_to_all(value, 'ctx', 0, 0, axis_index_groups=lines)  3.63 us
  transfers between devices with their start and end apart: 9, of which 5 were waited for; matrix products, arithmetic and copies ran while one was open for 0% of the time, Pallas kernels for 3%

profile of v2, /device:TPU:1, one launch (start us, length us, event | category | flops | bytes accessed | tf_op | source)
XLA Modules:
  0.0 118.6 jit_solution(415958310311792382)
XLA Ops:
  0.0 4.3 %block_states.1 = (bf16[4,912,128]{2,1,0:T(8,128)(2,1)}, f32[40,128]{1,0:T(8,128)}) custom-call(bf16[128,2560]{1,0:T(8,128)(2,1)} %x_ref.3, bf16[128,128]{1,0:T(8,128)(2,1)} %b_ref.3, bf16[128,128]{1,0:T(8,128)(2,1)} %c_ref.3, f32[40,128]{1,0:T(8,128)} %decay_ref.1, f32[40,128]{1,0:T(8,128)} %step_ref.3, f32[7,40,128]{2,1,0:T(8,128)} %weight_ref.3), custom_call_target="tpu_custom_call" | custom-call | flops 100000000 | bytes 4000000 | tf_op jit(solution)/shard_map/block_states/pallas_call | solution.py:371
  4.4 28.0 %all_to_all.10.parts_ref = bf16[4,912,128]{2,1,0:T(8,128)(2,1)S(1)} all-to-all(bf16[4,912,128]{2,1,0:T(8,128)(2,1)} %get-tuple-element.10), channel_id=1, replica_groups={{0,8,16,24},{32,40,48,56},{64,72,80,88},{96,104,112,120},{128,136,144,1..., dimensions={0} | all-to-all | bytes 1867776 | tf_op jit(solution)/shard_map/all_to_all | solution.py:412
  32.3 0.1 group_state.1.own_ref
  32.5 11.6 %collective-permute-start.1 = (bf16[656,128]{1,0:T(8,128)(2,1)S(1)}, bf16[656,128]{1,0:T(8,128)(2,1)S(1)}, u32[]{:S(2)}, u32[]{:S(2)}) collective-permute-start(bf16[656,128]{1,0:T(8,128)(2,1)S(1)} %group_state.1.own_ref), channel_id=1, source_target_pairs={{0,96},{8,104},{16,112},{24,120},{32,0},{40,8},{48,16},{56,24},{64... | collective-permute-start | bytes 503816 | tf_op jit(solution)/shard_map/ppermute | solution.py:396
  44.1 1.9 %collective-permute-start = (bf16[656,128]{1,0:T(8,128)(2,1)S(1)}, bf16[656,128]{1,0:T(8,128)(2,1)S(1)}, u32[]{:S(2)}, u32[]{:S(2)}) collective-permute-start(bf16[656,128]{1,0:T(8,128)(2,1)S(1)} %group_state.1.own_ref), channel_id=1, source_target_pairs={{0,32},{8,40},{16,48},{24,56},{32,64},{40,72},{48,80},{56,88},{64,... | collective-permute-start | bytes 503816 | tf_op jit(solution)/shard_map/ppermute | solution.py:396
  46.0 12.1 %collective-permute-done.1.g3_ref = bf16[656,128]{1,0:T(8,128)(2,1)S(1)} collective-permute-done((bf16[656,128]{1,0:T(8,128)(2,1)S(1)}, bf16[656,128]{1,0:T(8,128)(2,1)S(1)}, u32[]{:S(2)}, u32[]{:S(2)}) %collective-permute-start.1) | collective-permute-done | bytes 167968 | tf_op jit(solution)/shard_map/ppermute | solution.py:396
  58.1 6.6 %collective-permute-start.2 = (bf16[336,128]{1,0:T(8,128)(2,1)S(1)}, bf16[336,128]{1,0:T(8,128)(2,1)S(1)}, u32[]{:S(2)}, u32[]{:S(2)}) collective-permute-start(bf16[336,128]{1,0:T(8,128)(2,1)S(1)} %slice.8), channel_id=1, source_target_pairs={{0,96},{8,104},{16,112},{24,120},{32,0},{40,8},{48,16},{56,24},{64... | collective-permute-start | bytes 258056 | tf_op jit(solution)/shard_map/ppermute | solution.py:396
  64.7 0.0 collective-permute-done.g1_ref
  64.7 2.6 %collective-permute-start.3 = (bf16[320,128]{1,0:T(8,128)(2,1)S(1)}, bf16[320,128]{1,0:T(8,128)(2,1)S(1)}, u32[]{:S(2)}, u32[]{:S(2)}) collective-permute-start(bf16[320,128]{1,0:T(8,128)(2,1)S(1)} %slice.9), channel_id=1, source_target_pairs={{0,32},{8,40},{16,48},{24,56},{32,64},{40,72},{48,80},{56,88},{64,... | collective-permute-start | bytes 245768 | tf_op jit(solution)/shard_map/ppermute | solution.py:396
  67.4 0.1 pad_add_fusion.place_ref
  67.4 8.7 %collective-permute-done.3.top_ref = bf16[320,128]{1,0:T(8,128)(2,1)S(1)} collective-permute-done((bf16[320,128]{1,0:T(8,128)(2,1)S(1)}, bf16[320,128]{1,0:T(8,128)(2,1)S(1)}, u32[]{:S(2)}, u32[]{:S(2)}) %collective-permute-start.3) | collective-permute-done | bytes 81952 | tf_op jit(solution)/shard_map/ppermute | solution.py:396
  76.2 0.0 collective-permute-done.2.low_ref
  76.2 0.7 row_state.1
  76.9 3.1 %collective-permute-start.4 = (bf16[656,128]{1,0:T(8,128)(2,1)S(1)}, bf16[656,128]{1,0:T(8,128)(2,1)S(1)}, u32[]{:S(2)}, u32[]{:S(2)}) collective-permute-start(bf16[656,128]{1,0:T(8,128)(2,1)S(1)} %row_state.1), channel_id=1, source_target_pairs={{0,128},{8,136},{16,144},{24,152},{32,160},{40,168},{48,176},{56,1... | collective-permute-start | bytes 503816 | tf_op jit(solution)/shard_map/ppermute | solution.py:405
  80.0 4.3 %collective-permute-start.5 = (bf16[656,128]{1,0:T(8,128)(2,1)S(1)}, bf16[656,128]{1,0:T(8,128)(2,1)S(1)}, u32[]{:S(2)}, u32[]{:S(2)}) collective-permute-start(bf16[656,128]{1,0:T(8,128)(2,1)S(1)} %row_state.1), channel_id=1, source_target_pairs={{0,256},{8,264},{16,272},{24,280},{32,288},{40,296},{48,304},{56,3... | collective-permute-start | bytes 503816 | tf_op jit(solution)/shard_map/ppermute | solution.py:405
  84.4 1.3 %collective-permute-start.6 = (bf16[656,128]{1,0:T(8,128)(2,1)S(1)}, bf16[656,128]{1,0:T(8,128)(2,1)S(1)}, u32[]{:S(2)}, u32[]{:S(2)}) collective-permute-start(bf16[656,128]{1,0:T(8,128)(2,1)S(1)} %row_state.1), channel_id=1, source_target_pairs={{0,384},{8,392},{16,400},{24,408},{32,416},{40,424},{48,432},{56,4... | collective-permute-start | bytes 503816 | tf_op jit(solution)/shard_map/ppermute | solution.py:405
  85.7 1.8 %near_levels.1.near_ref = f32[4,128,640]{2,1,0:T(8,128)S(1)} custom-call(s32[2]{0:T(128)S(1)} %pad_add_fusion.place_ref, bf16[4,912,128]{2,1,0:T(8,128)(2,1)S(1)} %all_to_all.10.parts_ref, bf16[656,128]{1,0:T(8,128)(2,1)S(1)} %collective-permute-done.g1_ref, bf16[320,128]{1,0:T(8,128)(2,1)S(1)} %collective-permute-done.3.top_ref, ...), custom_call_target="tpu_custom_call" | custom-call | flops 10000000000 | bytes 4000000 | tf_op jit(solution)/shard_map/near_levels/pallas_call | solution.py:371
  87.5 0.0 collective-permute-done.4.r1_ref
  87.5 0.0 collective-permute-done.5.r2_ref
  87.6 2.3 %collective-permute-done.6.r3_ref = bf16[656,128]{1,0:T(8,128)(2,1)S(1)} collective-permute-done((bf16[656,128]{1,0:T(8,128)(2,1)S(1)}, bf16[656,128]{1,0:T(8,128)(2,1)S(1)}, u32[]{:S(2)}, u32[]{:S(2)}) %collective-permute-start.6) | collective-permute-done | bytes 167968 | tf_op jit(solution)/shard_map/ppermute | solution.py:405
  89.9 2.4 %far_levels.1 = bf16[4,128,640]{2,1,0:T(8,128)(2,1)} custom-call(s32[2]{0:T(128)S(1)} %pad_add_fusion.place_ref, bf16[4,912,128]{2,1,0:T(8,128)(2,1)S(1)} %all_to_all.10.parts_ref, bf16[656,128]{1,0:T(8,128)(2,1)S(1)} %collective-permute-done.g1_ref, bf16[336,128]{1,0:T(8,128)(2,1)S(1)} %collective-permute-done.2.low_ref, ...), custom_call_target="tpu_custom_call" | custom-call | flops 100000000 | bytes 4000000 | tf_op jit(solution)/shard_map/far_levels/pallas_call | solution.py:371
  92.2 0.0 copy-start.1
  92.2 0.0 copy-start.2
  92.2 0.0 copy-start.3
  92.2 0.0 copy-start.4
  92.3 0.0 copy-start.5
  92.3 0.0 copy-start.6
  92.3 3.6 %all-to-all-start.1 = ((bf16[4,128,640]{2,1,0:T(8,128)(2,1)}), bf16[4,128,640]{2,1,0:T(8,128)(2,1)S(1)}, u32[]{:S(2)}, u32[]{:S(2)}) async-start(bf16[4,128,640]{2,1,0:T(8,128)(2,1)} %far_levels.1), calls=%async_computation.1 | async-start | bytes 1310720 | tf_op jit(solution)/shard_map/all_to_all | solution.py:412
  95.9 0.0 copy-done.1
  95.9 0.0 copy-done.2
  95.9 0.0 copy-done.3
  95.9 0.0 copy-done.4
  96.0 0.0 copy-done.5
  96.0 0.0 copy-done.6
  96.0 0.0 copy-start
  96.0 1.8 %local_part.1.local_ref = f32[128,2560]{1,0:T(8,128)S(1)} custom-call(bf16[128,2560]{1,0:T(8,128)(2,1)S(1)} %copy-done.1, bf16[128,128]{1,0:T(8,128)(2,1)S(1)} %copy-done.3, bf16[128,128]{1,0:T(8,128)(2,1)S(1)} %copy-done.4, f32[40,128]{1,0:T(8,128)S(1)} %copy-done.5, f32[7,40,128]{2,1,0:T(8,128)S(1)} %copy-done.2, f32[40,128]{1,0:T(8,128)S(1)} %copy-done.6), custom_call_target="tpu_custom_call" | custom-call | flops 10000000000 | bytes 10000000 | tf_op jit(solution)/shard_map/local_part/pallas_call | solution.py:371
  97.8 0.0 copy-start.7
  97.8 13.8 %all-to-all-done.1.reached_ref = bf16[4,128,640]{2,1,0:T(8,128)(2,1)S(1)} async-done(((bf16[4,128,640]{2,1,0:T(8,128)(2,1)}), bf16[4,128,640]{2,1,0:T(8,128)(2,1)S(1)}, u32[]{:S(2)}, u32[]{:S(2)}) %all-to-all-start.1) | async-done | bytes 655392 | tf_op jit(solution)/shard_map/all_to_all | solution.py:412
  111.6 0.0 copy-done
  111.6 0.6 gate.1
  112.2 4.5 %collective-permute-start.7 = (f32[128,128]{1,0:T(8,128)S(1)}, f32[128,128]{1,0:T(8,128)S(1)}, u32[]{:S(2)}, u32[]{:S(2)}) collective-permute-start(f32[128,128]{1,0:T(8,128)S(1)} %get-tuple-element.12.own_ref), channel_id=1, source_target_pairs={{0,4},{4,0},{1,5},{5,1},{2,6},{6,2},{3,7},{7,3},{8,12},{12,8},{9,1... | collective-permute-start | bytes 196616 | tf_op jit(solution)/shard_map/ppermute | solution.py:500
  116.7 0.0 copy-done.7
  116.7 0.9 collective-permute-done.7.other_ref
  117.5 1.1 norm.1
  (3 shorter events, 0.0 us)
Async XLA Ops:
  32.5 25.7 %collective-permute-start.1 = (bf16[656,128]{1,0:T(8,128)(2,1)S(1)}, bf16[656,128]{1,0:T(8,128)(2,1)S(1)}, u32[]{:S(2)}, u32[]{:S(2)}) collective-permute-start(bf16[656,128]{1,0:T(8,128)(2,1)S(1)} %group_state.1.own_ref), channel_id=1, source_target_pairs={{0,96},{8,104},{16,112},{24,120},{32,0},{40,8},{48,16},{56,24},{64... | collective-permute-start | bytes 503816 | tf_op jit(solution)/shard_map/ppermute | solution.py:396
  44.1 20.6 %collective-permute-start = (bf16[656,128]{1,0:T(8,128)(2,1)S(1)}, bf16[656,128]{1,0:T(8,128)(2,1)S(1)}, u32[]{:S(2)}, u32[]{:S(2)}) collective-permute-start(bf16[656,128]{1,0:T(8,128)(2,1)S(1)} %group_state.1.own_ref), channel_id=1, source_target_pairs={{0,32},{8,40},{16,48},{24,56},{32,64},{40,72},{48,80},{56,88},{64,... | collective-permute-start | bytes 503816 | tf_op jit(solution)/shard_map/ppermute | solution.py:396
  58.1 18.1 %collective-permute-start.2 = (bf16[336,128]{1,0:T(8,128)(2,1)S(1)}, bf16[336,128]{1,0:T(8,128)(2,1)S(1)}, u32[]{:S(2)}, u32[]{:S(2)}) collective-permute-start(bf16[336,128]{1,0:T(8,128)(2,1)S(1)} %slice.8), channel_id=1, source_target_pairs={{0,96},{8,104},{16,112},{24,120},{32,0},{40,8},{48,16},{56,24},{64... | collective-permute-start | bytes 258056 | tf_op jit(solution)/shard_map/ppermute | solution.py:396
  64.7 11.5 %collective-permute-start.3 = (bf16[320,128]{1,0:T(8,128)(2,1)S(1)}, bf16[320,128]{1,0:T(8,128)(2,1)S(1)}, u32[]{:S(2)}, u32[]{:S(2)}) collective-permute-start(bf16[320,128]{1,0:T(8,128)(2,1)S(1)} %slice.9), channel_id=1, source_target_pairs={{0,32},{8,40},{16,48},{24,56},{32,64},{40,72},{48,80},{56,88},{64,... | collective-permute-start | bytes 245768 | tf_op jit(solution)/shard_map/ppermute | solution.py:396
  76.9 10.6 %collective-permute-start.4 = (bf16[656,128]{1,0:T(8,128)(2,1)S(1)}, bf16[656,128]{1,0:T(8,128)(2,1)S(1)}, u32[]{:S(2)}, u32[]{:S(2)}) collective-permute-start(bf16[656,128]{1,0:T(8,128)(2,1)S(1)} %row_state.1), channel_id=1, source_target_pairs={{0,128},{8,136},{16,144},{24,152},{32,160},{40,168},{48,176},{56,1... | collective-permute-start | bytes 503816 | tf_op jit(solution)/shard_map/ppermute | solution.py:405
  80.0 7.5 %collective-permute-start.5 = (bf16[656,128]{1,0:T(8,128)(2,1)S(1)}, bf16[656,128]{1,0:T(8,128)(2,1)S(1)}, u32[]{:S(2)}, u32[]{:S(2)}) collective-permute-start(bf16[656,128]{1,0:T(8,128)(2,1)S(1)} %row_state.1), channel_id=1, source_target_pairs={{0,256},{8,264},{16,272},{24,280},{32,288},{40,296},{48,304},{56,3... | collective-permute-start | bytes 503816 | tf_op jit(solution)/shard_map/ppermute | solution.py:405
  84.4 5.5 %collective-permute-start.6 = (bf16[656,128]{1,0:T(8,128)(2,1)S(1)}, bf16[656,128]{1,0:T(8,128)(2,1)S(1)}, u32[]{:S(2)}, u32[]{:S(2)}) collective-permute-start(bf16[656,128]{1,0:T(8,128)(2,1)S(1)} %row_state.1), channel_id=1, source_target_pairs={{0,384},{8,392},{16,400},{24,408},{32,416},{40,424},{48,432},{56,4... | collective-permute-start | bytes 503816 | tf_op jit(solution)/shard_map/ppermute | solution.py:405
  92.2 3.7 %copy-start.1 = (bf16[128,2560]{1,0:T(8,128)(2,1)S(1)}, bf16[128,2560]{1,0:T(8,128)(2,1)}, u32[]{:S(2)}) copy-start(bf16[128,2560]{1,0:T(8,128)(2,1)} %x_ref.3) | copy-start | bytes 1966084
  92.2 3.7 %copy-start.2 = (f32[7,40,128]{2,1,0:T(8,128)S(1)}, f32[7,40,128]{2,1,0:T(8,128)}, u32[]{:S(2)}) copy-start(f32[7,40,128]{2,1,0:T(8,128)} %weight_ref.3) | copy-start | bytes 430084
  92.2 3.7 %copy-start.3 = (bf16[128,128]{1,0:T(8,128)(2,1)S(1)}, bf16[128,128]{1,0:T(8,128)(2,1)}, u32[]{:S(2)}) copy-start(bf16[128,128]{1,0:T(8,128)(2,1)} %b_ref.3) | copy-start | bytes 98308
  92.2 3.7 %copy-start.4 = (bf16[128,128]{1,0:T(8,128)(2,1)S(1)}, bf16[128,128]{1,0:T(8,128)(2,1)}, u32[]{:S(2)}) copy-start(bf16[128,128]{1,0:T(8,128)(2,1)} %c_ref.3) | copy-start | bytes 98308
  92.3 3.7 %copy-start.5 = (f32[40,128]{1,0:T(8,128)S(1)}, f32[40,128]{1,0:T(8,128)}, u32[]{:S(2)}) copy-start(f32[40,128]{1,0:T(8,128)} %step_ref.3) | copy-start | bytes 61444
  92.3 3.7 %copy-start.6 = (f32[40,128]{1,0:T(8,128)S(1)}, f32[40,128]{1,0:T(8,128)}, u32[]{:S(2)}) copy-start(f32[40,128]{1,0:T(8,128)} %get-tuple-element.9.within_ref) | copy-start | bytes 61444
  92.3 19.3 %all-to-all-start.1 = ((bf16[4,128,640]{2,1,0:T(8,128)(2,1)}), bf16[4,128,640]{2,1,0:T(8,128)(2,1)S(1)}, u32[]{:S(2)}, u32[]{:S(2)}) async-start(bf16[4,128,640]{2,1,0:T(8,128)(2,1)} %far_levels.1), calls=%async_computation.1 | async-start | bytes 1310720 | tf_op jit(solution)/shard_map/all_to_all | solution.py:412
  96.0 15.6 %copy-start = (bf16[128,2560]{1,0:T(8,128)(2,1)S(1)}, bf16[128,2560]{1,0:T(8,128)(2,1)}, u32[]{:S(2)}) copy-start(bf16[128,2560]{1,0:T(8,128)(2,1)} %gate_ref.1) | copy-start | bytes 1966084
  97.8 18.8 %copy-start.7 = (f32[2560]{0:T(1024)S(1)}, f32[2560]{0:T(1024)}, u32[]{:S(2)}) copy-start(f32[2560]{0:T(1024)} %param.15) | copy-start | bytes 30724
  112.2 5.3 %collective-permute-start.7 = (f32[128,128]{1,0:T(8,128)S(1)}, f32[128,128]{1,0:T(8,128)S(1)}, u32[]{:S(2)}, u32[]{:S(2)}) collective-permute-start(f32[128,128]{1,0:T(8,128)S(1)} %get-tuple-element.12.own_ref), channel_id=1, source_target_pairs={{0,4},{4,0},{1,5},{5,1},{2,6},{6,2},{3,7},{7,3},{8,12},{12,8},{9,1... | collective-permute-start | bytes 196616 | tf_op jit(solution)/shard_map/ppermute | solution.py:500

commit v3 on v2

v3 whole, which is shorter than its diff:
```python
import functools

import jax
import jax.numpy as jnp
from jax import lax
from jax.experimental import pallas as pl
from jax.experimental.pallas import tpu as pltpu
from jax.sharding import PartitionSpec as P

ROWS, GROUPS, PLACES = 4, 4, 4
BLOCK = 128
STATE = 128
HEADDIM = 64
HEADS = 40
COLS = HEADS * HEADDIM
PART_HEADS = HEADS // PLACES
PART = COLS // PLACES
TILES = PART // 128
BODY = TILES * STATE
AHEAD = 3
META = 16
SIDE = BODY + META
KEEP = SIDE + 64
MSG = KEEP + 64
LEVELS = 6
FIRST, SECOND = (2, 3, 1), (0,)
MASKS = FIRST + SECOND
f32, bf16, i32 = jnp.float32, jnp.bfloat16, jnp.int32
VMEM = 24 * 2**20


def spots():
    position = lax.axis_index("ctx")
    return position // 4 % 4, position // 16, position % 4, lax.axis_index("head")


def dot(a, b):
    return jnp.dot(a, b, preferred_element_type=f32)


def three(v):
    hi = v.astype(bf16)
    rest = v - hi.astype(f32)
    mid = rest.astype(bf16)
    return hi, mid, (rest - mid.astype(f32)).astype(bf16)


def iota(shape, dim):
    return lax.broadcasted_iota(i32, shape, dim)


def ones_where(cond):
    return jnp.where(cond, 1.0, 0.0).astype(bf16)


def row_mod(rows, period, shape):
    r = iota(shape, 0)
    turn = jnp.zeros(shape, i32)
    for k in range(period, rows, period):
        turn = turn + jnp.where(r >= k, 1, 0)
    return r - turn * period, turn


def worker_message(part, x, carry_t, last, b_t, gains, c_half, msg_ref):
    head, _ = row_mod(120, HEADS, (128, 128))
    head = jnp.where(iota((128, 128), 0) >= 120, 999, head)
    side = jnp.where(iota((128, 128), 1) >= HEADDIM, 1, 0)
    lane = iota((META, 128), 1)
    lane_term = jnp.where(lane >= 2 * HEADS, 2, jnp.where(lane >= HEADS, 1, 0))
    meta_row = iota((META, 128), 0)
    base = part * PART_HEADS
    spread = [ones_where(head - base == 2 * k + side) for k in range(TILES)]
    scaled = (dot(carry_t, jnp.concatenate(spread, axis=1)) * x.astype(f32)).astype(bf16)
    state = dot(b_t, scaled).astype(bf16)
    meta = jnp.zeros((META, 128), f32)
    for k in range(TILES):
        msg_ref[k * STATE : (k + 1) * STATE, :] = state[:, k * 128 : (k + 1) * 128]
        pick = jnp.where(meta_row == 3 * k + lane_term, last, 0.0).astype(bf16)
        meta = meta + dot(pick, spread[k])
    msg_ref[BODY:SIDE, :] = meta.astype(bf16)
    msg_ref[SIDE:KEEP, :] = level_gains(part, gains)
    msg_ref[KEEP:, :] = c_half


def level_gains(part, gains):
    shape = (256, 128)
    head, level = row_mod(240, HEADS, shape)
    level = jnp.where(iota(shape, 0) >= 240, 99, level)
    own = head - part * PART_HEADS
    ok = jnp.logical_and(jnp.logical_and(own >= 0, own < PART_HEADS), level < LEVELS)
    target = jnp.where(ok, level * PART_HEADS + own, 999)
    lane = iota(shape, 1)
    packed = dot(gains[:64, :], ones_where(lane == target))
    return (packed + dot(gains[64:, :], ones_where(lane == target + 64))).astype(bf16)


def column_copies(masks, x_ref, x_buf, sems):
    copies = []
    for i, mask in enumerate(masks):
        cols = pl.ds(pl.multiple_of((spots()[2] ^ mask) * PART, 128), PART)
        copies.append(pltpu.make_async_copy(x_ref.at[:, cols], x_buf.at[i], sems.at[i]))
    return copies


def first_kernel(
    x_ref, b_ref, c_ref, decay_ref, step_ref, weight_ref,
    far_ref, cross_ref, beside_ref, within_ref, carry_ref, last_ref, bt_ref, gains_ref,
    x_buf, b_buf, c_buf, decay_buf, step_buf, weight_buf, sems,
):
    half = pl.ds(pl.multiple_of(spots()[3] * 64, 64), 64)
    copies = column_copies(FIRST, x_ref, x_buf, sems) + [
        pltpu.make_async_copy(decay_ref, decay_buf, sems.at[3]),
        pltpu.make_async_copy(step_ref, step_buf, sems.at[4]),
        pltpu.make_async_copy(b_ref, b_buf, sems.at[5]),
        pltpu.make_async_copy(weight_ref, weight_buf, sems.at[6]),
        pltpu.make_async_copy(c_ref.at[half, :], c_buf, sems.at[7]),
    ]
    for c in copies[3:] + copies[:3]:
        c.start()
    upper = ones_where(iota((128, 128), 0) <= iota((128, 128), 1))
    copies[3].wait()
    within = sum(dot(p, upper) for p in three(decay_buf[...]))
    within_ref[...] = within
    total = within[:, 127:128]
    copies[4].wait()
    carry = jnp.exp(total - within) * step_buf[...]
    pad = jnp.zeros((8, 128), f32)

    def stacked(v):
        return jnp.concatenate([p.astype(f32) for p in three(v)] + [pad], axis=0).T

    carry_t = stacked(carry).astype(bf16)
    last = stacked(within)[127:128, :]
    copies[5].wait()
    b_t = b_buf[...].astype(f32).T.astype(bf16)
    copies[6].wait()
    grown = jnp.exp(within)
    rows = [weight_buf[level] * grown for level in range(1, LEVELS + 1)]
    gains = jnp.concatenate(rows + [jnp.zeros((16, 128), f32)], axis=0).T.astype(bf16)
    carry_ref[...] = carry_t
    last_ref[...] = jnp.broadcast_to(last, (8, 128))
    bt_ref[...] = b_t
    gains_ref[...] = gains
    copies[7].wait()
    for c in copies[:3]:
        c.wait()
    for i, (mask, msg_ref) in enumerate(zip(FIRST, (far_ref, cross_ref, beside_ref))):
        part = spots()[2] ^ mask
        worker_message(part, x_buf[i], carry_t, last, b_t, gains, c_buf[...], msg_ref)


def second_kernel(
    x_ref, c_ref, carry_ref, last_ref, bt_ref, gains_ref, own_ref,
    x_buf, c_buf, sems,
):
    half = pl.ds(pl.multiple_of(spots()[3] * 64, 64), 64)
    copies = column_copies(SECOND, x_ref, x_buf, sems)
    copies.append(pltpu.make_async_copy(c_ref.at[half, :], c_buf, sems.at[1]))
    for c in copies:
        c.start()
    for c in copies:
        c.wait()
    for i, (mask, msg_ref) in enumerate(zip(SECOND, (own_ref,))):
        part = spots()[2] ^ mask
        worker_message(
            part, x_buf[i], carry_ref[...], last_ref[0:1, :], bt_ref[...], gains_ref[...], c_buf[...], msg_ref
        )


def local_kernel(
    x_hbm, b_hbm, c_hbm, step_hbm, weight_hbm, within_ref, out_ref,
    x_ref, b_ref, c_ref, step_ref, weight_ref, sems,
):
    pairs = ((x_hbm, x_ref), (b_hbm, b_ref), (c_hbm, c_ref), (step_hbm, step_ref), (weight_hbm.at[0], weight_ref))
    copies = [pltpu.make_async_copy(*p, sems.at[i]) for i, p in enumerate(pairs)]
    for c in copies:
        c.start()
    for c in copies:
        c.wait()
    scores = lax.dot_general(
        c_ref[...], b_ref[...], (((1,), (1,)), ((), ())), preferred_element_type=f32
    )
    scores = jnp.where(iota((128, 128), 0) >= iota((128, 128), 1), scores, 0.0)
    pad = jnp.zeros((128 - HEADS, 128), f32)
    within = within_ref[...]
    within_t = jnp.concatenate([within, pad], axis=0).T
    weight_t = jnp.concatenate([weight_ref[...], pad], axis=0).T
    step = step_ref[...]
    left = iota((128, 128), 1) < HEADDIM
    zero = jnp.zeros((128, 128), bf16)

    def mixing(h):
        gap = jnp.minimum(within_t[:, h : h + 1] - within[h : h + 1, :], 0.0)
        gain = weight_t[:, h : h + 1] * jnp.exp(gap)
        return (gain * scores * step[h : h + 1, :]).astype(bf16)

    for pair in range(HEADS // 2):
        cols = slice(pair * 128, (pair + 1) * 128)
        x = x_ref[:, cols]
        both = jnp.concatenate([mixing(2 * pair), mixing(2 * pair + 1)], axis=1)
        sides = jnp.concatenate([jnp.where(left, x, zero), jnp.where(left, zero, x)], axis=0)
        out_ref[:, cols] = dot(both, sides)


def total_of(meta, tile):
    return meta[3 * tile : 3 * tile + 1] + meta[3 * tile + 1 : 3 * tile + 2] + meta[3 * tile + 2 : 3 * tile + 3]


def put_total(meta, tile, total):
    row = iota((META, 128), 0)
    for k, p in enumerate(three(total)):
        meta = jnp.where(row == 3 * tile + k, p.astype(f32), meta)
    return meta


def tile_rows(tile):
    return slice(tile * STATE, (tile + 1) * STATE)


def group_kernel(*refs):
    got, (first_ref, second_ref, parts_ref, half_ref) = refs[:PLACES], refs[PLACES:]
    for mask, ref in zip(MASKS, got):
        parts_ref[spots()[2] ^ mask] = ref[:KEEP, :]
        half_ref[spots()[2] ^ mask] = ref[KEEP:, :]
    metas = [parts_ref[j, BODY:SIDE, :].astype(f32) for j in range(PLACES)]
    for tiles, out_ref in ((range(AHEAD), first_ref), (range(AHEAD, TILES), second_ref)):
        meta = jnp.zeros((META, 128), f32)
        for tile in tiles:
            rows = tile_rows(tile)
            t = [total_of(m, tile) for m in metas]
            acc = parts_ref[0, rows, :].astype(f32)
            for j in range(1, PLACES):
                acc = jnp.exp(t[j]) * acc + parts_ref[j, rows, :].astype(f32)
            out_ref[tile_rows(tile - tiles[0]), :] = acc.astype(bf16)
            meta = put_total(meta, tile - tiles[0], t[0] + t[1] + t[2] + t[3])
        out_ref[len(tiles) * STATE :, :] = meta.astype(bf16)


def flag(cond):
    return jnp.where(cond, 1.0, 0.0).astype(f32)


def joined(later, own, own_t, other, other_t):
    return jnp.exp(other_t * (1.0 - later)) * own + jnp.exp(own_t * later) * other


def pair_kernel(own_ref, other_ref, out_ref):
    later = flag(spots()[0] % 2 == 1)
    end = AHEAD * STATE
    own_meta, other_meta = own_ref[end:, :].astype(f32), other_ref[end:, :].astype(f32)
    meta = jnp.zeros((META, 128), f32)
    for tile in range(AHEAD):
        rows = tile_rows(tile)
        own_t, other_t = total_of(own_meta, tile), total_of(other_meta, tile)
        own, other = own_ref[rows, :].astype(f32), other_ref[rows, :].astype(f32)
        out_ref[rows, :] = joined(later, own, own_t, other, other_t).astype(bf16)
        meta = put_total(meta, tile, own_t + other_t)
    out_ref[end:, :] = meta.astype(bf16)


def both_kernel(own_ref, opposite_ref, out_ref):
    out_ref[0] = own_ref[...]
    out_ref[1] = opposite_ref[...]


def row_kernel(
    next_ref, pair_ref, far_ref, own_ref, opposite_ref, beside_ref, next_out, far_out, total_out
):
    odd, upper = flag(spots()[0] % 2 == 1), flag(spots()[0] >= 2)
    next_sum = jnp.zeros((META, 128), f32)
    far_sum, total_sum = next_sum, next_sum
    end, late = AHEAD * STATE, (TILES - AHEAD) * STATE
    next_meta, pair_meta, far_meta = (r[end:, :].astype(f32) for r in (next_ref, pair_ref, far_ref))
    own_meta, opposite_meta = own_ref[late:, :].astype(f32), opposite_ref[late:, :].astype(f32)
    beside_meta, last_meta = beside_ref[0, late:, :].astype(f32), beside_ref[1, late:, :].astype(f32)
    for tile in range(TILES):
        rows = tile_rows(tile)
        if tile < AHEAD:
            next_t, pair_t, far_t = (total_of(m, tile) for m in (next_meta, pair_meta, far_meta))
            next_out[rows, :] = next_ref[rows, :]
            far_out[rows, :] = far_ref[rows, :]
            pair, far = pair_ref[rows, :].astype(f32), far_ref[rows, :].astype(f32)
        else:
            spot = tile_rows(tile - AHEAD)
            own_t, next_t, opposite_t, last_t = (
                total_of(m, tile - AHEAD) for m in (own_meta, beside_meta, opposite_meta, last_meta)
            )
            own, opposite = own_ref[spot, :].astype(f32), opposite_ref[spot, :].astype(f32)
            beside, last = beside_ref[0, spot, :].astype(f32), beside_ref[1, spot, :].astype(f32)
            pair = joined(odd, own, own_t, beside, next_t)
            far = joined(1.0 - odd, opposite, opposite_t, last, last_t)
            pair_t, far_t = own_t + next_t, opposite_t + last_t
            next_out[rows, :] = beside_ref[0, spot, :]
            far_out[rows, :] = far.astype(bf16)
        total_out[rows, :] = joined(upper, pair, pair_t, far, far_t).astype(bf16)
        next_sum = put_total(next_sum, tile, next_t)
        far_sum = put_total(far_sum, tile, far_t)
        total_sum = put_total(total_sum, tile, pair_t + far_t)
    for out, meta in ((next_out, next_sum), (far_out, far_sum), (total_out, total_sum)):
        out[BODY:, :] = meta.astype(bf16)


def split(v):
    hi = v.astype(bf16)
    return jnp.concatenate([hi, (v - hi.astype(f32)).astype(bf16)], axis=0)


def wide(pieces):
    return pieces[0] if len(pieces) == 1 else jnp.concatenate(pieces, axis=1)


def gain_spread(tiles, level):
    slot = iota((128, 128), 0)
    side = jnp.where(iota((128, 128), 1) >= HEADDIM, 1, 0)
    return [
        wide([ones_where(slot == base + level * PART_HEADS + 2 * tile + side) for tile in tiles])
        for base in (0, 64)
    ]


def spread_gain(gains, spread):
    return jnp.concatenate([dot(gains, s) for s in spread], axis=0)


def block_lead(metas, place, tiles):
    return wide(
        [
            jnp.exp(sum(flag(place > j) * total_of(metas[j], tile) for j in range(PLACES - 1)))
            for tile in tiles
        ]
    )


def near_kernel(
    parts_ref, half_ref, other_ref, next_ref, pair_ref, out_ref, c_ref
):
    group = spots()[0]
    for place in range(PLACES):
        for core, ref in ((spots()[3], half_ref), (1 - spots()[3], other_ref)):
            c_ref[place, pl.ds(pl.multiple_of(core * 64, 64), 64), :] = ref[place]
    part_metas = [parts_ref[j, BODY:SIDE, :].astype(f32) for j in range(PLACES)]
    next_meta = next_ref[BODY:, :].astype(f32)
    odd, upper, third = flag(group % 2 == 1), flag(group >= 2), flag(group == 3)
    for start in range(0, TILES, 2):
        tiles = range(start, min(start + 2, TILES))
        low_b, mid_b, high_b, b3, b4, skip = [], [], [], [], [], []
        for tile in tiles:
            rows = tile_rows(tile)
            t = [total_of(m, tile) for m in part_metas]
            s0, s1 = parts_ref[0, rows, :], parts_ref[1, rows, :]
            low_b.append(s0)
            mid_b.append(split(jnp.exp(t[1]) * s0.astype(f32) + s1.astype(f32)))
            high_b.append(parts_ref[2, rows, :])
            skip.append(jnp.exp(t[2]))
            b3.append(split(odd * next_ref[rows, :].astype(f32)))
            w4 = upper * jnp.exp(third * total_of(next_meta, tile))
            b4.append(split(w4 * pair_ref[rows, :].astype(f32)))
        spread = [gain_spread(tiles, level) for level in range(4)]
        low_w, mid_w, high_w = wide(low_b), wide(mid_b), wide(high_b)
        b3_w, b4_w = wide(b3), wide(b4)
        lanes = slice(start * 128, (start + len(tiles)) * 128)
        for place in range(PLACES):
            c = c_ref[place]
            cc = jnp.concatenate([c, c], axis=1)
            gains = parts_ref[place, SIDE:, :]
            acc = spread_gain(gains, spread[2]) * dot(cc, b3_w)
            acc = acc + spread_gain(gains, spread[3]) * dot(cc, b4_w)
            if place:
                acc = acc * block_lead(part_metas, place, tiles)
            if place == 1:
                acc = acc + spread_gain(gains, spread[0]) * dot(c, low_w)
            if place == 3:
                acc = acc + spread_gain(gains, spread[0]) * dot(c, high_w)
            if place >= 2:
                term = spread_gain(gains, spread[1]) * dot(cc, mid_w)
                acc = acc + (term * wide(skip) if place == 3 else term)
            out_ref[place, :, lanes] = acc


def far_kernel(
    masks, parts_ref, c_ref, next_ref, pair_ref, r1_ref, r2_ref, r3_ref, near_ref, *out_refs
):
    group, row = spots()[:2]
    part_metas = [parts_ref[j, BODY:SIDE, :].astype(f32) for j in range(PLACES)]
    metas = [r[BODY:, :].astype(f32) for r in (next_ref, pair_ref)]
    odd_group, upper_group = flag(group % 2 == 1), flag(group >= 2)
    row_metas = [r[BODY:, :].astype(f32) for r in (r1_ref, r2_ref)]
    odd, upper = flag(row % 2 == 1), flag(row >= 2)
    second, third = flag(row == 2), flag(row == 3)
    for start in range(0, TILES, 2):
        tiles = range(start, min(start + 2, TILES))
        b5, b6 = [], []
        for tile in tiles:
            rows = tile_rows(tile)
            t = [total_of(m, tile) for m in metas]
            t1, t2 = (total_of(m, tile) for m in row_metas)
            lead = jnp.exp(odd_group * t[0] + upper_group * t[1])
            v1, v2, v3 = (r[rows, :].astype(f32) for r in (r1_ref, r2_ref, r3_ref))
            b5.append(split((lead * odd) * v1))
            w2, w3 = lead * upper * jnp.exp(t1), lead * third * jnp.exp(t1 + t2)
            b6.append(split((lead * second) * v1 + w2 * v2 + w3 * v3))
        spread = [gain_spread(tiles, level) for level in (4, 5)]
        b5_w, b6_w = wide(b5), wide(b6)
        lanes = slice(start * 128, (start + len(tiles)) * 128)
        for mask, out_ref in zip(masks, out_refs):
            place = spots()[2] ^ mask
            c = c_ref[place]
            cc = jnp.concatenate([c, c], axis=1)
            gains = parts_ref[place, SIDE:, :]
            acc = spread_gain(gains, spread[0]) * dot(cc, b5_w)
            acc = acc + spread_gain(gains, spread[1]) * dot(cc, b6_w)
            acc = acc * block_lead(part_metas, place, tiles) + near_ref[place, :, lanes]
            out_ref[:, lanes] = acc.astype(bf16)


def gate_kernel(local_ref, gate_ref, *refs):
    reached, (gated_ref, square_ref) = refs[:PLACES], refs[PLACES:]
    acc = jnp.zeros((128, 128), f32)
    for mask, reached_ref in zip(MASKS, reached):
        start = (spots()[2] ^ mask) * PART
        for tile in range(TILES):
            cols = pl.ds(pl.multiple_of(start + tile * 128, 128), 128)
            mixed = local_ref[:, cols] + reached_ref[:, tile * 128 : (tile + 1) * 128].astype(f32)
            gate = gate_ref[:, cols].astype(f32)
            gated = (mixed * (gate / (1.0 + jnp.exp(-gate)))).astype(bf16)
            gated_ref[:, cols] = gated
            full = gated.astype(f32)
            acc = acc + full * full
    square_ref[...] = acc


def norm_kernel(gated_ref, own_ref, other_ref, weight_ref, out_ref):
    mean = jnp.sum(own_ref[...] + other_ref[...], axis=1, keepdims=True) / (2.0 * COLS)
    inverse = jnp.broadcast_to(lax.rsqrt(mean + 1e-05), (128, 128))
    for pair in range(HEADS // 2):
        cols = slice(pair * 128, (pair + 1) * 128)
        out_ref[:, cols] = (
            gated_ref[:, cols].astype(f32) * inverse * weight_ref[:, cols]
        ).astype(bf16)


def call(kernel, name, outs, *args, far=0, scratch=(), flops=10**8, size=4 * 10**6, vmem=VMEM):
    whole = pl.BlockSpec(memory_space=pltpu.VMEM)
    specs = [pl.BlockSpec(memory_space=pltpu.HBM)] * far + [whole] * (len(args) - far)
    return pl.pallas_call(
        kernel,
        name=name,
        in_specs=specs,
        out_specs=[whole] * len(outs),
        out_shape=[jax.ShapeDtypeStruct(*o) for o in outs],
        scratch_shapes=list(scratch),
        cost_estimate=pl.CostEstimate(flops=flops, bytes_accessed=size, transcendentals=0),
        compiler_params=pltpu.CompilerParams(vmem_limit_bytes=vmem),
    )(*args)


def spot_of(index):
    return index // 16, index // 4 % 4, index % 4


def index_of(row, group, place):
    return row * 16 + group * 4 + place


def to_group(value, partner):
    pairs = []
    for index in range(ROWS * GROUPS * PLACES):
        row, group, place = spot_of(index)
        pairs.append((index, index_of(row, partner(group), place)))
    return lax.ppermute(value, "ctx", pairs)


def to_row(value, shift):
    pairs = []
    for index in range(ROWS * GROUPS * PLACES):
        row, group, place = spot_of(index)
        if row + shift < ROWS:
            pairs.append((index, index_of(row + shift, group, place)))
    return lax.ppermute(value, "ctx", pairs)


def to_place(value, mask):
    if not mask:
        return value
    return lax.ppermute(value, "ctx", [(i, i ^ mask) for i in range(ROWS * GROUPS * PLACES)])


def on_device(
    mixer_input,
    gate_input,
    input_proj,
    output_proj,
    step_size,
    decay_log,
    level_weight,
    norm_weight,
):
    message = ((MSG, 128), bf16)
    far, cross, beside, within, carry_t, last, b_t, gains = call(
        first_kernel,
        "first_states",
        [
            message,
            message,
            message,
            ((HEADS, 128), f32),
            ((128, 128), bf16),
            ((8, 128), f32),
            ((128, 128), bf16),
            ((128, 256), bf16),
        ],
        mixer_input,
        input_proj,
        output_proj,
        decay_log,
        step_size,
        level_weight,
        far=6,
        vmem=60 * 2**20,
        scratch=[
            pltpu.VMEM((len(FIRST), 128, PART), bf16),
            pltpu.VMEM((128, 128), bf16),
            pltpu.VMEM((64, 128), bf16),
            pltpu.VMEM((HEADS, 128), f32),
            pltpu.VMEM((HEADS, 128), f32),
            pltpu.VMEM((LEVELS + 1, HEADS, 128), f32),
            pltpu.SemaphoreType.DMA((8,)),
        ],
    )
    (own,) = call(
        second_kernel,
        "second_states",
        [message],
        mixer_input,
        output_proj,
        carry_t,
        last,
        b_t,
        gains,
        far=2,
        flops=4 * 10**10,
        scratch=[
            pltpu.VMEM((len(SECOND), 128, PART), bf16),
            pltpu.VMEM((64, 128), bf16),
            pltpu.SemaphoreType.DMA((2,)),
        ],
    )
    (local,) = call(
        local_kernel,
        "local_part",
        [((128, COLS), f32)],
        mixer_input,
        input_proj,
        output_proj,
        step_size,
        level_weight,
        within,
        far=5,
        scratch=[
            pltpu.VMEM((128, COLS), bf16),
            pltpu.VMEM((128, 128), bf16),
            pltpu.VMEM((128, 128), bf16),
            pltpu.VMEM((HEADS, 128), f32),
            pltpu.VMEM((HEADS, 128), f32),
            pltpu.SemaphoreType.DMA((5,)),
        ],
        flops=10**10,
        size=10**7,
    )
    got = [to_place(v, mask) for mask, v in zip(MASKS, (far, cross, beside, own))]
    ahead = ((AHEAD * STATE + META, 128), bf16)
    behind = (((TILES - AHEAD) * STATE + META, 128), bf16)
    whole = ((BODY + META, 128), bf16)
    sums, late_sums, parts, halves = call(
        group_kernel,
        "group_state",
        [ahead, behind, ((PLACES, KEEP, 128), bf16), ((PLACES, 64, 128), bf16)],
        *got,
    )
    beside = to_group(sums, lambda g: g ^ 1)
    opposite = to_group(late_sums, lambda g: 3 - g)
    (pair,) = call(pair_kernel, "pair_state", [ahead], sums, beside)
    (both,) = call(
        both_kernel, "two_states", [((2,) + behind[0], bf16)], late_sums, opposite
    )
    late_beside = to_group(both, lambda g: g ^ 1)
    other_pair = to_group(pair, lambda g: 3 - g)
    halves_now, _ = lax.optimization_barrier((halves, pair))
    others = lax.ppermute(halves_now, "head", [(0, 1), (1, 0)])
    neighbour, other_pair, total = call(
        row_kernel,
        "row_state",
        [whole, whole, whole],
        beside,
        pair,
        other_pair,
        late_sums,
        opposite,
        late_beside,
    )
    rows = [to_row(total, k) for k in (1, 2, 3)]
    near, c_all = call(
        near_kernel,
        "near_levels",
        [((PLACES, 128, PART), f32), ((PLACES, 128, 128), bf16)],
        parts,
        halves,
        others,
        neighbour,
        other_pair,
        flops=10**10,
    )
    reached = []
    for masks in (FIRST, SECOND):
        reached += call(
            functools.partial(far_kernel, masks),
            "far_levels",
            [((128, PART), bf16)] * len(masks),
                parts,
            c_all,
            neighbour,
            other_pair,
            *rows,
            near,
                flops=10**10,
        )
    back = [to_place(v, mask) for mask, v in zip(MASKS, reached)]
    gated, square = call(
        gate_kernel,
        "gate",
        [((128, COLS), bf16), ((128, 128), f32)],
        local,
        gate_input,
        *back,
    )
    other = lax.ppermute(square, "head", [(0, 1), (1, 0)])
    (out,) = call(
        norm_kernel,
        "norm",
        [((128, COLS), bf16)],
        gated,
        square,
        other,
        norm_weight.reshape(1, COLS),
    )
    return out


def solution(mesh):
    in_specs = (
        P(("seq", "ctx"), "head"),
        P(("seq", "ctx"), "head"),
        P(("seq", "ctx"), None),
        P(("seq", "ctx"), None),
        P("head", ("seq", "ctx")),
        P("head", ("seq", "ctx")),
        P(None, "head", ("seq", "ctx")),
        P("head"),
    )
    out_specs = P(("seq", "ctx"), "head")
    return jax.shard_map(
        on_device, mesh=mesh, in_specs=in_specs, out_specs=out_specs, check_vma=False
    )
```

time: 119 us -> 108 us (0.908)
  blocking collectives: 28 us -> 0 us
  starting transfers between devices: 39.5 us -> 62.1 us
  waiting for transfers between devices: 37.7 us -> 29 us
  local copies, waits for them, and re-layouts: 0.06 us -> 4.92 us
  Pallas kernels: 13 us -> 10.7 us
    all_to_all x1 -> x0, blocking collectives: 28 us -> none  [exchange(): return lax.all_to_all(value, 'ctx', 0, 0, axis_index_groups=lines)]
    ppermute x0 -> x7, starting transfers between devices: none -> 22.7 us  [the longest x6 19.7 us: to_place(): lax.ppermute(value, 'ctx', [(i, i ^ mask) for i in range(ROWS * GROUPS *...]
    ppermute x0 -> x7, waiting for transfers between devices: none -> 16.9 us  [the longest x6 16.9 us: to_place(): lax.ppermute(value, 'ctx', [(i, i ^ mask) for i in range(ROWS * GROUPS *...]
    all_to_all x1 -> x0, waiting for transfers between devices: 13.8 us -> none  [exchange(): return lax.all_to_all(value, 'ctx', 0, 0, axis_index_groups=lines)]
    ppermute x4, waiting for transfers between devices: 20.8 us -> 8.97 us  [to_group(): return lax.ppermute(value, 'ctx', pairs)]
    ppermute x4, starting transfers between devices: 22.7 us -> 28.2 us  [to_group(): return lax.ppermute(value, 'ctx', pairs)]
    unnamed x16 -> x26, local copies, waits for them, and re-layouts: 0.04 us -> 4.91 us
    all_to_all x1 -> x0, starting transfers between devices: 3.63 us -> none  [exchange(): return lax.all_to_all(value, 'ctx', 0, 0, axis_index_groups=lines)]
  transfers between devices with their start and end apart: 9 -> 15, of which waited for: 5 -> 9; matrix products, arithmetic and copies ran while one was open for 0% -> 0% of each run, Pallas kernels for 3% -> 4%
where the time goes in v3:
time: 108 us; the launch traced here: 107 us
  starting transfers between devices  62.1 us (58%)
  waiting for transfers between devices  29 us (27%)
  Pallas kernels  10.7 us (10%)
  local copies, waits for them, and re-layouts  4.92 us (5%)
    ppermute x4, starting transfers between devices, to_group(): return lax.ppermute(value, 'ctx', pairs)  28.2 us
    ppermute x6, starting transfers between devices, to_place(): lax.ppermute(value, 'ctx', [(i, i ^ mask) for i in range(ROWS * GROUPS *...  19.7 us
    ppermute x6, waiting for transfers between devices, to_place(): lax.ppermute(value, 'ctx', [(i, i ^ mask) for i in range(ROWS * GROUPS *...  16.9 us
    pallas_call x12, Pallas kernels, call(): pl.pallas_call(kernel, name=name, in_specs=specs, out_specs=[whole] * len...  10.7 us
    ppermute x4, waiting for transfers between devices, to_group(): return lax.ppermute(value, 'ctx', pairs)  8.97 us
    ppermute x3, starting transfers between devices, to_row(): return lax.ppermute(value, 'ctx', pairs)  8.77 us
    unnamed x26, local copies, waits for them, and re-layouts  4.91 us
    ppermute x1, starting transfers between devices, on_device(): others = lax.ppermute(halves_now, 'head', [(0, 1), (1, 0)])  3.02 us
  transfers between devices with their start and end apart: 15, of which 9 were waited for; matrix products, arithmetic and copies ran while one was open for 0% of the time, Pallas kernels for 4%

profile of v3, /device:TPU:1, one launch (start us, length us, event | category | flops | bytes accessed | tf_op | source)
XLA Modules:
  0.0 106.9 jit_solution(13991829427884251377)
XLA Ops:
  0.0 3.1 %first_states.1 = (bf16[784,128]{1,0:T(8,128)(2,1)}, bf16[784,128]{1,0:T(8,128)(2,1)}, bf16[784,128]{1,0:T(8,128)(2,1)}, f32[40,128]{1,0:T(8,128)}, bf16[128,128...) custom-call(bf16[128,2560]{1,0:T(8,128)(2,1)} %x_ref.3, ...), custom_call_target="tpu_custom_call" | custom-call | flops 100000000 | bytes 4000000 | tf_op jit(solution)/shard_map/first_states/pallas_call | solution.py:445
  3.1 5.7 %collective-permute-start = (bf16[784,128]{1,0:T(8,128)(2,1)}, bf16[784,128]{1,0:T(8,128)(2,1)S(1)}, u32[]{:S(2)}, u32[]{:S(2)}) collective-permute-start(bf16[784,128]{1,0:T(8,128)(2,1)} %get-tuple-element.29), channel_id=1, source_target_pairs={{0,16},{8,24},{16,0},{24,8},{32,48},{40,56},{48,32},{56,40},{64,80... | collective-permute-start | bytes 602120 | tf_op jit(solution)/shard_map/ppermute | solution.py:485
  8.9 3.3 %collective-permute-start.1 = (bf16[784,128]{1,0:T(8,128)(2,1)}, bf16[784,128]{1,0:T(8,128)(2,1)S(1)}, u32[]{:S(2)}, u32[]{:S(2)}) collective-permute-start(bf16[784,128]{1,0:T(8,128)(2,1)} %get-tuple-element.30), channel_id=1, source_target_pairs={{0,24},{8,16},{16,8},{24,0},{32,56},{40,48},{48,40},{56,32},{64,88... | collective-permute-start | bytes 602120 | tf_op jit(solution)/shard_map/ppermute | solution.py:485
  12.1 2.2 %collective-permute-start.2 = (bf16[784,128]{1,0:T(8,128)(2,1)}, bf16[784,128]{1,0:T(8,128)(2,1)S(1)}, u32[]{:S(2)}, u32[]{:S(2)}) collective-permute-start(bf16[784,128]{1,0:T(8,128)(2,1)} %get-tuple-element.31), channel_id=1, source_target_pairs={{0,8},{8,0},{16,24},{24,16},{32,40},{40,32},{48,56},{56,48},{64,72... | collective-permute-start | bytes 602120 | tf_op jit(solution)/shard_map/ppermute | solution.py:485
  14.3 0.0 copy-start.1
  14.4 1.1 %copy-done.1 = bf16[128,2560]{1,0:T(8,128)(2,1)S(1)} copy-done((bf16[128,2560]{1,0:T(8,128)(2,1)S(1)}, bf16[128,2560]{1,0:T(8,128)(2,1)}, u32[]{:S(2)}) %copy-start.1) | copy-done | bytes 655384
  15.4 0.8 copy-done.5
  16.2 0.8 copy-done.7
  17.0 0.8 copy-done.8
  17.8 0.8 copy-done.9
  18.5 0.7 copy-done.11
  19.2 0.5 second_states.1.refs_3_
  19.7 0.0 copy-start.2
  19.7 0.0 copy-start.3
  19.7 0.0 copy-start.4
  19.8 0.0 copy-start.6
  19.8 0.3 collective-permute-done.refs_0_
  20.1 7.3 %collective-permute-done.2.refs_2_ = bf16[784,128]{1,0:T(8,128)(2,1)S(1)} collective-permute-done((bf16[784,128]{1,0:T(8,128)(2,1)}, bf16[784,128]{1,0:T(8,128)(2,1)S(1)}, u32[]{:S(2)}, u32[]{:S(2)}) %collective-permute-start.2) | collective-permute-done | bytes 200736 | tf_op jit(solution)/shard_map/ppermute | solution.py:485
  27.3 0.2 group_state.1
  27.6 8.9 %collective-permute-start.3 = (bf16[400,128]{1,0:T(8,128)(2,1)S(1)}, bf16[400,128]{1,0:T(8,128)(2,1)S(1)}, u32[]{:S(2)}, u32[]{:S(2)}) collective-permute-start(bf16[400,128]{1,0:T(8,128)(2,1)S(1)} %get-tuple-element.38.own_ref), channel_id=1, source_target_pairs={{0,32},{8,40},{16,48},{24,56},{32,0},{40,8},{48,16},{56,24},{64,96... | collective-permute-start | bytes 307208 | tf_op jit(solution)/shard_map/ppermute | solution.py:470
  36.5 8.2 %collective-permute-start.6 = (bf16[272,128]{1,0:T(8,128)(2,1)S(1)}, bf16[272,128]{1,0:T(8,128)(2,1)S(1)}, u32[]{:S(2)}, u32[]{:S(2)}) collective-permute-start(bf16[272,128]{1,0:T(8,128)(2,1)S(1)} %get-tuple-element.40.own_ref), channel_id=1, source_target_pairs={{0,96},{8,104},{16,112},{24,120},{32,64},{40,72},{48,80},{56,88},{... | collective-permute-start | bytes 208904 | tf_op jit(solution)/shard_map/ppermute | solution.py:470
  44.6 5.9 %collective-permute-done.6.opposite_ref = bf16[272,128]{1,0:T(8,128)(2,1)S(1)} collective-permute-done((bf16[272,128]{1,0:T(8,128)(2,1)S(1)}, bf16[272,128]{1,0:T(8,128)(2,1)S(1)}, u32[]{:S(2)}, u32[]{:S(2)}) %collective-permute-start.6) | collective-permute-done | bytes 69664 | tf_op jit(solution)/shard_map/ppermute | solution.py:470
  50.5 4.8 %collective-permute-start.7 = (bf16[2,272,128]{2,1,0:T(8,128)(2,1)S(1)}, bf16[2,272,128]{2,1,0:T(8,128)(2,1)S(1)}, u32[]{:S(2)}, u32[]{:S(2)}) collective-permute-start(bf16[2,272,128]{2,1,0:T(8,128)(2,1)S(1)} %two_states.1), channel_id=1, source_target_pairs={{0,32},{8,40},{16,48},{24,56},{32,0},{40,8},{48,16},{56,24},{64,96... | collective-permute-start | bytes 417800 | tf_op jit(solution)/shard_map/ppermute | solution.py:470
  55.4 0.1 pair_state.1.pair_ref
  55.4 6.3 %collective-permute-start.5 = (bf16[400,128]{1,0:T(8,128)(2,1)S(1)}, bf16[400,128]{1,0:T(8,128)(2,1)S(1)}, u32[]{:S(2)}, u32[]{:S(2)}) collective-permute-start(bf16[400,128]{1,0:T(8,128)(2,1)S(1)} %pair_state.1.pair_ref), channel_id=1, source_target_pairs={{0,96},{8,104},{16,112},{24,120},{32,64},{40,72},{48,80},{56,88},{... | collective-permute-start | bytes 307208 | tf_op jit(solution)/shard_map/ppermute | solution.py:470
  61.7 3.0 %collective-permute-start.4 = (bf16[4,64,128]{2,1,0:T(8,128)(2,1)S(1)}, bf16[4,64,128]{2,1,0:T(8,128)(2,1)S(1)}, u32[]{:S(2)}, u32[]{:S(2)}) collective-permute-start(bf16[4,64,128]{2,1,0:T(8,128)(2,1)S(1)} %get-tuple-element.39.half_ref), channel_id=1, source_target_pairs={{0,4},{4,0},{1,5},{5,1},{2,6},{6,2},{3,7},{7,3},{8,12},{12,8},{9,1... | collective-permute-start | bytes 196616 | tf_op jit(solution)/shard_map/ppermute | solution.py:589
  64.8 2.2 %local_part.1.local_ref = f32[128,2560]{1,0:T(8,128)S(1)} custom-call(bf16[128,2560]{1,0:T(8,128)(2,1)S(1)} %copy-done.2, bf16[128,128]{1,0:T(8,128)(2,1)S(1)} %copy-done.4, bf16[128,128]{1,0:T(8,128)(2,1)S(1)} %copy-done.5, f32[40,128]{1,0:T(8,128)S(1)} %copy-done.6, f32[7,40,128]{2,1,0:T(8,128)S(1)} %copy-done.3, f32[40,128]{1,0:T(8,128)S(1)} %copy-done.10), custom_call_target="tpu_custom_call" | custom-call | flops 10000000000 | bytes 10000000 | tf_op jit(solution)/shard_map/local_part/pallas_call | solution.py:445
  67.0 1.7 %collective-permute-done.5.far_ref = bf16[400,128]{1,0:T(8,128)(2,1)S(1)} collective-permute-done((bf16[400,128]{1,0:T(8,128)(2,1)S(1)}, bf16[400,128]{1,0:T(8,128)(2,1)S(1)}, u32[]{:S(2)}, u32[]{:S(2)}) %collective-permute-start.5) | collective-permute-done | bytes 102432 | tf_op jit(solution)/shard_map/ppermute | solution.py:470
  68.7 1.4 %collective-permute-done.7.beside_ref = bf16[2,272,128]{2,1,0:T(8,128)(2,1)S(1)} collective-permute-done((bf16[2,272,128]{2,1,0:T(8,128)(2,1)S(1)}, bf16[2,272,128]{2,1,0:T(8,128)(2,1)S(1)}, u32[]{:S(2)}, u32[]{:S(2)}) %collective-permute-start.7) | collective-permute-done | bytes 139296 | tf_op jit(solution)/shard_map/ppermute | solution.py:470
  70.1 0.2 row_state.1
  70.3 4.4 %collective-permute-start.10 = (bf16[656,128]{1,0:T(8,128)(2,1)S(1)}, bf16[656,128]{1,0:T(8,128)(2,1)S(1)}, u32[]{:S(2)}, u32[]{:S(2)}) collective-permute-start(bf16[656,128]{1,0:T(8,128)(2,1)S(1)} %get-tuple-element.44), channel_id=1, source_target_pairs={{0,384},{8,392},{16,400},{24,408},{32,416},{40,424},{48,432},{56,4... | collective-permute-start | bytes 503816 | tf_op jit(solution)/shard_map/ppermute | solution.py:479
  74.7 1.3 %collective-permute-start.8 = (bf16[656,128]{1,0:T(8,128)(2,1)S(1)}, bf16[656,128]{1,0:T(8,128)(2,1)S(1)}, u32[]{:S(2)}, u32[]{:S(2)}) collective-permute-start(bf16[656,128]{1,0:T(8,128)(2,1)S(1)} %get-tuple-element.44), channel_id=1, source_target_pairs={{0,128},{8,136},{16,144},{24,152},{32,160},{40,168},{48,176},{56,1... | collective-permute-start | bytes 503816 | tf_op jit(solution)/shard_map/ppermute | solution.py:479
  76.0 3.1 %collective-permute-start.9 = (bf16[656,128]{1,0:T(8,128)(2,1)S(1)}, bf16[656,128]{1,0:T(8,128)(2,1)S(1)}, u32[]{:S(2)}, u32[]{:S(2)}) collective-permute-start(bf16[656,128]{1,0:T(8,128)(2,1)S(1)} %get-tuple-element.44), channel_id=1, source_target_pairs={{0,256},{8,264},{16,272},{24,280},{32,288},{40,296},{48,304},{56,3... | collective-permute-start | bytes 503816 | tf_op jit(solution)/shard_map/ppermute | solution.py:479
  79.1 1.4 %near_levels.1 = (f32[4,128,640]{2,1,0:T(8,128)S(1)}, bf16[4,128,128]{2,1,0:T(8,128)(2,1)S(1)}) custom-call(bf16[4,720,128]{2,1,0:T(8,128)(2,1)S(1)} %get-tuple-element.36.parts_ref, bf16[4,64,128]{2,1,0:T(8,128)(2,1)S(1)} %get-tuple-element.39.half_ref, bf16[4,64,128]{2,1,0:T(8,128)(2,1)S(1)} %collective-permute-done.4.other_ref, ...), custom_call_target="tpu_custom_call" | custom-call | flops 10000000000 | bytes 4000000 | tf_op jit(solution)/shard_map/near_levels/pallas_call | solution.py:445
  80.5 2.3 %collective-permute-done.9.r2_ref = bf16[656,128]{1,0:T(8,128)(2,1)S(1)} collective-permute-done((bf16[656,128]{1,0:T(8,128)(2,1)S(1)}, bf16[656,128]{1,0:T(8,128)(2,1)S(1)}, u32[]{:S(2)}, u32[]{:S(2)}) %collective-permute-start.9) | collective-permute-done | bytes 167968 | tf_op jit(solution)/shard_map/ppermute | solution.py:479
  82.7 0.9 far_levels.2
  83.6 1.9 %collective-permute-start.11 = (bf16[128,640]{1,0:T(8,128)(2,1)S(1)}, bf16[128,640]{1,0:T(8,128)(2,1)S(1)}, u32[]{:S(2)}, u32[]{:S(2)}) collective-permute-start(bf16[128,640]{1,0:T(8,128)(2,1)S(1)} %get-tuple-element.46), channel_id=1, source_target_pairs={{0,16},{8,24},{16,0},{24,8},{32,48},{40,56},{48,32},{56,40},{64,80... | collective-permute-start | bytes 491528 | tf_op jit(solution)/shard_map/ppermute | solution.py:485
  85.5 3.1 %collective-permute-start.12 = (bf16[128,640]{1,0:T(8,128)(2,1)S(1)}, bf16[128,640]{1,0:T(8,128)(2,1)S(1)}, u32[]{:S(2)}, u32[]{:S(2)}) collective-permute-start(bf16[128,640]{1,0:T(8,128)(2,1)S(1)} %get-tuple-element.47), channel_id=1, source_target_pairs={{0,24},{8,16},{16,8},{24,0},{32,56},{40,48},{48,40},{56,32},{64,88... | collective-permute-start | bytes 491528 | tf_op jit(solution)/shard_map/ppermute | solution.py:485
  88.7 0.0 copy-start
  88.7 3.4 %collective-permute-start.13 = (bf16[128,640]{1,0:T(8,128)(2,1)S(1)}, bf16[128,640]{1,0:T(8,128)(2,1)S(1)}, u32[]{:S(2)}, u32[]{:S(2)}) collective-permute-start(bf16[128,640]{1,0:T(8,128)(2,1)S(1)} %get-tuple-element.48), channel_id=1, source_target_pairs={{0,8},{8,0},{16,24},{24,16},{32,40},{40,32},{48,56},{56,48},{64,72... | collective-permute-start | bytes 491528 | tf_op jit(solution)/shard_map/ppermute | solution.py:485
  92.1 0.4 far_levels.3.refs_3_
  92.6 0.0 copy-start.12
  92.6 4.9 %collective-permute-done.11.refs_0_ = bf16[128,640]{1,0:T(8,128)(2,1)S(1)} collective-permute-done((bf16[128,640]{1,0:T(8,128)(2,1)S(1)}, bf16[128,640]{1,0:T(8,128)(2,1)S(1)}, u32[]{:S(2)}, u32[]{:S(2)}) %collective-permute-start.11) | collective-permute-done | bytes 163872 | tf_op jit(solution)/shard_map/ppermute | solution.py:485
  97.5 4.4 %collective-permute-done.13.refs_2_ = bf16[128,640]{1,0:T(8,128)(2,1)S(1)} collective-permute-done((bf16[128,640]{1,0:T(8,128)(2,1)S(1)}, bf16[128,640]{1,0:T(8,128)(2,1)S(1)}, u32[]{:S(2)}, u32[]{:S(2)}) %collective-permute-start.13) | collective-permute-done | bytes 163872 | tf_op jit(solution)/shard_map/ppermute | solution.py:485
  101.9 0.6 gate.1
  102.6 2.4 %collective-permute-start.14 = (f32[128,128]{1,0:T(8,128)S(1)}, f32[128,128]{1,0:T(8,128)S(1)}, u32[]{:S(2)}, u32[]{:S(2)}) collective-permute-start(f32[128,128]{1,0:T(8,128)S(1)} %get-tuple-element.50.own_ref), channel_id=1, source_target_pairs={{0,4},{4,0},{1,5},{5,1},{2,6},{6,2},{3,7},{7,3},{8,12},{12,8},{9,1... | collective-permute-start | bytes 196616 | tf_op jit(solution)/shard_map/ppermute | solution.py:636
  105.0 0.9 collective-permute-done.14.other_ref
  105.8 1.1 %norm.1 = bf16[128,2560]{1,0:T(8,128)(2,1)} custom-call(bf16[128,2560]{1,0:T(8,128)(2,1)S(1)} %get-tuple-element.49.gated_ref, f32[128,128]{1,0:T(8,128)S(1)} %get-tuple-element.50.own_ref, f32[128,128]{1,0:T(8,128)S(1)} %collective-permute-done.14.other_ref, f32[1,2560]{1,0:T(1,128)S(1)} %reshape.3.weight_ref), custom_call_target="tpu_custom_call" | custom-call | flops 100000000 | bytes 4000000 | tf_op jit(solution)/shard_map/norm/pallas_call | solution.py:445
  (21 shorter events, 0.1 us)
Async XLA Ops:
  3.1 17.0 %collective-permute-start = (bf16[784,128]{1,0:T(8,128)(2,1)}, bf16[784,128]{1,0:T(8,128)(2,1)S(1)}, u32[]{:S(2)}, u32[]{:S(2)}) collective-permute-start(bf16[784,128]{1,0:T(8,128)(2,1)} %get-tuple-element.29), channel_id=1, source_target_pairs={{0,16},{8,24},{16,0},{24,8},{32,48},{40,56},{48,32},{56,40},{64,80... | collective-permute-start | bytes 602120 | tf_op jit(solution)/shard_map/ppermute | solution.py:485
  8.9 11.2 %collective-permute-start.1 = (bf16[784,128]{1,0:T(8,128)(2,1)}, bf16[784,128]{1,0:T(8,128)(2,1)S(1)}, u32[]{:S(2)}, u32[]{:S(2)}) collective-permute-start(bf16[784,128]{1,0:T(8,128)(2,1)} %get-tuple-element.30), channel_id=1, source_target_pairs={{0,24},{8,16},{16,8},{24,0},{32,56},{40,48},{48,40},{56,32},{64,88... | collective-permute-start | bytes 602120 | tf_op jit(solution)/shard_map/ppermute | solution.py:485
  12.1 15.2 %collective-permute-start.2 = (bf16[784,128]{1,0:T(8,128)(2,1)}, bf16[784,128]{1,0:T(8,128)(2,1)S(1)}, u32[]{:S(2)}, u32[]{:S(2)}) collective-permute-start(bf16[784,128]{1,0:T(8,128)(2,1)} %get-tuple-element.31), channel_id=1, source_target_pairs={{0,8},{8,0},{16,24},{24,16},{32,40},{40,32},{48,56},{56,48},{64,72... | collective-permute-start | bytes 602120 | tf_op jit(solution)/shard_map/ppermute | solution.py:485
  14.3 1.1 %copy-start.1 = (bf16[128,2560]{1,0:T(8,128)(2,1)S(1)}, bf16[128,2560]{1,0:T(8,128)(2,1)}, u32[]{:S(2)}) copy-start(bf16[128,2560]{1,0:T(8,128)(2,1)} %x_ref.3) | copy-start | bytes 1966084
  15.4 0.8 copy-start.5
  16.2 0.8 copy-start.7
  17.0 0.8 copy-start.8
  17.8 0.8 copy-start.9
  18.5 0.7 copy-start.11
  19.7 45.0 %copy-start.2 = (bf16[128,2560]{1,0:T(8,128)(2,1)S(1)}, bf16[128,2560]{1,0:T(8,128)(2,1)}, u32[]{:S(2)}) copy-start(bf16[128,2560]{1,0:T(8,128)(2,1)} %x_ref.3) | copy-start | bytes 1966084
  19.7 45.0 %copy-start.3 = (f32[7,40,128]{2,1,0:T(8,128)S(1)}, f32[7,40,128]{2,1,0:T(8,128)}, u32[]{:S(2)}) copy-start(f32[7,40,128]{2,1,0:T(8,128)} %weight_hbm.1) | copy-start | bytes 430084
  19.7 45.0 %copy-start.4 = (bf16[128,128]{1,0:T(8,128)(2,1)S(1)}, bf16[128,128]{1,0:T(8,128)(2,1)}, u32[]{:S(2)}) copy-start(bf16[128,128]{1,0:T(8,128)(2,1)} %b_hbm.1) | copy-start | bytes 98308
  19.8 45.0 %copy-start.6 = (f32[40,128]{1,0:T(8,128)S(1)}, f32[40,128]{1,0:T(8,128)}, u32[]{:S(2)}) copy-start(f32[40,128]{1,0:T(8,128)} %step_hbm.1) | copy-start | bytes 61444
  19.8 45.0 %copy-start.10 = (f32[40,128]{1,0:T(8,128)S(1)}, f32[40,128]{1,0:T(8,128)}, u32[]{:S(2)}) copy-start(f32[40,128]{1,0:T(8,128)} %get-tuple-element.28.within_ref) | copy-start | bytes 61444
  27.6 27.8 %collective-permute-start.3 = (bf16[400,128]{1,0:T(8,128)(2,1)S(1)}, bf16[400,128]{1,0:T(8,128)(2,1)S(1)}, u32[]{:S(2)}, u32[]{:S(2)}) collective-permute-start(bf16[400,128]{1,0:T(8,128)(2,1)S(1)} %get-tuple-element.38.own_ref), channel_id=1, source_target_pairs={{0,32},{8,40},{16,48},{24,56},{32,0},{40,8},{48,16},{56,24},{64,96... | collective-permute-start | bytes 307208 | tf_op jit(solution)/shard_map/ppermute | solution.py:470
  36.5 14.0 %collective-permute-start.6 = (bf16[272,128]{1,0:T(8,128)(2,1)S(1)}, bf16[272,128]{1,0:T(8,128)(2,1)S(1)}, u32[]{:S(2)}, u32[]{:S(2)}) collective-permute-start(bf16[272,128]{1,0:T(8,128)(2,1)S(1)} %get-tuple-element.40.own_ref), channel_id=1, source_target_pairs={{0,96},{8,104},{16,112},{24,120},{32,64},{40,72},{48,80},{56,88},{... | collective-permute-start | bytes 208904 | tf_op jit(solution)/shard_map/ppermute | solution.py:470
  50.5 19.6 %collective-permute-start.7 = (bf16[2,272,128]{2,1,0:T(8,128)(2,1)S(1)}, bf16[2,272,128]{2,1,0:T(8,128)(2,1)S(1)}, u32[]{:S(2)}, u32[]{:S(2)}) collective-permute-start(bf16[2,272,128]{2,1,0:T(8,128)(2,1)S(1)} %two_states.1), channel_id=1, source_target_pairs={{0,32},{8,40},{16,48},{24,56},{32,0},{40,8},{48,16},{56,24},{64,96... | collective-permute-start | bytes 417800 | tf_op jit(solution)/shard_map/ppermute | solution.py:470
  55.4 13.3 %collective-permute-start.5 = (bf16[400,128]{1,0:T(8,128)(2,1)S(1)}, bf16[400,128]{1,0:T(8,128)(2,1)S(1)}, u32[]{:S(2)}, u32[]{:S(2)}) collective-permute-start(bf16[400,128]{1,0:T(8,128)(2,1)S(1)} %pair_state.1.pair_ref), channel_id=1, source_target_pairs={{0,96},{8,104},{16,112},{24,120},{32,64},{40,72},{48,80},{56,88},{... | collective-permute-start | bytes 307208 | tf_op jit(solution)/shard_map/ppermute | solution.py:470
  61.7 17.4 %collective-permute-start.4 = (bf16[4,64,128]{2,1,0:T(8,128)(2,1)S(1)}, bf16[4,64,128]{2,1,0:T(8,128)(2,1)S(1)}, u32[]{:S(2)}, u32[]{:S(2)}) collective-permute-start(bf16[4,64,128]{2,1,0:T(8,128)(2,1)S(1)} %get-tuple-element.39.half_ref), channel_id=1, source_target_pairs={{0,4},{4,0},{1,5},{5,1},{2,6},{6,2},{3,7},{7,3},{8,12},{12,8},{9,1... | collective-permute-start | bytes 196616 | tf_op jit(solution)/shard_map/ppermute | solution.py:589
  70.3 10.2 %collective-permute-start.10 = (bf16[656,128]{1,0:T(8,128)(2,1)S(1)}, bf16[656,128]{1,0:T(8,128)(2,1)S(1)}, u32[]{:S(2)}, u32[]{:S(2)}) collective-permute-start(bf16[656,128]{1,0:T(8,128)(2,1)S(1)} %get-tuple-element.44), channel_id=1, source_target_pairs={{0,384},{8,392},{16,400},{24,408},{32,416},{40,424},{48,432},{56,4... | collective-permute-start | bytes 503816 | tf_op jit(solution)/shard_map/ppermute | solution.py:479
  74.7 5.8 %collective-permute-start.8 = (bf16[656,128]{1,0:T(8,128)(2,1)S(1)}, bf16[656,128]{1,0:T(8,128)(2,1)S(1)}, u32[]{:S(2)}, u32[]{:S(2)}) collective-permute-start(bf16[656,128]{1,0:T(8,128)(2,1)S(1)} %get-tuple-element.44), channel_id=1, source_target_pairs={{0,128},{8,136},{16,144},{24,152},{32,160},{40,168},{48,176},{56,1... | collective-permute-start | bytes 503816 | tf_op jit(solution)/shard_map/ppermute | solution.py:479
  76.0 6.7 %collective-permute-start.9 = (bf16[656,128]{1,0:T(8,128)(2,1)S(1)}, bf16[656,128]{1,0:T(8,128)(2,1)S(1)}, u32[]{:S(2)}, u32[]{:S(2)}) collective-permute-start(bf16[656,128]{1,0:T(8,128)(2,1)S(1)} %get-tuple-element.44), channel_id=1, source_target_pairs={{0,256},{8,264},{16,272},{24,280},{32,288},{40,296},{48,304},{56,3... | collective-permute-start | bytes 503816 | tf_op jit(solution)/shard_map/ppermute | solution.py:479
  83.6 13.9 %collective-permute-start.11 = (bf16[128,640]{1,0:T(8,128)(2,1)S(1)}, bf16[128,640]{1,0:T(8,128)(2,1)S(1)}, u32[]{:S(2)}, u32[]{:S(2)}) collective-permute-start(bf16[128,640]{1,0:T(8,128)(2,1)S(1)} %get-tuple-element.46), channel_id=1, source_target_pairs={{0,16},{8,24},{16,0},{24,8},{32,48},{40,56},{48,32},{56,40},{64,80... | collective-permute-start | bytes 491528 | tf_op jit(solution)/shard_map/ppermute | solution.py:485
  85.5 12.0 %collective-permute-start.12 = (bf16[128,640]{1,0:T(8,128)(2,1)S(1)}, bf16[128,640]{1,0:T(8,128)(2,1)S(1)}, u32[]{:S(2)}, u32[]{:S(2)}) collective-permute-start(bf16[128,640]{1,0:T(8,128)(2,1)S(1)} %get-tuple-element.47), channel_id=1, source_target_pairs={{0,24},{8,16},{16,8},{24,0},{32,56},{40,48},{48,40},{56,32},{64,88... | collective-permute-start | bytes 491528 | tf_op jit(solution)/shard_map/ppermute | solution.py:485
  88.7 13.3 %copy-start = (bf16[128,2560]{1,0:T(8,128)(2,1)S(1)}, bf16[128,2560]{1,0:T(8,128)(2,1)}, u32[]{:S(2)}) copy-start(bf16[128,2560]{1,0:T(8,128)(2,1)} %gate_ref.1) | copy-start | bytes 1966084
  88.7 13.2 %collective-permute-start.13 = (bf16[128,640]{1,0:T(8,128)(2,1)S(1)}, bf16[128,640]{1,0:T(8,128)(2,1)S(1)}, u32[]{:S(2)}, u32[]{:S(2)}) collective-permute-start(bf16[128,640]{1,0:T(8,128)(2,1)S(1)} %get-tuple-element.48), channel_id=1, source_target_pairs={{0,8},{8,0},{16,24},{24,16},{32,40},{40,32},{48,56},{56,48},{64,72... | collective-permute-start | bytes 491528 | tf_op jit(solution)/shard_map/ppermute | solution.py:485
  92.6 12.4 %copy-start.12 = (f32[2560]{0:T(1024)S(1)}, f32[2560]{0:T(1024)}, u32[]{:S(2)}) copy-start(f32[2560]{0:T(1024)} %param.15) | copy-start | bytes 30724
  102.6 3.3 %collective-permute-start.14 = (f32[128,128]{1,0:T(8,128)S(1)}, f32[128,128]{1,0:T(8,128)S(1)}, u32[]{:S(2)}, u32[]{:S(2)}) collective-permute-start(f32[128,128]{1,0:T(8,128)S(1)} %get-tuple-element.50.own_ref), channel_id=1, source_target_pairs={{0,4},{4,0},{1,5},{5,1},{2,6},{6,2},{3,7},{7,3},{8,12},{12,8},{9,1... | collective-permute-start | bytes 196616 | tf_op jit(solution)/shard_map/ppermute | solution.py:636

commit v4 on v3

--- a/solution.py
+++ b/solution.py
@@ -168,10 +168,13 @@
 
 
 def local_kernel(
-    x_hbm, b_hbm, c_hbm, step_hbm, weight_hbm, within_ref, out_ref,
-    x_ref, b_ref, c_ref, step_ref, weight_ref, sems,
+    x_hbm, b_hbm, c_hbm, step_hbm, weight_hbm, gate_hbm, within_ref, out_ref, silu_ref,
+    x_ref, b_ref, c_ref, step_ref, weight_ref, gate_ref, sems,
 ):
-    pairs = ((x_hbm, x_ref), (b_hbm, b_ref), (c_hbm, c_ref), (step_hbm, step_ref), (weight_hbm.at[0], weight_ref))
+    pairs = (
+        (x_hbm, x_ref), (b_hbm, b_ref), (c_hbm, c_ref), (step_hbm, step_ref),
+        (weight_hbm.at[0], weight_ref), (gate_hbm, gate_ref),
+    )
     copies = [pltpu.make_async_copy(*p, sems.at[i]) for i, p in enumerate(pairs)]
     for c in copies:
         c.start()
@@ -200,6 +203,8 @@
         both = jnp.concatenate([mixing(2 * pair), mixing(2 * pair + 1)], axis=1)
         sides = jnp.concatenate([jnp.where(left, x, zero), jnp.where(left, zero, x)], axis=0)
         out_ref[:, cols] = dot(both, sides)
+        gate = gate_ref[:, cols].astype(f32)
+        silu_ref[:, cols] = gate / (1.0 + jnp.exp(-gate))
 
 
 def total_of(meta, tile):
@@ -332,7 +337,7 @@
 
 
 def near_kernel(
-    parts_ref, half_ref, other_ref, next_ref, pair_ref, out_ref, c_ref
+    parts_ref, half_ref, other_ref, next_ref, pair_ref, out_ref, c_ref, gain_ref
 ):
     group = spots()[0]
     for place in range(PLACES):
@@ -355,7 +360,7 @@
             b3.append(split(odd * next_ref[rows, :].astype(f32)))
             w4 = upper * jnp.exp(third * total_of(next_meta, tile))
             b4.append(split(w4 * pair_ref[rows, :].astype(f32)))
-        spread = [gain_spread(tiles, level) for level in range(4)]
+        spread = [gain_spread(tiles, level) for level in range(LEVELS)]
         low_w, mid_w, high_w = wide(low_b), wide(mid_b), wide(high_b)
         b3_w, b4_w = wide(b3), wide(b4)
         lanes = slice(start * 128, (start + len(tiles)) * 128)
@@ -365,8 +370,10 @@
             gains = parts_ref[place, SIDE:, :]
             acc = spread_gain(gains, spread[2]) * dot(cc, b3_w)
             acc = acc + spread_gain(gains, spread[3]) * dot(cc, b4_w)
-            if place:
-                acc = acc * block_lead(part_metas, place, tiles)
+            lead = block_lead(part_metas, place, tiles)
+            for k in range(2):
+                gain_ref[place, k, :, lanes] = spread_gain(gains, spread[4 + k]) * lead
+            acc = acc * lead
             if place == 1:
                 acc = acc + spread_gain(gains, spread[0]) * dot(c, low_w)
             if place == 3:
@@ -378,10 +385,9 @@
 
 
 def far_kernel(
-    masks, parts_ref, c_ref, next_ref, pair_ref, r1_ref, r2_ref, r3_ref, near_ref, *out_refs
+    masks, c_ref, gain_ref, next_ref, pair_ref, r1_ref, r2_ref, r3_ref, near_ref, *out_refs
 ):
     group, row = spots()[:2]
-    part_metas = [parts_ref[j, BODY:SIDE, :].astype(f32) for j in range(PLACES)]
     metas = [r[BODY:, :].astype(f32) for r in (next_ref, pair_ref)]
     odd_group, upper_group = flag(group % 2 == 1), flag(group >= 2)
     row_metas = [r[BODY:, :].astype(f32) for r in (r1_ref, r2_ref)]
@@ -399,21 +405,19 @@
             b5.append(split((lead * odd) * v1))
             w2, w3 = lead * upper * jnp.exp(t1), lead * third * jnp.exp(t1 + t2)
             b6.append(split((lead * second) * v1 + w2 * v2 + w3 * v3))
-        spread = [gain_spread(tiles, level) for level in (4, 5)]
         b5_w, b6_w = wide(b5), wide(b6)
         lanes = slice(start * 128, (start + len(tiles)) * 128)
         for mask, out_ref in zip(masks, out_refs):
             place = spots()[2] ^ mask
             c = c_ref[place]
             cc = jnp.concatenate([c, c], axis=1)
-            gains = parts_ref[place, SIDE:, :]
-            acc = spread_gain(gains, spread[0]) * dot(cc, b5_w)
-            acc = acc + spread_gain(gains, spread[1]) * dot(cc, b6_w)
-            acc = acc * block_lead(part_metas, place, tiles) + near_ref[place, :, lanes]
+            acc = gain_ref[place, 0, :, lanes] * dot(cc, b5_w)
+            acc = acc + gain_ref[place, 1, :, lanes] * dot(cc, b6_w)
+            acc = acc + near_ref[place, :, lanes]
             out_ref[:, lanes] = acc.astype(bf16)
 
 
-def gate_kernel(local_ref, gate_ref, *refs):
+def gate_kernel(local_ref, silu_ref, *refs):
     reached, (gated_ref, square_ref) = refs[:PLACES], refs[PLACES:]
     acc = jnp.zeros((128, 128), f32)
     for mask, reached_ref in zip(MASKS, reached):
@@ -421,8 +425,7 @@
         for tile in range(TILES):
             cols = pl.ds(pl.multiple_of(start + tile * 128, 128), 128)
             mixed = local_ref[:, cols] + reached_ref[:, tile * 128 : (tile + 1) * 128].astype(f32)
-            gate = gate_ref[:, cols].astype(f32)
-            gated = (mixed * (gate / (1.0 + jnp.exp(-gate)))).astype(bf16)
+            gated = (mixed * silu_ref[:, cols]).astype(bf16)
             gated_ref[:, cols] = gated
             full = gated.astype(f32)
             acc = acc + full * full
@@ -545,24 +548,26 @@
             pltpu.SemaphoreType.DMA((2,)),
         ],
     )
-    (local,) = call(
+    local, silu = call(
         local_kernel,
         "local_part",
-        [((128, COLS), f32)],
+        [((128, COLS), f32), ((128, COLS), f32)],
         mixer_input,
         input_proj,
         output_proj,
         step_size,
         level_weight,
+        gate_input,
         within,
-        far=5,
+        far=6,
         scratch=[
             pltpu.VMEM((128, COLS), bf16),
             pltpu.VMEM((128, 128), bf16),
             pltpu.VMEM((128, 128), bf16),
             pltpu.VMEM((HEADS, 128), f32),
             pltpu.VMEM((HEADS, 128), f32),
-            pltpu.SemaphoreType.DMA((5,)),
+            pltpu.VMEM((128, COLS), bf16),
+            pltpu.SemaphoreType.DMA((6,)),
         ],
         flops=10**10,
         size=10**7,
@@ -577,12 +582,12 @@
         [ahead, behind, ((PLACES, KEEP, 128), bf16), ((PLACES, 64, 128), bf16)],
         *got,
     )
-    beside = to_group(sums, lambda g: g ^ 1)
     opposite = to_group(late_sums, lambda g: 3 - g)
-    (pair,) = call(pair_kernel, "pair_state", [ahead], sums, beside)
     (both,) = call(
         both_kernel, "two_states", [((2,) + behind[0], bf16)], late_sums, opposite
     )
+    beside = to_group(sums, lambda g: g ^ 1)
+    (pair,) = call(pair_kernel, "pair_state", [ahead], sums, beside)
     late_beside = to_group(both, lambda g: g ^ 1)
     other_pair = to_group(pair, lambda g: 3 - g)
     halves_now, _ = lax.optimization_barrier((halves, pair))
@@ -599,10 +604,10 @@
         late_beside,
     )
     rows = [to_row(total, k) for k in (1, 2, 3)]
-    near, c_all = call(
+    near, c_all, far_gains = call(
         near_kernel,
         "near_levels",
-        [((PLACES, 128, PART), f32), ((PLACES, 128, 128), bf16)],
+        [((PLACES, 128, PART), f32), ((PLACES, 128, 128), bf16), ((PLACES, 2, 128, PART), f32)],
         parts,
         halves,
         others,
@@ -616,8 +621,8 @@
             functools.partial(far_kernel, masks),
             "far_levels",
             [((128, PART), bf16)] * len(masks),
-                parts,
-            c_all,
+                c_all,
+            far_gains,
             neighbour,
             other_pair,
             *rows,
@@ -630,7 +635,7 @@
         "gate",
         [((128, COLS), bf16), ((128, 128), f32)],
         local,
-        gate_input,
+        silu,
         *back,
     )
     other = lax.ppermute(square, "head", [(0, 1), (1, 0)])

time: 108 us -> 108 us (level)
  transfers between devices with their start and end apart: 15 -> 15, of which waited for: 9 -> 9; matrix products, arithmetic and copies ran while one was open for 0% -> 0% of each run, Pallas kernels for 4% -> 5%
where the time goes in v4:
time: 108 us; the launch traced here: 106 us
  starting transfers between devices  61.9 us (57%)
  waiting for transfers between devices  28.3 us (26%)
  Pallas kernels  10.9 us (10%)
  local copies, waits for them, and re-layouts  4.92 us (5%)
    ppermute x4, starting transfers between devices, to_group(): return lax.ppermute(value, 'ctx', pairs)  28.2 us
    ppermute x6, starting transfers between devices, to_place(): lax.ppermute(value, 'ctx', [(i, i ^ mask) for i in range(ROWS * GROUPS *...  19.6 us
    ppermute x6, waiting for transfers between devices, to_place(): lax.ppermute(value, 'ctx', [(i, i ^ mask) for i in range(ROWS * GROUPS *...  17.1 us
    pallas_call x12, Pallas kernels, call(): pl.pallas_call(kernel, name=name, in_specs=specs, out_specs=[whole] * len...  10.9 us
    ppermute x3, starting transfers between devices, to_row(): return lax.ppermute(value, 'ctx', pairs)  8.77 us
    ppermute x4, waiting for transfers between devices, to_group(): return lax.ppermute(value, 'ctx', pairs)  8.6 us
    unnamed x26, local copies, waits for them, and re-layouts  4.91 us
    ppermute x1, starting transfers between devices, on_device(): others = lax.ppermute(halves_now, 'head', [(0, 1), (1, 0)])  3.02 us
  transfers between devices with their start and end apart: 15, of which 9 were waited for; matrix products, arithmetic and copies ran while one was open for 0% of the time, Pallas kernels for 5%

profile of v4, /device:TPU:1, one launch (start us, length us, event | category | flops | bytes accessed | tf_op | source)
XLA Modules:
  0.0 106.5 jit_solution(7662418368889464314)
XLA Ops:
  0.0 3.1 %first_states.1 = (bf16[784,128]{1,0:T(8,128)(2,1)}, bf16[784,128]{1,0:T(8,128)(2,1)}, bf16[784,128]{1,0:T(8,128)(2,1)}, f32[40,128]{1,0:T(8,128)}, bf16[128,128...) custom-call(bf16[128,2560]{1,0:T(8,128)(2,1)} %x_ref.3, ...), custom_call_target="tpu_custom_call" | custom-call | flops 100000000 | bytes 4000000 | tf_op jit(solution)/shard_map/first_states/pallas_call | solution.py:448
  3.1 5.7 %collective-permute-start = (bf16[784,128]{1,0:T(8,128)(2,1)}, bf16[784,128]{1,0:T(8,128)(2,1)S(1)}, u32[]{:S(2)}, u32[]{:S(2)}) collective-permute-start(bf16[784,128]{1,0:T(8,128)(2,1)} %get-tuple-element.34), channel_id=1, source_target_pairs={{0,16},{8,24},{16,0},{24,8},{32,48},{40,56},{48,32},{56,40},{64,80... | collective-permute-start | bytes 602120 | tf_op jit(solution)/shard_map/ppermute | solution.py:488
  8.9 3.3 %collective-permute-start.1 = (bf16[784,128]{1,0:T(8,128)(2,1)}, bf16[784,128]{1,0:T(8,128)(2,1)S(1)}, u32[]{:S(2)}, u32[]{:S(2)}) collective-permute-start(bf16[784,128]{1,0:T(8,128)(2,1)} %get-tuple-element.35), channel_id=1, source_target_pairs={{0,24},{8,16},{16,8},{24,0},{32,56},{40,48},{48,40},{56,32},{64,88... | collective-permute-start | bytes 602120 | tf_op jit(solution)/shard_map/ppermute | solution.py:488
  12.1 2.2 %collective-permute-start.2 = (bf16[784,128]{1,0:T(8,128)(2,1)}, bf16[784,128]{1,0:T(8,128)(2,1)S(1)}, u32[]{:S(2)}, u32[]{:S(2)}) collective-permute-start(bf16[784,128]{1,0:T(8,128)(2,1)} %get-tuple-element.36), channel_id=1, source_target_pairs={{0,8},{8,0},{16,24},{24,16},{32,40},{40,32},{48,56},{56,48},{64,72... | collective-permute-start | bytes 602120 | tf_op jit(solution)/shard_map/ppermute | solution.py:488
  14.3 0.0 copy-start
  14.3 1.1 %copy-done = bf16[128,2560]{1,0:T(8,128)(2,1)S(1)} copy-done((bf16[128,2560]{1,0:T(8,128)(2,1)S(1)}, bf16[128,2560]{1,0:T(8,128)(2,1)}, u32[]{:S(2)}) %copy-start) | copy-done | bytes 655384
  15.4 0.8 copy-done.4
  16.2 0.8 copy-done.7
  17.0 0.8 copy-done.8
  17.8 0.8 copy-done.9
  18.5 0.7 copy-done.11
  19.2 0.5 second_states.1.refs_3_
  19.7 0.0 copy-start.1
  19.7 0.0 copy-start.2
  19.7 0.0 copy-start.3
  19.8 0.0 copy-start.5
  19.8 0.0 copy-start.6
  19.8 0.3 collective-permute-done.refs_0_
  20.1 0.0 collective-permute-done.1.refs_1_
  20.1 7.3 %collective-permute-done.2.refs_2_ = bf16[784,128]{1,0:T(8,128)(2,1)S(1)} collective-permute-done((bf16[784,128]{1,0:T(8,128)(2,1)}, bf16[784,128]{1,0:T(8,128)(2,1)S(1)}, u32[]{:S(2)}, u32[]{:S(2)}) %collective-permute-start.2) | collective-permute-done | bytes 200736 | tf_op jit(solution)/shard_map/ppermute | solution.py:488
  27.3 0.2 group_state.1
  27.6 8.9 %collective-permute-start.3 = (bf16[400,128]{1,0:T(8,128)(2,1)S(1)}, bf16[400,128]{1,0:T(8,128)(2,1)S(1)}, u32[]{:S(2)}, u32[]{:S(2)}) collective-permute-start(bf16[400,128]{1,0:T(8,128)(2,1)S(1)} %get-tuple-element.43.own_ref), channel_id=1, source_target_pairs={{0,32},{8,40},{16,48},{24,56},{32,0},{40,8},{48,16},{56,24},{64,96... | collective-permute-start | bytes 307208 | tf_op jit(solution)/shard_map/ppermute | solution.py:473
  36.5 8.2 %collective-permute-start.6 = (bf16[272,128]{1,0:T(8,128)(2,1)S(1)}, bf16[272,128]{1,0:T(8,128)(2,1)S(1)}, u32[]{:S(2)}, u32[]{:S(2)}) collective-permute-start(bf16[272,128]{1,0:T(8,128)(2,1)S(1)} %get-tuple-element.45.own_ref), channel_id=1, source_target_pairs={{0,96},{8,104},{16,112},{24,120},{32,64},{40,72},{48,80},{56,88},{... | collective-permute-start | bytes 208904 | tf_op jit(solution)/shard_map/ppermute | solution.py:473
  44.6 5.9 %collective-permute-done.6.opposite_ref = bf16[272,128]{1,0:T(8,128)(2,1)S(1)} collective-permute-done((bf16[272,128]{1,0:T(8,128)(2,1)S(1)}, bf16[272,128]{1,0:T(8,128)(2,1)S(1)}, u32[]{:S(2)}, u32[]{:S(2)}) %collective-permute-start.6) | collective-permute-done | bytes 69664 | tf_op jit(solution)/shard_map/ppermute | solution.py:473
  50.5 4.8 %collective-permute-start.7 = (bf16[2,272,128]{2,1,0:T(8,128)(2,1)S(1)}, bf16[2,272,128]{2,1,0:T(8,128)(2,1)S(1)}, u32[]{:S(2)}, u32[]{:S(2)}) collective-permute-start(bf16[2,272,128]{2,1,0:T(8,128)(2,1)S(1)} %two_states.1), channel_id=1, source_target_pairs={{0,32},{8,40},{16,48},{24,56},{32,0},{40,8},{48,16},{56,24},{64,96... | collective-permute-start | bytes 417800 | tf_op jit(solution)/shard_map/ppermute | solution.py:473
  55.4 0.1 pair_state.1.pair_ref
  55.4 6.3 %collective-permute-start.5 = (bf16[400,128]{1,0:T(8,128)(2,1)S(1)}, bf16[400,128]{1,0:T(8,128)(2,1)S(1)}, u32[]{:S(2)}, u32[]{:S(2)}) collective-permute-start(bf16[400,128]{1,0:T(8,128)(2,1)S(1)} %pair_state.1.pair_ref), channel_id=1, source_target_pairs={{0,96},{8,104},{16,112},{24,120},{32,64},{40,72},{48,80},{56,88},{... | collective-permute-start | bytes 307208 | tf_op jit(solution)/shard_map/ppermute | solution.py:473
  61.7 3.0 %collective-permute-start.4 = (bf16[4,64,128]{2,1,0:T(8,128)(2,1)S(1)}, bf16[4,64,128]{2,1,0:T(8,128)(2,1)S(1)}, u32[]{:S(2)}, u32[]{:S(2)}) collective-permute-start(bf16[4,64,128]{2,1,0:T(8,128)(2,1)S(1)} %get-tuple-element.44.half_ref), channel_id=1, source_target_pairs={{0,4},{4,0},{1,5},{5,1},{2,6},{6,2},{3,7},{7,3},{8,12},{12,8},{9,1... | collective-permute-start | bytes 196616 | tf_op jit(solution)/shard_map/ppermute | solution.py:594
  64.8 2.6 %local_part.1 = (f32[128,2560]{1,0:T(8,128)S(1)}, f32[128,2560]{1,0:T(8,128)S(1)}) custom-call(bf16[128,2560]{1,0:T(8,128)(2,1)S(1)} %copy-done.1, bf16[128,128]{1,0:T(8,128)(2,1)S(1)} %copy-done.3, bf16[128,128]{1,0:T(8,128)(2,1)S(1)} %copy-done.4, f32[40,128]{1,0:T(8,128)S(1)} %copy-done.5, f32[7,40,128]{2,1,0:T(8,128)S(1)} %copy-done.2, ...), custom_call_target="tpu_custom_call" | custom-call | flops 10000000000 | bytes 10000000 | tf_op jit(solution)/shard_map/local_part/pallas_call | solution.py:448
  67.4 1.3 %collective-permute-done.5.far_ref = bf16[400,128]{1,0:T(8,128)(2,1)S(1)} collective-permute-done((bf16[400,128]{1,0:T(8,128)(2,1)S(1)}, bf16[400,128]{1,0:T(8,128)(2,1)S(1)}, u32[]{:S(2)}, u32[]{:S(2)}) %collective-permute-start.5) | collective-permute-done | bytes 102432 | tf_op jit(solution)/shard_map/ppermute | solution.py:473
  68.7 1.4 %collective-permute-done.7.beside_ref = bf16[2,272,128]{2,1,0:T(8,128)(2,1)S(1)} collective-permute-done((bf16[2,272,128]{2,1,0:T(8,128)(2,1)S(1)}, bf16[2,272,128]{2,1,0:T(8,128)(2,1)S(1)}, u32[]{:S(2)}, u32[]{:S(2)}) %collective-permute-start.7) | collective-permute-done | bytes 139296 | tf_op jit(solution)/shard_map/ppermute | solution.py:473
  70.1 0.2 row_state.1
  70.3 4.4 %collective-permute-start.10 = (bf16[656,128]{1,0:T(8,128)(2,1)S(1)}, bf16[656,128]{1,0:T(8,128)(2,1)S(1)}, u32[]{:S(2)}, u32[]{:S(2)}) collective-permute-start(bf16[656,128]{1,0:T(8,128)(2,1)S(1)} %get-tuple-element.50), channel_id=1, source_target_pairs={{0,384},{8,392},{16,400},{24,408},{32,416},{40,424},{48,432},{56,4... | collective-permute-start | bytes 503816 | tf_op jit(solution)/shard_map/ppermute | solution.py:482
  74.7 1.3 %collective-permute-start.8 = (bf16[656,128]{1,0:T(8,128)(2,1)S(1)}, bf16[656,128]{1,0:T(8,128)(2,1)S(1)}, u32[]{:S(2)}, u32[]{:S(2)}) collective-permute-start(bf16[656,128]{1,0:T(8,128)(2,1)S(1)} %get-tuple-element.50), channel_id=1, source_target_pairs={{0,128},{8,136},{16,144},{24,152},{32,160},{40,168},{48,176},{56,1... | collective-permute-start | bytes 503816 | tf_op jit(solution)/shard_map/ppermute | solution.py:482
  76.0 3.1 %collective-permute-start.9 = (bf16[656,128]{1,0:T(8,128)(2,1)S(1)}, bf16[656,128]{1,0:T(8,128)(2,1)S(1)}, u32[]{:S(2)}, u32[]{:S(2)}) collective-permute-start(bf16[656,128]{1,0:T(8,128)(2,1)S(1)} %get-tuple-element.50), channel_id=1, source_target_pairs={{0,256},{8,264},{16,272},{24,280},{32,288},{40,296},{48,304},{56,3... | collective-permute-start | bytes 503816 | tf_op jit(solution)/shard_map/ppermute | solution.py:482
  79.1 1.8 %near_levels.1 = (f32[4,128,640]{2,1,0:T(8,128)S(1)}, bf16[4,128,128]{2,1,0:T(8,128)(2,1)S(1)}, f32[4,2,128,640]{3,2,1,0:T(8,128)S(1)}) custom-call(bf16[4,720,128]{2,1,0:T(8,128)(2,1)S(1)} %get-tuple-element.41.parts_ref, bf16[4,64,128]{2,1,0:T(8,128)(2,1)S(1)} %get-tuple-element.44.half_ref, bf16[4,64,128]{2,1,0:T(8,128)(2,1)S(1)} %collective-permute-done.4.other_ref, ...), custom_call_target="tpu_custom_call" | custom-call | flops 10000000000 | bytes 4000000 | tf_op jit(solution)/shard_map/near_levels/pallas_call | solution.py:448
  80.9 1.8 %collective-permute-done.9.r2_ref = bf16[656,128]{1,0:T(8,128)(2,1)S(1)} collective-permute-done((bf16[656,128]{1,0:T(8,128)(2,1)S(1)}, bf16[656,128]{1,0:T(8,128)(2,1)S(1)}, u32[]{:S(2)}, u32[]{:S(2)}) %collective-permute-start.9) | collective-permute-done | bytes 167968 | tf_op jit(solution)/shard_map/ppermute | solution.py:482
  82.7 0.6 far_levels.2
  83.3 1.9 %collective-permute-start.11 = (bf16[128,640]{1,0:T(8,128)(2,1)S(1)}, bf16[128,640]{1,0:T(8,128)(2,1)S(1)}, u32[]{:S(2)}, u32[]{:S(2)}) collective-permute-start(bf16[128,640]{1,0:T(8,128)(2,1)S(1)} %get-tuple-element.52), channel_id=1, source_target_pairs={{0,16},{8,24},{16,0},{24,8},{32,48},{40,56},{48,32},{56,40},{64,80... | collective-permute-start | bytes 491528 | tf_op jit(solution)/shard_map/ppermute | solution.py:488
  85.3 3.2 %collective-permute-start.12 = (bf16[128,640]{1,0:T(8,128)(2,1)S(1)}, bf16[128,640]{1,0:T(8,128)(2,1)S(1)}, u32[]{:S(2)}, u32[]{:S(2)}) collective-permute-start(bf16[128,640]{1,0:T(8,128)(2,1)S(1)} %get-tuple-element.53), channel_id=1, source_target_pairs={{0,24},{8,16},{16,8},{24,0},{32,56},{40,48},{48,40},{56,32},{64,88... | collective-permute-start | bytes 491528 | tf_op jit(solution)/shard_map/ppermute | solution.py:488
  88.4 3.3 %collective-permute-start.13 = (bf16[128,640]{1,0:T(8,128)(2,1)S(1)}, bf16[128,640]{1,0:T(8,128)(2,1)S(1)}, u32[]{:S(2)}, u32[]{:S(2)}) collective-permute-start(bf16[128,640]{1,0:T(8,128)(2,1)S(1)} %get-tuple-element.54), channel_id=1, source_target_pairs={{0,8},{8,0},{16,24},{24,16},{32,40},{40,32},{48,56},{56,48},{64,72... | collective-permute-start | bytes 491528 | tf_op jit(solution)/shard_map/ppermute | solution.py:488
  91.7 0.4 far_levels.3.refs_3_
  92.2 5.1 %collective-permute-done.11.refs_0_ = bf16[128,640]{1,0:T(8,128)(2,1)S(1)} collective-permute-done((bf16[128,640]{1,0:T(8,128)(2,1)S(1)}, bf16[128,640]{1,0:T(8,128)(2,1)S(1)}, u32[]{:S(2)}, u32[]{:S(2)}) %collective-permute-start.11) | collective-permute-done | bytes 163872 | tf_op jit(solution)/shard_map/ppermute | solution.py:488
  97.3 4.4 %collective-permute-done.13.refs_2_ = bf16[128,640]{1,0:T(8,128)(2,1)S(1)} collective-permute-done((bf16[128,640]{1,0:T(8,128)(2,1)S(1)}, bf16[128,640]{1,0:T(8,128)(2,1)S(1)}, u32[]{:S(2)}, u32[]{:S(2)}) %collective-permute-start.13) | collective-permute-done | bytes 163872 | tf_op jit(solution)/shard_map/ppermute | solution.py:488
  101.7 0.4 gate.1
  102.1 2.4 %collective-permute-start.14 = (f32[128,128]{1,0:T(8,128)S(1)}, f32[128,128]{1,0:T(8,128)S(1)}, u32[]{:S(2)}, u32[]{:S(2)}) collective-permute-start(f32[128,128]{1,0:T(8,128)S(1)} %get-tuple-element.56.own_ref), channel_id=1, source_target_pairs={{0,4},{4,0},{1,5},{5,1},{2,6},{6,2},{3,7},{7,3},{8,12},{12,8},{9,1... | collective-permute-start | bytes 196616 | tf_op jit(solution)/shard_map/ppermute | solution.py:641
  104.5 0.9 collective-permute-done.14.other_ref
  105.4 1.1 %norm.1 = bf16[128,2560]{1,0:T(8,128)(2,1)} custom-call(bf16[128,2560]{1,0:T(8,128)(2,1)S(1)} %get-tuple-element.55.gated_ref, f32[128,128]{1,0:T(8,128)S(1)} %get-tuple-element.56.own_ref, f32[128,128]{1,0:T(8,128)S(1)} %collective-permute-done.14.other_ref, f32[1,2560]{1,0:T(1,128)S(1)} %reshape.3.weight_ref), custom_call_target="tpu_custom_call" | custom-call | flops 100000000 | bytes 4000000 | tf_op jit(solution)/shard_map/norm/pallas_call | solution.py:448
  (21 shorter events, 0.1 us)
Async XLA Ops:
  3.1 17.0 %collective-permute-start = (bf16[784,128]{1,0:T(8,128)(2,1)}, bf16[784,128]{1,0:T(8,128)(2,1)S(1)}, u32[]{:S(2)}, u32[]{:S(2)}) collective-permute-start(bf16[784,128]{1,0:T(8,128)(2,1)} %get-tuple-element.34), channel_id=1, source_target_pairs={{0,16},{8,24},{16,0},{24,8},{32,48},{40,56},{48,32},{56,40},{64,80... | collective-permute-start | bytes 602120 | tf_op jit(solution)/shard_map/ppermute | solution.py:488
  8.9 11.2 %collective-permute-start.1 = (bf16[784,128]{1,0:T(8,128)(2,1)}, bf16[784,128]{1,0:T(8,128)(2,1)S(1)}, u32[]{:S(2)}, u32[]{:S(2)}) collective-permute-start(bf16[784,128]{1,0:T(8,128)(2,1)} %get-tuple-element.35), channel_id=1, source_target_pairs={{0,24},{8,16},{16,8},{24,0},{32,56},{40,48},{48,40},{56,32},{64,88... | collective-permute-start | bytes 602120 | tf_op jit(solution)/shard_map/ppermute | solution.py:488
  12.1 15.2 %collective-permute-start.2 = (bf16[784,128]{1,0:T(8,128)(2,1)}, bf16[784,128]{1,0:T(8,128)(2,1)S(1)}, u32[]{:S(2)}, u32[]{:S(2)}) collective-permute-start(bf16[784,128]{1,0:T(8,128)(2,1)} %get-tuple-element.36), channel_id=1, source_target_pairs={{0,8},{8,0},{16,24},{24,16},{32,40},{40,32},{48,56},{56,48},{64,72... | collective-permute-start | bytes 602120 | tf_op jit(solution)/shard_map/ppermute | solution.py:488
  14.3 1.1 %copy-start = (bf16[128,2560]{1,0:T(8,128)(2,1)S(1)}, bf16[128,2560]{1,0:T(8,128)(2,1)}, u32[]{:S(2)}) copy-start(bf16[128,2560]{1,0:T(8,128)(2,1)} %x_ref.3) | copy-start | bytes 1966084
  15.4 0.8 copy-start.4
  16.2 0.8 copy-start.7
  17.0 0.8 copy-start.8
  17.8 0.8 copy-start.9
  18.5 0.7 copy-start.11
  19.7 45.0 %copy-start.1 = (bf16[128,2560]{1,0:T(8,128)(2,1)S(1)}, bf16[128,2560]{1,0:T(8,128)(2,1)}, u32[]{:S(2)}) copy-start(bf16[128,2560]{1,0:T(8,128)(2,1)} %x_ref.3) | copy-start | bytes 1966084
  19.7 45.0 %copy-start.2 = (f32[7,40,128]{2,1,0:T(8,128)S(1)}, f32[7,40,128]{2,1,0:T(8,128)}, u32[]{:S(2)}) copy-start(f32[7,40,128]{2,1,0:T(8,128)} %weight_hbm.1) | copy-start | bytes 430084
  19.7 45.0 %copy-start.3 = (bf16[128,128]{1,0:T(8,128)(2,1)S(1)}, bf16[128,128]{1,0:T(8,128)(2,1)}, u32[]{:S(2)}) copy-start(bf16[128,128]{1,0:T(8,128)(2,1)} %b_hbm.1) | copy-start | bytes 98308
  19.8 45.0 %copy-start.5 = (f32[40,128]{1,0:T(8,128)S(1)}, f32[40,128]{1,0:T(8,128)}, u32[]{:S(2)}) copy-start(f32[40,128]{1,0:T(8,128)} %step_hbm.1) | copy-start | bytes 61444
  19.8 45.0 %copy-start.6 = (bf16[128,2560]{1,0:T(8,128)(2,1)S(1)}, bf16[128,2560]{1,0:T(8,128)(2,1)}, u32[]{:S(2)}) copy-start(bf16[128,2560]{1,0:T(8,128)(2,1)} %gate_hbm.1) | copy-start | bytes 1966084
  19.8 45.0 %copy-start.10 = (f32[40,128]{1,0:T(8,128)S(1)}, f32[40,128]{1,0:T(8,128)}, u32[]{:S(2)}) copy-start(f32[40,128]{1,0:T(8,128)} %get-tuple-element.31.within_ref) | copy-start | bytes 61444
  27.6 27.8 %collective-permute-start.3 = (bf16[400,128]{1,0:T(8,128)(2,1)S(1)}, bf16[400,128]{1,0:T(8,128)(2,1)S(1)}, u32[]{:S(2)}, u32[]{:S(2)}) collective-permute-start(bf16[400,128]{1,0:T(8,128)(2,1)S(1)} %get-tuple-element.43.own_ref), channel_id=1, source_target_pairs={{0,32},{8,40},{16,48},{24,56},{32,0},{40,8},{48,16},{56,24},{64,96... | collective-permute-start | bytes 307208 | tf_op jit(solution)/shard_map/ppermute | solution.py:473
  36.5 14.0 %collective-permute-start.6 = (bf16[272,128]{1,0:T(8,128)(2,1)S(1)}, bf16[272,128]{1,0:T(8,128)(2,1)S(1)}, u32[]{:S(2)}, u32[]{:S(2)}) collective-permute-start(bf16[272,128]{1,0:T(8,128)(2,1)S(1)} %get-tuple-element.45.own_ref), channel_id=1, source_target_pairs={{0,96},{8,104},{16,112},{24,120},{32,64},{40,72},{48,80},{56,88},{... | collective-permute-start | bytes 208904 | tf_op jit(solution)/shard_map/ppermute | solution.py:473
  50.5 19.6 %collective-permute-start.7 = (bf16[2,272,128]{2,1,0:T(8,128)(2,1)S(1)}, bf16[2,272,128]{2,1,0:T(8,128)(2,1)S(1)}, u32[]{:S(2)}, u32[]{:S(2)}) collective-permute-start(bf16[2,272,128]{2,1,0:T(8,128)(2,1)S(1)} %two_states.1), channel_id=1, source_target_pairs={{0,32},{8,40},{16,48},{24,56},{32,0},{40,8},{48,16},{56,24},{64,96... | collective-permute-start | bytes 417800 | tf_op jit(solution)/shard_map/ppermute | solution.py:473
  55.4 13.3 %collective-permute-start.5 = (bf16[400,128]{1,0:T(8,128)(2,1)S(1)}, bf16[400,128]{1,0:T(8,128)(2,1)S(1)}, u32[]{:S(2)}, u32[]{:S(2)}) collective-permute-start(bf16[400,128]{1,0:T(8,128)(2,1)S(1)} %pair_state.1.pair_ref), channel_id=1, source_target_pairs={{0,96},{8,104},{16,112},{24,120},{32,64},{40,72},{48,80},{56,88},{... | collective-permute-start | bytes 307208 | tf_op jit(solution)/shard_map/ppermute | solution.py:473
  61.7 17.4 %collective-permute-start.4 = (bf16[4,64,128]{2,1,0:T(8,128)(2,1)S(1)}, bf16[4,64,128]{2,1,0:T(8,128)(2,1)S(1)}, u32[]{:S(2)}, u32[]{:S(2)}) collective-permute-start(bf16[4,64,128]{2,1,0:T(8,128)(2,1)S(1)} %get-tuple-element.44.half_ref), channel_id=1, source_target_pairs={{0,4},{4,0},{1,5},{5,1},{2,6},{6,2},{3,7},{7,3},{8,12},{12,8},{9,1... | collective-permute-start | bytes 196616 | tf_op jit(solution)/shard_map/ppermute | solution.py:594
  70.3 10.6 %collective-permute-start.10 = (bf16[656,128]{1,0:T(8,128)(2,1)S(1)}, bf16[656,128]{1,0:T(8,128)(2,1)S(1)}, u32[]{:S(2)}, u32[]{:S(2)}) collective-permute-start(bf16[656,128]{1,0:T(8,128)(2,1)S(1)} %get-tuple-element.50), channel_id=1, source_target_pairs={{0,384},{8,392},{16,400},{24,408},{32,416},{40,424},{48,432},{56,4... | collective-permute-start | bytes 503816 | tf_op jit(solution)/shard_map/ppermute | solution.py:482
  74.7 6.2 %collective-permute-start.8 = (bf16[656,128]{1,0:T(8,128)(2,1)S(1)}, bf16[656,128]{1,0:T(8,128)(2,1)S(1)}, u32[]{:S(2)}, u32[]{:S(2)}) collective-permute-start(bf16[656,128]{1,0:T(8,128)(2,1)S(1)} %get-tuple-element.50), channel_id=1, source_target_pairs={{0,128},{8,136},{16,144},{24,152},{32,160},{40,168},{48,176},{56,1... | collective-permute-start | bytes 503816 | tf_op jit(solution)/shard_map/ppermute | solution.py:482
  76.0 6.7 %collective-permute-start.9 = (bf16[656,128]{1,0:T(8,128)(2,1)S(1)}, bf16[656,128]{1,0:T(8,128)(2,1)S(1)}, u32[]{:S(2)}, u32[]{:S(2)}) collective-permute-start(bf16[656,128]{1,0:T(8,128)(2,1)S(1)} %get-tuple-element.50), channel_id=1, source_target_pairs={{0,256},{8,264},{16,272},{24,280},{32,288},{40,296},{48,304},{56,3... | collective-permute-start | bytes 503816 | tf_op jit(solution)/shard_map/ppermute | solution.py:482
  83.3 13.9 %collective-permute-start.11 = (bf16[128,640]{1,0:T(8,128)(2,1)S(1)}, bf16[128,640]{1,0:T(8,128)(2,1)S(1)}, u32[]{:S(2)}, u32[]{:S(2)}) collective-permute-start(bf16[128,640]{1,0:T(8,128)(2,1)S(1)} %get-tuple-element.52), channel_id=1, source_target_pairs={{0,16},{8,24},{16,0},{24,8},{32,48},{40,56},{48,32},{56,40},{64,80... | collective-permute-start | bytes 491528 | tf_op jit(solution)/shard_map/ppermute | solution.py:488
  85.3 12.0 %collective-permute-start.12 = (bf16[128,640]{1,0:T(8,128)(2,1)S(1)}, bf16[128,640]{1,0:T(8,128)(2,1)S(1)}, u32[]{:S(2)}, u32[]{:S(2)}) collective-permute-start(bf16[128,640]{1,0:T(8,128)(2,1)S(1)} %get-tuple-element.53), channel_id=1, source_target_pairs={{0,24},{8,16},{16,8},{24,0},{32,56},{40,48},{48,40},{56,32},{64,88... | collective-permute-start | bytes 491528 | tf_op jit(solution)/shard_map/ppermute | solution.py:488
  88.4 13.2 %collective-permute-start.13 = (bf16[128,640]{1,0:T(8,128)(2,1)S(1)}, bf16[128,640]{1,0:T(8,128)(2,1)S(1)}, u32[]{:S(2)}, u32[]{:S(2)}) collective-permute-start(bf16[128,640]{1,0:T(8,128)(2,1)S(1)} %get-tuple-element.54), channel_id=1, source_target_pairs={{0,8},{8,0},{16,24},{24,16},{32,40},{40,32},{48,56},{56,48},{64,72... | collective-permute-start | bytes 491528 | tf_op jit(solution)/shard_map/ppermute | solution.py:488
  101.7 2.8 %copy-start.12 = (f32[2560]{0:T(1024)S(1)}, f32[2560]{0:T(1024)}, u32[]{:S(2)}) copy-start(f32[2560]{0:T(1024)} %param.15) | copy-start | bytes 30724
  102.1 3.3 %collective-permute-start.14 = (f32[128,128]{1,0:T(8,128)S(1)}, f32[128,128]{1,0:T(8,128)S(1)}, u32[]{:S(2)}, u32[]{:S(2)}) collective-permute-start(f32[128,128]{1,0:T(8,128)S(1)} %get-tuple-element.56.own_ref), channel_id=1, source_target_pairs={{0,4},{4,0},{1,5},{5,1},{2,6},{6,2},{3,7},{7,3},{8,12},{12,8},{9,1... | collective-permute-start | bytes 196616 | tf_op jit(solution)/shard_map/ppermute | solution.py:641

commit v5 on v4

--- a/solution.py
+++ b/solution.py
@@ -19,9 +19,8 @@
 BODY = TILES * STATE
 AHEAD = 3
 META = 16
-SIDE = BODY + META
-KEEP = SIDE + 64
-MSG = KEEP + 64
+MSG = BODY + META
+EXTRA = 192
 LEVELS = 6
 FIRST, SECOND = (2, 3, 1), (0,)
 MASKS = FIRST + SECOND
@@ -61,7 +60,7 @@
     return r - turn * period, turn
 
 
-def worker_message(part, x, carry_t, last, b_t, gains, c_half, msg_ref):
+def worker_message(part, x, carry_t, last, b_t, gains, c, msg_ref, side_ref):
     head, _ = row_mod(120, HEADS, (128, 128))
     head = jnp.where(iota((128, 128), 0) >= 120, 999, head)
     side = jnp.where(iota((128, 128), 1) >= HEADDIM, 1, 0)
@@ -77,9 +76,9 @@
         msg_ref[k * STATE : (k + 1) * STATE, :] = state[:, k * 128 : (k + 1) * 128]
         pick = jnp.where(meta_row == 3 * k + lane_term, last, 0.0).astype(bf16)
         meta = meta + dot(pick, spread[k])
-    msg_ref[BODY:SIDE, :] = meta.astype(bf16)
-    msg_ref[SIDE:KEEP, :] = level_gains(part, gains)
-    msg_ref[KEEP:, :] = c_half
+    msg_ref[BODY:, :] = meta.astype(bf16)
+    side_ref[:128, :] = c
+    side_ref[128:, :] = level_gains(part, gains)
 
 
 def level_gains(part, gains):
@@ -104,16 +103,15 @@
 
 def first_kernel(
     x_ref, b_ref, c_ref, decay_ref, step_ref, weight_ref,
-    far_ref, cross_ref, beside_ref, within_ref, carry_ref, last_ref, bt_ref, gains_ref,
+    far_ref, cross_ref, beside_ref, far_side, cross_side, beside_side, within_ref, carry_ref, last_ref, bt_ref, gains_ref,
     x_buf, b_buf, c_buf, decay_buf, step_buf, weight_buf, sems,
 ):
-    half = pl.ds(pl.multiple_of(spots()[3] * 64, 64), 64)
     copies = column_copies(FIRST, x_ref, x_buf, sems) + [
         pltpu.make_async_copy(decay_ref, decay_buf, sems.at[3]),
         pltpu.make_async_copy(step_ref, step_buf, sems.at[4]),
         pltpu.make_async_copy(b_ref, b_buf, sems.at[5]),
         pltpu.make_async_copy(weight_ref, weight_buf, sems.at[6]),
-        pltpu.make_async_copy(c_ref.at[half, :], c_buf, sems.at[7]),
+        pltpu.make_async_copy(c_ref, c_buf, sems.at[7]),
     ]
     for c in copies[3:] + copies[:3]:
         c.start()
@@ -144,27 +142,25 @@
     copies[7].wait()
     for c in copies[:3]:
         c.wait()
-    for i, (mask, msg_ref) in enumerate(zip(FIRST, (far_ref, cross_ref, beside_ref))):
+    messages = zip((far_ref, cross_ref, beside_ref), (far_side, cross_side, beside_side))
+    for i, (mask, refs) in enumerate(zip(FIRST, messages)):
         part = spots()[2] ^ mask
-        worker_message(part, x_buf[i], carry_t, last, b_t, gains, c_buf[...], msg_ref)
+        worker_message(part, x_buf[i], carry_t, last, b_t, gains, c_buf[...], *refs)
 
 
 def second_kernel(
-    x_ref, c_ref, carry_ref, last_ref, bt_ref, gains_ref, own_ref,
+    x_ref, c_ref, carry_ref, last_ref, bt_ref, gains_ref, own_ref, own_side,
     x_buf, c_buf, sems,
 ):
-    half = pl.ds(pl.multiple_of(spots()[3] * 64, 64), 64)
     copies = column_copies(SECOND, x_ref, x_buf, sems)
-    copies.append(pltpu.make_async_copy(c_ref.at[half, :], c_buf, sems.at[1]))
+    copies.append(pltpu.make_async_copy(c_ref, c_buf, sems.at[1]))
     for c in copies:
         c.start()
     for c in copies:
         c.wait()
-    for i, (mask, msg_ref) in enumerate(zip(SECOND, (own_ref,))):
-        part = spots()[2] ^ mask
-        worker_message(
-            part, x_buf[i], carry_ref[...], last_ref[0:1, :], bt_ref[...], gains_ref[...], c_buf[...], msg_ref
-        )
+    worker_message(
+        spots()[2], x_buf[0], carry_ref[...], last_ref[0:1, :], bt_ref[...], gains_ref[...], c_buf[...], own_ref, own_side
+    )
 
 
 def local_kernel(
@@ -223,11 +219,10 @@
 
 
 def group_kernel(*refs):
-    got, (first_ref, second_ref, parts_ref, half_ref) = refs[:PLACES], refs[PLACES:]
+    got, (first_ref, second_ref, parts_ref) = refs[:PLACES], refs[PLACES:]
     for mask, ref in zip(MASKS, got):
-        parts_ref[spots()[2] ^ mask] = ref[:KEEP, :]
-        half_ref[spots()[2] ^ mask] = ref[KEEP:, :]
-    metas = [parts_ref[j, BODY:SIDE, :].astype(f32) for j in range(PLACES)]
+        parts_ref[spots()[2] ^ mask] = ref[...]
+    metas = [parts_ref[j, BODY:, :].astype(f32) for j in range(PLACES)]
     for tiles, out_ref in ((range(AHEAD), first_ref), (range(AHEAD, TILES), second_ref)):
         meta = jnp.zeros((META, 128), f32)
         for tile in tiles:
@@ -337,13 +332,14 @@
 
 
 def near_kernel(
-    parts_ref, half_ref, other_ref, next_ref, pair_ref, out_ref, c_ref, gain_ref
+    parts_ref, next_ref, pair_ref, far_side, cross_side, beside_side, own_side,
+    out_ref, c_ref, gain_ref, gains_ref,
 ):
     group = spots()[0]
-    for place in range(PLACES):
-        for core, ref in ((spots()[3], half_ref), (1 - spots()[3], other_ref)):
-            c_ref[place, pl.ds(pl.multiple_of(core * 64, 64), 64), :] = ref[place]
-    part_metas = [parts_ref[j, BODY:SIDE, :].astype(f32) for j in range(PLACES)]
+    for mask, ref in zip(MASKS, (far_side, cross_side, beside_side, own_side)):
+        c_ref[spots()[2] ^ mask] = ref[:128, :]
+        gains_ref[spots()[2] ^ mask] = ref[128:, :]
+    part_metas = [parts_ref[j, BODY:, :].astype(f32) for j in range(PLACES)]
     next_meta = next_ref[BODY:, :].astype(f32)
     odd, upper, third = flag(group % 2 == 1), flag(group >= 2), flag(group == 3)
     for start in range(0, TILES, 2):
@@ -367,7 +363,7 @@
         for place in range(PLACES):
             c = c_ref[place]
             cc = jnp.concatenate([c, c], axis=1)
-            gains = parts_ref[place, SIDE:, :]
+            gains = gains_ref[place]
             acc = spread_gain(gains, spread[2]) * dot(cc, b3_w)
             acc = acc + spread_gain(gains, spread[3]) * dot(cc, b4_w)
             lead = block_lead(part_metas, place, tiles)
@@ -498,14 +494,17 @@
     level_weight,
     norm_weight,
 ):
-    message = ((MSG, 128), bf16)
-    far, cross, beside, within, carry_t, last, b_t, gains = call(
+    message, extra = ((MSG, 128), bf16), ((EXTRA, 128), bf16)
+    far, cross, beside, far_side, cross_side, beside_side, within, carry_t, last, b_t, gains = call(
         first_kernel,
         "first_states",
         [
             message,
             message,
             message,
+            extra,
+            extra,
+            extra,
             ((HEADS, 128), f32),
             ((128, 128), bf16),
             ((8, 128), f32),
@@ -523,17 +522,17 @@
         scratch=[
             pltpu.VMEM((len(FIRST), 128, PART), bf16),
             pltpu.VMEM((128, 128), bf16),
-            pltpu.VMEM((64, 128), bf16),
+            pltpu.VMEM((128, 128), bf16),
             pltpu.VMEM((HEADS, 128), f32),
             pltpu.VMEM((HEADS, 128), f32),
             pltpu.VMEM((LEVELS + 1, HEADS, 128), f32),
             pltpu.SemaphoreType.DMA((8,)),
         ],
     )
-    (own,) = call(
+    own, own_side = call(
         second_kernel,
         "second_states",
-        [message],
+        [message, extra],
         mixer_input,
         output_proj,
         carry_t,
@@ -544,7 +543,7 @@
         flops=4 * 10**10,
         scratch=[
             pltpu.VMEM((len(SECOND), 128, PART), bf16),
-            pltpu.VMEM((64, 128), bf16),
+            pltpu.VMEM((128, 128), bf16),
             pltpu.SemaphoreType.DMA((2,)),
         ],
     )
@@ -576,10 +575,10 @@
     ahead = ((AHEAD * STATE + META, 128), bf16)
     behind = (((TILES - AHEAD) * STATE + META, 128), bf16)
     whole = ((BODY + META, 128), bf16)
-    sums, late_sums, parts, halves = call(
+    sums, late_sums, parts = call(
         group_kernel,
         "group_state",
-        [ahead, behind, ((PLACES, KEEP, 128), bf16), ((PLACES, 64, 128), bf16)],
+        [ahead, behind, ((PLACES, MSG, 128), bf16)],
         *got,
     )
     opposite = to_group(late_sums, lambda g: 3 - g)
@@ -590,8 +589,8 @@
     (pair,) = call(pair_kernel, "pair_state", [ahead], sums, beside)
     late_beside = to_group(both, lambda g: g ^ 1)
     other_pair = to_group(pair, lambda g: 3 - g)
-    halves_now, _ = lax.optimization_barrier((halves, pair))
-    others = lax.ppermute(halves_now, "head", [(0, 1), (1, 0)])
+    sides, _ = lax.optimization_barrier(((far_side, cross_side, beside_side), sums))
+    sides = [to_place(v, mask) for mask, v in zip(MASKS, sides)] + [own_side]
     neighbour, other_pair, total = call(
         row_kernel,
         "row_state",
@@ -609,10 +608,10 @@
         "near_levels",
         [((PLACES, 128, PART), f32), ((PLACES, 128, 128), bf16), ((PLACES, 2, 128, PART), f32)],
         parts,
-        halves,
-        others,
         neighbour,
         other_pair,
+        *sides,
+        scratch=[pltpu.VMEM((PLACES, 64, 128), bf16)],
         flops=10**10,
     )
     reached = []

time: 108 us -> 107 us (level)
  waiting for transfers between devices: 28.3 us -> 24.4 us
  starting transfers between devices: 61.9 us -> 65.7 us
    ppermute x6 -> x9, starting transfers between devices: 19.6 us -> 27.9 us  [to_place(): lax.ppermute(value, 'ctx', [(i, i ^ mask) for i in range(ROWS * GROUPS *...]
    ppermute x6 -> x9, waiting for transfers between devices: 17.1 us -> 13.7 us  [to_place(): lax.ppermute(value, 'ctx', [(i, i ^ mask) for i in range(ROWS * GROUPS *...]
    ppermute x1 -> x0, starting transfers between devices: 3.02 us -> none  [on_device(): others = lax.ppermute(halves_now, 'head', [(0, 1), (1, 0)])]
    ppermute x4, starting transfers between devices: 28.2 us -> 26.5 us  [to_group(): return lax.ppermute(value, 'ctx', pairs)]
    unnamed x26 -> x34, local copies, waits for them, and re-layouts: 4.91 us -> 4.93 us
  transfers between devices with their start and end apart: 15 -> 17, of which waited for: 9 -> 7; matrix products, arithmetic and copies ran while one was open for 0% -> 0% of each run, Pallas kernels for 5% -> 5%
where the time goes in v5:
time: 107 us; the launch traced here: 106 us
  starting transfers between devices  65.7 us (61%)
  waiting for transfers between devices  24.4 us (23%)
  Pallas kernels  11 us (10%)
  local copies, waits for them, and re-layouts  4.94 us (5%)
    ppermute x9, starting transfers between devices, to_place(): lax.ppermute(value, 'ctx', [(i, i ^ mask) for i in range(ROWS * GROUPS *...  27.9 us
    ppermute x4, starting transfers between devices, to_group(): return lax.ppermute(value, 'ctx', pairs)  26.5 us
    ppermute x9, waiting for transfers between devices, to_place(): lax.ppermute(value, 'ctx', [(i, i ^ mask) for i in range(ROWS * GROUPS *...  13.7 us
    pallas_call x12, Pallas kernels, call(): pl.pallas_call(kernel, name=name, in_specs=specs, out_specs=[whole] * len...  11 us
    ppermute x3, starting transfers between devices, to_row(): return lax.ppermute(value, 'ctx', pairs)  8.88 us
    ppermute x4, waiting for transfers between devices, to_group(): return lax.ppermute(value, 'ctx', pairs)  8 us
    unnamed x34, local copies, waits for them, and re-layouts  4.93 us
    ppermute x1, starting transfers between devices, on_device(): other = lax.ppermute(square, 'head', [(0, 1), (1, 0)])  2.4 us
  transfers between devices with their start and end apart: 17, of which 7 were waited for; matrix products, arithmetic and copies ran while one was open for 0% of the time, Pallas kernels for 5%

profile of v5, /device:TPU:1, one launch (start us, length us, event | category | flops | bytes accessed | tf_op | source)
XLA Modules:
  0.0 106.5 jit_solution(1512661907446584807)
XLA Ops:
  0.0 3.0 %first_states.1 = (bf16[656,128]{1,0:T(8,128)(2,1)}, bf16[656,128]{1,0:T(8,128)(2,1)}, bf16[656,128]{1,0:T(8,128)(2,1)}, bf16[192,128]{1,0:T(8,128)(2,1)}, bf16[...) custom-call(bf16[128,2560]{1,0:T(8,128)(2,1)} %x_ref.3, ...), custom_call_target="tpu_custom_call" | custom-call | flops 100000000 | bytes 4000000 | tf_op jit(solution)/shard_map/first_states/pallas_call | solution.py:444
  3.1 5.7 %collective-permute-start = (bf16[656,128]{1,0:T(8,128)(2,1)}, bf16[656,128]{1,0:T(8,128)(2,1)S(1)}, u32[]{:S(2)}, u32[]{:S(2)}) collective-permute-start(bf16[656,128]{1,0:T(8,128)(2,1)} %get-tuple-element.40), channel_id=1, source_target_pairs={{0,16},{8,24},{16,0},{24,8},{32,48},{40,56},{48,32},{56,40},{64,80... | collective-permute-start | bytes 503816 | tf_op jit(solution)/shard_map/ppermute | solution.py:484
  8.8 3.3 %collective-permute-start.1 = (bf16[656,128]{1,0:T(8,128)(2,1)}, bf16[656,128]{1,0:T(8,128)(2,1)S(1)}, u32[]{:S(2)}, u32[]{:S(2)}) collective-permute-start(bf16[656,128]{1,0:T(8,128)(2,1)} %get-tuple-element.41), channel_id=1, source_target_pairs={{0,24},{8,16},{16,8},{24,0},{32,56},{40,48},{48,40},{56,32},{64,88... | collective-permute-start | bytes 503816 | tf_op jit(solution)/shard_map/ppermute | solution.py:484
  12.1 2.2 %collective-permute-start.2 = (bf16[656,128]{1,0:T(8,128)(2,1)}, bf16[656,128]{1,0:T(8,128)(2,1)S(1)}, u32[]{:S(2)}, u32[]{:S(2)}) collective-permute-start(bf16[656,128]{1,0:T(8,128)(2,1)} %get-tuple-element.42), channel_id=1, source_target_pairs={{0,8},{8,0},{16,24},{24,16},{32,40},{40,32},{48,56},{56,48},{64,72... | collective-permute-start | bytes 503816 | tf_op jit(solution)/shard_map/ppermute | solution.py:484
  14.3 0.0 copy-start
  14.3 1.1 %copy-done = bf16[128,2560]{1,0:T(8,128)(2,1)S(1)} copy-done((bf16[128,2560]{1,0:T(8,128)(2,1)S(1)}, bf16[128,2560]{1,0:T(8,128)(2,1)}, u32[]{:S(2)}) %copy-start) | copy-done | bytes 655384
  15.4 0.8 copy-done.4
  16.1 0.8 copy-done.8
  17.0 0.8 copy-done.9
  17.7 0.8 copy-done.10
  18.5 0.7 copy-done.12
  19.2 0.5 second_states.1
  19.7 0.0 copy-start.1
  19.7 0.0 copy-start.2
  19.7 0.0 copy-start.3
  19.8 0.0 copy-start.5
  19.8 0.0 copy-start.6
  19.8 0.0 collective-permute-done.1.refs_1_
  19.8 3.7 %collective-permute-done.2.refs_2_ = bf16[656,128]{1,0:T(8,128)(2,1)S(1)} collective-permute-done((bf16[656,128]{1,0:T(8,128)(2,1)}, bf16[656,128]{1,0:T(8,128)(2,1)S(1)}, u32[]{:S(2)}, u32[]{:S(2)}) %collective-permute-start.2) | collective-permute-done | bytes 167968 | tf_op jit(solution)/shard_map/ppermute | solution.py:484
  23.5 0.2 group_state.1
  23.7 9.8 %collective-permute-start.3 = (bf16[400,128]{1,0:T(8,128)(2,1)S(1)}, bf16[400,128]{1,0:T(8,128)(2,1)S(1)}, u32[]{:S(2)}, u32[]{:S(2)}) collective-permute-start(bf16[400,128]{1,0:T(8,128)(2,1)S(1)} %get-tuple-element.49.own_ref), channel_id=1, source_target_pairs={{0,32},{8,40},{16,48},{24,56},{32,0},{40,8},{48,16},{56,24},{64,96... | collective-permute-start | bytes 307208 | tf_op jit(solution)/shard_map/ppermute | solution.py:469
  33.6 8.2 %collective-permute-start.5 = (bf16[272,128]{1,0:T(8,128)(2,1)S(1)}, bf16[272,128]{1,0:T(8,128)(2,1)S(1)}, u32[]{:S(2)}, u32[]{:S(2)}) collective-permute-start(bf16[272,128]{1,0:T(8,128)(2,1)S(1)} %get-tuple-element.50.own_ref), channel_id=1, source_target_pairs={{0,96},{8,104},{16,112},{24,120},{32,64},{40,72},{48,80},{56,88},{... | collective-permute-start | bytes 208904 | tf_op jit(solution)/shard_map/ppermute | solution.py:469
  41.8 2.2 %collective-permute-start.7 = (bf16[192,128]{1,0:T(8,128)(2,1)S(1)}, bf16[192,128]{1,0:T(8,128)(2,1)S(1)}, u32[]{:S(2)}, u32[]{:S(2)}) collective-permute-start(bf16[192,128]{1,0:T(8,128)(2,1)S(1)} %copy-done.16), channel_id=1, source_target_pairs={{0,16},{8,24},{16,0},{24,8},{32,48},{40,56},{48,32},{56,40},{64,80... | collective-permute-start | bytes 147464 | tf_op jit(solution)/shard_map/ppermute | solution.py:484
  44.0 3.5 %collective-permute-start.8 = (bf16[192,128]{1,0:T(8,128)(2,1)S(1)}, bf16[192,128]{1,0:T(8,128)(2,1)S(1)}, u32[]{:S(2)}, u32[]{:S(2)}) collective-permute-start(bf16[192,128]{1,0:T(8,128)(2,1)S(1)} %copy-done.15), channel_id=1, source_target_pairs={{0,24},{8,16},{16,8},{24,0},{32,56},{40,48},{48,40},{56,32},{64,88... | collective-permute-start | bytes 147464 | tf_op jit(solution)/shard_map/ppermute | solution.py:484
  47.6 2.6 %collective-permute-start.9 = (bf16[192,128]{1,0:T(8,128)(2,1)S(1)}, bf16[192,128]{1,0:T(8,128)(2,1)S(1)}, u32[]{:S(2)}, u32[]{:S(2)}) collective-permute-start(bf16[192,128]{1,0:T(8,128)(2,1)S(1)} %copy-done.14), channel_id=1, source_target_pairs={{0,8},{8,0},{16,24},{24,16},{32,40},{40,32},{48,56},{56,48},{64,72... | collective-permute-start | bytes 147464 | tf_op jit(solution)/shard_map/ppermute | solution.py:484
  50.2 4.0 %collective-permute-start.6 = (bf16[2,272,128]{2,1,0:T(8,128)(2,1)S(1)}, bf16[2,272,128]{2,1,0:T(8,128)(2,1)S(1)}, u32[]{:S(2)}, u32[]{:S(2)}) collective-permute-start(bf16[2,272,128]{2,1,0:T(8,128)(2,1)S(1)} %two_states.1), channel_id=1, source_target_pairs={{0,32},{8,40},{16,48},{24,56},{32,0},{40,8},{48,16},{56,24},{64,96... | collective-permute-start | bytes 417800 | tf_op jit(solution)/shard_map/ppermute | solution.py:469
  54.3 0.1 pair_state.1.pair_ref
  54.3 4.5 %collective-permute-start.4 = (bf16[400,128]{1,0:T(8,128)(2,1)S(1)}, bf16[400,128]{1,0:T(8,128)(2,1)S(1)}, u32[]{:S(2)}, u32[]{:S(2)}) collective-permute-start(bf16[400,128]{1,0:T(8,128)(2,1)S(1)} %pair_state.1.pair_ref), channel_id=1, source_target_pairs={{0,96},{8,104},{16,112},{24,120},{32,64},{40,72},{48,80},{56,88},{... | collective-permute-start | bytes 307208 | tf_op jit(solution)/shard_map/ppermute | solution.py:469
  58.9 2.6 %local_part.1 = (f32[128,2560]{1,0:T(8,128)S(1)}, f32[128,2560]{1,0:T(8,128)S(1)}) custom-call(bf16[128,2560]{1,0:T(8,128)(2,1)S(1)} %copy-done.1, bf16[128,128]{1,0:T(8,128)(2,1)S(1)} %copy-done.3, bf16[128,128]{1,0:T(8,128)(2,1)S(1)} %copy-done.5, f32[40,128]{1,0:T(8,128)S(1)} %copy-done.6, f32[7,40,128]{2,1,0:T(8,128)S(1)} %copy-done.2, ...), custom_call_target="tpu_custom_call" | custom-call | flops 10000000000 | bytes 10000000 | tf_op jit(solution)/shard_map/local_part/pallas_call | solution.py:444
  61.5 5.9 %collective-permute-done.4.far_ref = bf16[400,128]{1,0:T(8,128)(2,1)S(1)} collective-permute-done((bf16[400,128]{1,0:T(8,128)(2,1)S(1)}, bf16[400,128]{1,0:T(8,128)(2,1)S(1)}, u32[]{:S(2)}, u32[]{:S(2)}) %collective-permute-start.4) | collective-permute-done | bytes 102432 | tf_op jit(solution)/shard_map/ppermute | solution.py:469
  67.4 2.1 %collective-permute-done.6.beside_ref = bf16[2,272,128]{2,1,0:T(8,128)(2,1)S(1)} collective-permute-done((bf16[2,272,128]{2,1,0:T(8,128)(2,1)S(1)}, bf16[2,272,128]{2,1,0:T(8,128)(2,1)S(1)}, u32[]{:S(2)}, u32[]{:S(2)}) %collective-permute-start.6) | collective-permute-done | bytes 139296 | tf_op jit(solution)/shard_map/ppermute | solution.py:469
  69.5 0.2 row_state.1
  69.7 3.3 %collective-permute-start.10 = (bf16[656,128]{1,0:T(8,128)(2,1)S(1)}, bf16[656,128]{1,0:T(8,128)(2,1)S(1)}, u32[]{:S(2)}, u32[]{:S(2)}) collective-permute-start(bf16[656,128]{1,0:T(8,128)(2,1)S(1)} %get-tuple-element.62), channel_id=1, source_target_pairs={{0,128},{8,136},{16,144},{24,152},{32,160},{40,168},{48,176},{56,1... | collective-permute-start | bytes 503816 | tf_op jit(solution)/shard_map/ppermute | solution.py:478
  72.9 4.3 %collective-permute-start.11 = (bf16[656,128]{1,0:T(8,128)(2,1)S(1)}, bf16[656,128]{1,0:T(8,128)(2,1)S(1)}, u32[]{:S(2)}, u32[]{:S(2)}) collective-permute-start(bf16[656,128]{1,0:T(8,128)(2,1)S(1)} %get-tuple-element.62), channel_id=1, source_target_pairs={{0,256},{8,264},{16,272},{24,280},{32,288},{40,296},{48,304},{56,3... | collective-permute-start | bytes 503816 | tf_op jit(solution)/shard_map/ppermute | solution.py:478
  77.3 1.3 %collective-permute-start.12 = (bf16[656,128]{1,0:T(8,128)(2,1)S(1)}, bf16[656,128]{1,0:T(8,128)(2,1)S(1)}, u32[]{:S(2)}, u32[]{:S(2)}) collective-permute-start(bf16[656,128]{1,0:T(8,128)(2,1)S(1)} %get-tuple-element.62), channel_id=1, source_target_pairs={{0,384},{8,392},{16,400},{24,408},{32,416},{40,424},{48,432},{56,4... | collective-permute-start | bytes 503816 | tf_op jit(solution)/shard_map/ppermute | solution.py:478
  78.6 1.8 %near_levels.1 = (f32[4,128,640]{2,1,0:T(8,128)S(1)}, bf16[4,128,128]{2,1,0:T(8,128)(2,1)S(1)}, f32[4,2,128,640]{3,2,1,0:T(8,128)S(1)}) custom-call(bf16[4,656,128]{2,1,0:T(8,128)(2,1)S(1)} %get-tuple-element.48.parts_ref, bf16[656,128]{1,0:T(8,128)(2,1)S(1)} %get-tuple-element.51.next_ref, bf16[656,128]{1,0:T(8,128)(2,1)S(1)} %get-tuple-element.52.pair_ref, ...), custom_call_target="tpu_custom_call" | custom-call | flops 10000000000 | bytes 4000000 | tf_op jit(solution)/shard_map/near_levels/pallas_call | solution.py:444
  80.4 1.8 %collective-permute-done.12.r3_ref = bf16[656,128]{1,0:T(8,128)(2,1)S(1)} collective-permute-done((bf16[656,128]{1,0:T(8,128)(2,1)S(1)}, bf16[656,128]{1,0:T(8,128)(2,1)S(1)}, u32[]{:S(2)}, u32[]{:S(2)}) %collective-permute-start.12) | collective-permute-done | bytes 167968 | tf_op jit(solution)/shard_map/ppermute | solution.py:478
  82.2 0.6 far_levels.2
  82.9 1.9 %collective-permute-start.13 = (bf16[128,640]{1,0:T(8,128)(2,1)S(1)}, bf16[128,640]{1,0:T(8,128)(2,1)S(1)}, u32[]{:S(2)}, u32[]{:S(2)}) collective-permute-start(bf16[128,640]{1,0:T(8,128)(2,1)S(1)} %get-tuple-element.64), channel_id=1, source_target_pairs={{0,16},{8,24},{16,0},{24,8},{32,48},{40,56},{48,32},{56,40},{64,80... | collective-permute-start | bytes 491528 | tf_op jit(solution)/shard_map/ppermute | solution.py:484
  84.8 3.6 %collective-permute-start.14 = (bf16[128,640]{1,0:T(8,128)(2,1)S(1)}, bf16[128,640]{1,0:T(8,128)(2,1)S(1)}, u32[]{:S(2)}, u32[]{:S(2)}) collective-permute-start(bf16[128,640]{1,0:T(8,128)(2,1)S(1)} %get-tuple-element.65), channel_id=1, source_target_pairs={{0,24},{8,16},{16,8},{24,0},{32,56},{40,48},{48,40},{56,32},{64,88... | collective-permute-start | bytes 491528 | tf_op jit(solution)/shard_map/ppermute | solution.py:484
  88.4 2.8 %collective-permute-start.15 = (bf16[128,640]{1,0:T(8,128)(2,1)S(1)}, bf16[128,640]{1,0:T(8,128)(2,1)S(1)}, u32[]{:S(2)}, u32[]{:S(2)}) collective-permute-start(bf16[128,640]{1,0:T(8,128)(2,1)S(1)} %get-tuple-element.66), channel_id=1, source_target_pairs={{0,8},{8,0},{16,24},{24,16},{32,40},{40,32},{48,56},{56,48},{64,72... | collective-permute-start | bytes 491528 | tf_op jit(solution)/shard_map/ppermute | solution.py:484
  91.3 0.4 far_levels.3.refs_3_
  91.7 6.0 %collective-permute-done.13.refs_0_ = bf16[128,640]{1,0:T(8,128)(2,1)S(1)} collective-permute-done((bf16[128,640]{1,0:T(8,128)(2,1)S(1)}, bf16[128,640]{1,0:T(8,128)(2,1)S(1)}, u32[]{:S(2)}, u32[]{:S(2)}) %collective-permute-start.13) | collective-permute-done | bytes 163872 | tf_op jit(solution)/shard_map/ppermute | solution.py:484
  97.7 4.0 %collective-permute-done.15.refs_2_ = bf16[128,640]{1,0:T(8,128)(2,1)S(1)} collective-permute-done((bf16[128,640]{1,0:T(8,128)(2,1)S(1)}, bf16[128,640]{1,0:T(8,128)(2,1)S(1)}, u32[]{:S(2)}, u32[]{:S(2)}) %collective-permute-start.15) | collective-permute-done | bytes 163872 | tf_op jit(solution)/shard_map/ppermute | solution.py:484
  101.7 0.4 gate.1
  102.1 2.4 %collective-permute-start.16 = (f32[128,128]{1,0:T(8,128)S(1)}, f32[128,128]{1,0:T(8,128)S(1)}, u32[]{:S(2)}, u32[]{:S(2)}) collective-permute-start(f32[128,128]{1,0:T(8,128)S(1)} %get-tuple-element.68.own_ref), channel_id=1, source_target_pairs={{0,4},{4,0},{1,5},{5,1},{2,6},{6,2},{3,7},{7,3},{8,12},{12,8},{9,1... | collective-permute-start | bytes 196616 | tf_op jit(solution)/shard_map/ppermute | solution.py:640
  104.5 0.9 collective-permute-done.16.other_ref
  105.4 1.1 %norm.1 = bf16[128,2560]{1,0:T(8,128)(2,1)} custom-call(bf16[128,2560]{1,0:T(8,128)(2,1)S(1)} %get-tuple-element.67.gated_ref, f32[128,128]{1,0:T(8,128)S(1)} %get-tuple-element.68.own_ref, f32[128,128]{1,0:T(8,128)S(1)} %collective-permute-done.16.other_ref, f32[1,2560]{1,0:T(1,128)S(1)} %reshape.3.weight_ref), custom_call_target="tpu_custom_call" | custom-call | flops 100000000 | bytes 4000000 | tf_op jit(solution)/shard_map/norm/pallas_call | solution.py:444
  (33 shorter events, 0.1 us)
Async XLA Ops:
  3.1 16.7 %collective-permute-start = (bf16[656,128]{1,0:T(8,128)(2,1)}, bf16[656,128]{1,0:T(8,128)(2,1)S(1)}, u32[]{:S(2)}, u32[]{:S(2)}) collective-permute-start(bf16[656,128]{1,0:T(8,128)(2,1)} %get-tuple-element.40), channel_id=1, source_target_pairs={{0,16},{8,24},{16,0},{24,8},{32,48},{40,56},{48,32},{56,40},{64,80... | collective-permute-start | bytes 503816 | tf_op jit(solution)/shard_map/ppermute | solution.py:484
  8.8 11.0 %collective-permute-start.1 = (bf16[656,128]{1,0:T(8,128)(2,1)}, bf16[656,128]{1,0:T(8,128)(2,1)S(1)}, u32[]{:S(2)}, u32[]{:S(2)}) collective-permute-start(bf16[656,128]{1,0:T(8,128)(2,1)} %get-tuple-element.41), channel_id=1, source_target_pairs={{0,24},{8,16},{16,8},{24,0},{32,56},{40,48},{48,40},{56,32},{64,88... | collective-permute-start | bytes 503816 | tf_op jit(solution)/shard_map/ppermute | solution.py:484
  12.1 11.4 %collective-permute-start.2 = (bf16[656,128]{1,0:T(8,128)(2,1)}, bf16[656,128]{1,0:T(8,128)(2,1)S(1)}, u32[]{:S(2)}, u32[]{:S(2)}) collective-permute-start(bf16[656,128]{1,0:T(8,128)(2,1)} %get-tuple-element.42), channel_id=1, source_target_pairs={{0,8},{8,0},{16,24},{24,16},{32,40},{40,32},{48,56},{56,48},{64,72... | collective-permute-start | bytes 503816 | tf_op jit(solution)/shard_map/ppermute | solution.py:484
  14.3 1.1 %copy-start = (bf16[128,2560]{1,0:T(8,128)(2,1)S(1)}, bf16[128,2560]{1,0:T(8,128)(2,1)}, u32[]{:S(2)}) copy-start(bf16[128,2560]{1,0:T(8,128)(2,1)} %x_ref.3) | copy-start | bytes 1966084
  15.4 0.8 copy-start.4
  16.1 0.8 copy-start.8
  17.0 0.8 copy-start.9
  17.7 0.8 copy-start.10
  18.5 0.7 copy-start.12
  19.2 22.6 %copy-start.16 = (bf16[192,128]{1,0:T(8,128)(2,1)S(1)}, bf16[192,128]{1,0:T(8,128)(2,1)}, u32[]{:S(2)}) copy-start(bf16[192,128]{1,0:T(8,128)(2,1)} %get-tuple-element.56) | copy-start | bytes 147460
  19.2 24.9 %copy-start.15 = (bf16[192,128]{1,0:T(8,128)(2,1)S(1)}, bf16[192,128]{1,0:T(8,128)(2,1)}, u32[]{:S(2)}) copy-start(bf16[192,128]{1,0:T(8,128)(2,1)} %get-tuple-element.57) | copy-start | bytes 147460
  19.2 28.4 %copy-start.14 = (bf16[192,128]{1,0:T(8,128)(2,1)S(1)}, bf16[192,128]{1,0:T(8,128)(2,1)}, u32[]{:S(2)}) copy-start(bf16[192,128]{1,0:T(8,128)(2,1)} %get-tuple-element.58) | copy-start | bytes 147460
  19.2 39.7 %copy-start.7 = (bf16[128,2560]{1,0:T(8,128)(2,1)S(1)}, bf16[128,2560]{1,0:T(8,128)(2,1)}, u32[]{:S(2)}) copy-start(bf16[128,2560]{1,0:T(8,128)(2,1)} %gate_hbm.1) | copy-start | bytes 1966084
  19.7 39.1 %copy-start.1 = (bf16[128,2560]{1,0:T(8,128)(2,1)S(1)}, bf16[128,2560]{1,0:T(8,128)(2,1)}, u32[]{:S(2)}) copy-start(bf16[128,2560]{1,0:T(8,128)(2,1)} %x_ref.3) | copy-start | bytes 1966084
  19.7 39.1 %copy-start.2 = (f32[7,40,128]{2,1,0:T(8,128)S(1)}, f32[7,40,128]{2,1,0:T(8,128)}, u32[]{:S(2)}) copy-start(f32[7,40,128]{2,1,0:T(8,128)} %weight_hbm.1) | copy-start | bytes 430084
  19.7 39.1 %copy-start.3 = (bf16[128,128]{1,0:T(8,128)(2,1)S(1)}, bf16[128,128]{1,0:T(8,128)(2,1)}, u32[]{:S(2)}) copy-start(bf16[128,128]{1,0:T(8,128)(2,1)} %b_hbm.1) | copy-start | bytes 98308
  19.8 39.1 %copy-start.5 = (bf16[128,128]{1,0:T(8,128)(2,1)S(1)}, bf16[128,128]{1,0:T(8,128)(2,1)}, u32[]{:S(2)}) copy-start(bf16[128,128]{1,0:T(8,128)(2,1)} %c_ref.3) | copy-start | bytes 98308
  19.8 39.1 %copy-start.6 = (f32[40,128]{1,0:T(8,128)S(1)}, f32[40,128]{1,0:T(8,128)}, u32[]{:S(2)}) copy-start(f32[40,128]{1,0:T(8,128)} %step_hbm.1) | copy-start | bytes 61444
  19.8 39.1 %copy-start.11 = (f32[40,128]{1,0:T(8,128)S(1)}, f32[40,128]{1,0:T(8,128)}, u32[]{:S(2)}) copy-start(f32[40,128]{1,0:T(8,128)} %get-tuple-element.37.within_ref) | copy-start | bytes 61444
  23.7 30.5 %collective-permute-start.3 = (bf16[400,128]{1,0:T(8,128)(2,1)S(1)}, bf16[400,128]{1,0:T(8,128)(2,1)S(1)}, u32[]{:S(2)}, u32[]{:S(2)}) collective-permute-start(bf16[400,128]{1,0:T(8,128)(2,1)S(1)} %get-tuple-element.49.own_ref), channel_id=1, source_target_pairs={{0,32},{8,40},{16,48},{24,56},{32,0},{40,8},{48,16},{56,24},{64,96... | collective-permute-start | bytes 307208 | tf_op jit(solution)/shard_map/ppermute | solution.py:469
  33.6 16.6 %collective-permute-start.5 = (bf16[272,128]{1,0:T(8,128)(2,1)S(1)}, bf16[272,128]{1,0:T(8,128)(2,1)S(1)}, u32[]{:S(2)}, u32[]{:S(2)}) collective-permute-start(bf16[272,128]{1,0:T(8,128)(2,1)S(1)} %get-tuple-element.50.own_ref), channel_id=1, source_target_pairs={{0,96},{8,104},{16,112},{24,120},{32,64},{40,72},{48,80},{56,88},{... | collective-permute-start | bytes 208904 | tf_op jit(solution)/shard_map/ppermute | solution.py:469
  41.8 35.5 %collective-permute-start.7 = (bf16[192,128]{1,0:T(8,128)(2,1)S(1)}, bf16[192,128]{1,0:T(8,128)(2,1)S(1)}, u32[]{:S(2)}, u32[]{:S(2)}) collective-permute-start(bf16[192,128]{1,0:T(8,128)(2,1)S(1)} %copy-done.16), channel_id=1, source_target_pairs={{0,16},{8,24},{16,0},{24,8},{32,48},{40,56},{48,32},{56,40},{64,80... | collective-permute-start | bytes 147464 | tf_op jit(solution)/shard_map/ppermute | solution.py:484
  44.0 34.5 %collective-permute-start.8 = (bf16[192,128]{1,0:T(8,128)(2,1)S(1)}, bf16[192,128]{1,0:T(8,128)(2,1)S(1)}, u32[]{:S(2)}, u32[]{:S(2)}) collective-permute-start(bf16[192,128]{1,0:T(8,128)(2,1)S(1)} %copy-done.15), channel_id=1, source_target_pairs={{0,24},{8,16},{16,8},{24,0},{32,56},{40,48},{48,40},{56,32},{64,88... | collective-permute-start | bytes 147464 | tf_op jit(solution)/shard_map/ppermute | solution.py:484
  47.6 31.0 %collective-permute-start.9 = (bf16[192,128]{1,0:T(8,128)(2,1)S(1)}, bf16[192,128]{1,0:T(8,128)(2,1)S(1)}, u32[]{:S(2)}, u32[]{:S(2)}) collective-permute-start(bf16[192,128]{1,0:T(8,128)(2,1)S(1)} %copy-done.14), channel_id=1, source_target_pairs={{0,8},{8,0},{16,24},{24,16},{32,40},{40,32},{48,56},{56,48},{64,72... | collective-permute-start | bytes 147464 | tf_op jit(solution)/shard_map/ppermute | solution.py:484
  50.2 19.2 %collective-permute-start.6 = (bf16[2,272,128]{2,1,0:T(8,128)(2,1)S(1)}, bf16[2,272,128]{2,1,0:T(8,128)(2,1)S(1)}, u32[]{:S(2)}, u32[]{:S(2)}) collective-permute-start(bf16[2,272,128]{2,1,0:T(8,128)(2,1)S(1)} %two_states.1), channel_id=1, source_target_pairs={{0,32},{8,40},{16,48},{24,56},{32,0},{40,8},{48,16},{56,24},{64,96... | collective-permute-start | bytes 417800 | tf_op jit(solution)/shard_map/ppermute | solution.py:469
  54.3 13.1 %collective-permute-start.4 = (bf16[400,128]{1,0:T(8,128)(2,1)S(1)}, bf16[400,128]{1,0:T(8,128)(2,1)S(1)}, u32[]{:S(2)}, u32[]{:S(2)}) collective-permute-start(bf16[400,128]{1,0:T(8,128)(2,1)S(1)} %pair_state.1.pair_ref), channel_id=1, source_target_pairs={{0,96},{8,104},{16,112},{24,120},{32,64},{40,72},{48,80},{56,88},{... | collective-permute-start | bytes 307208 | tf_op jit(solution)/shard_map/ppermute | solution.py:469
  69.7 10.7 %collective-permute-start.10 = (bf16[656,128]{1,0:T(8,128)(2,1)S(1)}, bf16[656,128]{1,0:T(8,128)(2,1)S(1)}, u32[]{:S(2)}, u32[]{:S(2)}) collective-permute-start(bf16[656,128]{1,0:T(8,128)(2,1)S(1)} %get-tuple-element.62), channel_id=1, source_target_pairs={{0,128},{8,136},{16,144},{24,152},{32,160},{40,168},{48,176},{56,1... | collective-permute-start | bytes 503816 | tf_op jit(solution)/shard_map/ppermute | solution.py:478
  72.9 7.5 %collective-permute-start.11 = (bf16[656,128]{1,0:T(8,128)(2,1)S(1)}, bf16[656,128]{1,0:T(8,128)(2,1)S(1)}, u32[]{:S(2)}, u32[]{:S(2)}) collective-permute-start(bf16[656,128]{1,0:T(8,128)(2,1)S(1)} %get-tuple-element.62), channel_id=1, source_target_pairs={{0,256},{8,264},{16,272},{24,280},{32,288},{40,296},{48,304},{56,3... | collective-permute-start | bytes 503816 | tf_op jit(solution)/shard_map/ppermute | solution.py:478
  77.3 5.0 %collective-permute-start.12 = (bf16[656,128]{1,0:T(8,128)(2,1)S(1)}, bf16[656,128]{1,0:T(8,128)(2,1)S(1)}, u32[]{:S(2)}, u32[]{:S(2)}) collective-permute-start(bf16[656,128]{1,0:T(8,128)(2,1)S(1)} %get-tuple-element.62), channel_id=1, source_target_pairs={{0,384},{8,392},{16,400},{24,408},{32,416},{40,424},{48,432},{56,4... | collective-permute-start | bytes 503816 | tf_op jit(solution)/shard_map/ppermute | solution.py:478
  82.9 14.8 %collective-permute-start.13 = (bf16[128,640]{1,0:T(8,128)(2,1)S(1)}, bf16[128,640]{1,0:T(8,128)(2,1)S(1)}, u32[]{:S(2)}, u32[]{:S(2)}) collective-permute-start(bf16[128,640]{1,0:T(8,128)(2,1)S(1)} %get-tuple-element.64), channel_id=1, source_target_pairs={{0,16},{8,24},{16,0},{24,8},{32,48},{40,56},{48,32},{56,40},{64,80... | collective-permute-start | bytes 491528 | tf_op jit(solution)/shard_map/ppermute | solution.py:484
  84.8 12.9 %collective-permute-start.14 = (bf16[128,640]{1,0:T(8,128)(2,1)S(1)}, bf16[128,640]{1,0:T(8,128)(2,1)S(1)}, u32[]{:S(2)}, u32[]{:S(2)}) collective-permute-start(bf16[128,640]{1,0:T(8,128)(2,1)S(1)} %get-tuple-element.65), channel_id=1, source_target_pairs={{0,24},{8,16},{16,8},{24,0},{32,56},{40,48},{48,40},{56,32},{64,88... | collective-permute-start | bytes 491528 | tf_op jit(solution)/shard_map/ppermute | solution.py:484
  88.4 13.2 %collective-permute-start.15 = (bf16[128,640]{1,0:T(8,128)(2,1)S(1)}, bf16[128,640]{1,0:T(8,128)(2,1)S(1)}, u32[]{:S(2)}, u32[]{:S(2)}) collective-permute-start(bf16[128,640]{1,0:T(8,128)(2,1)S(1)} %get-tuple-element.66), channel_id=1, source_target_pairs={{0,8},{8,0},{16,24},{24,16},{32,40},{40,32},{48,56},{56,48},{64,72... | collective-permute-start | bytes 491528 | tf_op jit(solution)/shard_map/ppermute | solution.py:484
  101.7 2.8 %copy-start.13 = (f32[2560]{0:T(1024)S(1)}, f32[2560]{0:T(1024)}, u32[]{:S(2)}) copy-start(f32[2560]{0:T(1024)} %param.15) | copy-start | bytes 30724
  102.1 3.3 %collective-permute-start.16 = (f32[128,128]{1,0:T(8,128)S(1)}, f32[128,128]{1,0:T(8,128)S(1)}, u32[]{:S(2)}, u32[]{:S(2)}) collective-permute-start(f32[128,128]{1,0:T(8,128)S(1)} %get-tuple-element.68.own_ref), channel_id=1, source_target_pairs={{0,4},{4,0},{1,5},{5,1},{2,6},{6,2},{3,7},{7,3},{8,12},{12,8},{9,1... | collective-permute-start | bytes 196616 | tf_op jit(solution)/shard_map/ppermute | solution.py:640
